TPU v7x, 32 devices: a whole 2x2x4 slice. The times are simulated.
32 devices in a mesh: var: 8 (over z, core), tp: 4 (over y, x).
Axes of the slice: x: 2, y: 2, z: 4, core: 2. Of those that a mesh axis runs over, the one named last changes fastest.
Arguments:
- hidden_in: bfloat16 [24, 384, 2048], P('var'), may hold values from -100 to 100
- run_table: int32 [24, 2], P('var'), may hold values 0 or 1
- qkv_weight: bfloat16 [2048, 3072], P('var', 'tp'), may hold values from -1 to 1
- out_weight: bfloat16 [2048, 2048], P('tp', 'var'), may hold values from -0.125 to 0.125
- gate_up_weight: bfloat16 [2048, 2, 8192], P('var', None, 'tp'), may hold values from -0.125 to 0.125
- down_weight: bfloat16 [8192, 2048], P('tp', 'var'), may hold values from -0.0625 to 0.0625
Outputs:
- layer_out: bfloat16 [24, 384, 2048], P('var')
All inputs are finite; a program needn't handle non-finite values. No bound on the sum of `run_table` on one device may be relied on, other than what follows from the above.
Results may differ from a plain program's by a relative error of at most 0.0075.
Values may be sent and summed in bfloat16 or wider, within the bound.
A program may use at most 128 MiB of HBM per device.

v0:
```python
import jax
import jax.numpy as jnp
from jax import lax
from jax.sharding import PartitionSpec as P

QUERY_HEADS = 32
KEY_VALUE_HEADS = 8
HEAD_SIZE = 64


def rms_norm(tensor):
    widened = tensor.astype(jnp.float32)
    scaled = widened * lax.rsqrt(jnp.mean(widened * widened, axis=-1, keepdims=True) + 1e-05)
    return scaled.astype(jnp.bfloat16)


def rotary_embedding(tensor, token_positions):
    half_width = tensor.shape[-1] // 2
    exponent = jnp.arange(half_width, dtype=jnp.float32) * (2.0 / tensor.shape[-1])
    frequency = jnp.power(jnp.float32(500000.0), -exponent)
    angles = token_positions[:, None, None] * frequency[None, None, :]
    cosine = jnp.cos(angles)
    sine_part = jnp.sin(angles)
    first_half = tensor[..., :half_width]
    second_half = tensor[..., half_width:]
    return jnp.concatenate(
        [
            first_half * cosine - second_half * sine_part,
            second_half * cosine + first_half * sine_part,
        ],
        axis=-1,
    )


def attend(query_rows, keys_bfloat, values_bfloat, score_scale):
    scores = (
        jnp.einsum("bqkgd,bpkd->bkgqp", query_rows, keys_bfloat, preferred_element_type=jnp.float32)
        * score_scale
    )
    length = scores.shape[-1]
    causal = jnp.arange(length)[:, None] >= jnp.arange(length)[None, :]
    scores = jnp.where(causal, scores, jnp.float32(-1e30))
    row_max = jnp.max(scores, axis=-1, keepdims=True)
    exped = jnp.exp(scores - row_max)
    weights_bf = (exped / jnp.sum(exped, axis=-1, keepdims=True)).astype(jnp.bfloat16)
    head_outputs = jnp.einsum(
        "bkgqp,bpkd->bqkgd", weights_bf, values_bfloat, preferred_element_type=jnp.float32
    )
    return head_outputs.astype(jnp.bfloat16)


def shards(hidden_in, run_table, qkv_weight, out_weight, gate_up_weight, down_weight):
    tensor_parallel_count = lax.axis_size("tp")
    seq_count, full_len, model_width = hidden_in.shape
    row_count = seq_count * full_len
    query_slice = QUERY_HEADS // tensor_parallel_count
    key_value_slice = KEY_VALUE_HEADS // tensor_parallel_count
    group_width = QUERY_HEADS // KEY_VALUE_HEADS
    switches = run_table.astype(jnp.float32)
    flat_input = rms_norm(hidden_in).reshape(row_count, model_width)
    columns = flat_input
    projected_rows = jnp.dot(
        columns,
        lax.all_gather(qkv_weight, "var", axis=0, tiled=True),
        preferred_element_type=jnp.float32,
    )
    projected_rows = projected_rows.reshape(
        seq_count, full_len, query_slice + 2 * key_value_slice, HEAD_SIZE
    )
    token_positions = jnp.arange(full_len, dtype=jnp.float32)
    query_rows = rotary_embedding(projected_rows[:, :, :query_slice], token_positions).astype(
        jnp.bfloat16
    )
    query_rows = query_rows.reshape(seq_count, full_len, key_value_slice, group_width, HEAD_SIZE)
    keys_bfloat = rotary_embedding(
        projected_rows[:, :, query_slice : query_slice + key_value_slice], token_positions
    ).astype(jnp.bfloat16)
    values_bfloat = projected_rows[:, :, query_slice + key_value_slice :].astype(jnp.bfloat16)
    score_scale = HEAD_SIZE ** (-0.5)
    head_outputs = attend(query_rows, keys_bfloat, values_bfloat, score_scale)
    head_rows = head_outputs.reshape(row_count, query_slice * HEAD_SIZE)
    attn_terms = jnp.dot(
        head_rows,
        lax.all_gather(out_weight, "var", axis=1, tiled=True),
        preferred_element_type=jnp.float32,
    )
    attn_terms = attn_terms.reshape(seq_count, full_len, model_width)
    attn_switch = switches[:, 0][:, None, None]
    attention = lax.psum(attn_terms.astype(jnp.bfloat16), "tp").astype(jnp.float32)
    whole_after = (hidden_in.astype(jnp.float32) + attn_switch * attention).astype(jnp.bfloat16)
    mlp_input = rms_norm(whole_after)
    flat_mlp = mlp_input.reshape(row_count, model_width)
    ff_local = gate_up_weight.shape[2]
    block_piece = lax.all_gather(gate_up_weight, "var", axis=0, tiled=True)
    columns = flat_mlp
    flat_piece = block_piece.reshape(block_piece.shape[0], 2 * ff_local)
    gate_and_up = jnp.dot(columns, flat_piece, preferred_element_type=jnp.float32)
    hidden = (jax.nn.silu(gate_and_up[:, :ff_local]) * gate_and_up[:, ff_local:]).astype(
        jnp.bfloat16
    )
    mlp_terms = jnp.dot(
        hidden,
        lax.all_gather(down_weight, "var", axis=1, tiled=True),
        preferred_element_type=jnp.float32,
    )
    mlp_terms = mlp_terms.reshape(seq_count, full_len, model_width)
    mlp = lax.psum(mlp_terms.astype(jnp.bfloat16), "tp").astype(jnp.float32)
    mlp_switch = switches[:, 1][:, None, None]
    return (whole_after.astype(jnp.float32) + mlp_switch * mlp).astype(jnp.bfloat16)


def solution(mesh):
    return jax.shard_map(
        shards,
        mesh=mesh,
        in_specs=(
            P("var", None, None),
            P("var", None),
            P("var", "tp"),
            P("tp", "var"),
            P("var", None, "tp"),
            P("tp", "var"),
        ),
        out_specs=P("var", None, None),
        check_vma=False,
    )
```

profile of v0, /device:TPU:0, one launch (start us, length us, event | category | flops | bytes accessed | tf_op | source)
XLA Modules:
  0.0 578.9 jit_solution(13335061835774915613)
XLA Ops:
  6.5 0.7 all-gather.5.cloned.1.call-update
  7.3 0.7 all-gather.7.cloned.1.call-update
  8.1 3.3 fusion.2
  11.7 38.3 %all-gather.5.cloned.1.call-done = bf16[2048,768]{1,0:T(8,128)(2,1)} async-done(((bf16[256,768]{1,0:T(8,128)(2,1)}), bf16[2048,768]{1,0:T(8,128)(2,1)}) %all-gather.5.cloned.1.call-update) | async-done | bytes 3145744 | tf_op jit(solution)/shard_map/all_gather | solution.py:64
  50.0 3.2 copy.10
  53.2 6.7 %fusion.14 = f32[3,384,12,64]{1,3,2,0:T(8,128)S(1)} fusion(bf16[12,64,2048,1]{2,1,0,3:T(8,128)(2,1)S(1)} %bitcast.63, bf16[3,384,2048]{2,1,0:T(8,128)(2,1)} %param.6, f32[3,384]{1,0:T(4,128)S(1)} %add_rsqrt_fusion.1), kind=kOutput, calls=%fused_computation.25 | convolution fusion | flops 3630956544 | bytes 11407872 | tf_op jit(solution)/shard_map/dot_general | solution.py:62
  60.0 1.7 copy-done.2
  62.0 7.7 %fusion.35 = (f32[3,2,4,384]{3,2,1,0:T(4,128)S(1)}, f32[3,2,4,384,384]{3,4,2,1,0:T(8,128)}) fusion(pred[384,384]{0,1:T(8,128)(4,1)S(1)} %iota_compare_fusion, bf16[3,384,2,4,32]{1,4,3,2,0:T(8,128)(2,1)S(1)} %bitcast.65, bf16[3,384,2,4,32]{1,4,3,2,0:T(8,128)(2,1)S(1)} %bitcast.64, bf16[3,384,2,32]{1,3,2,0:T(8,128)(2,1)S(1)} %get-tuple-element.8, ...), kind=kOutput, calls=%fused_computation.54 | convolution fusion | flops 470090112 | bytes 15814656 | tf_op jit(solution)/shard_map/sub | solution.py:44
  69.7 6.7 %fusion.21 = bf16[3,2,64,4,384]{4,2,3,1,0:T(8,128)(2,1)S(1)} fusion(f32[3,2,4,384,384]{3,4,2,1,0:T(8,128)} %get-tuple-element.16, f32[3,2,4,384]{3,2,1,0:T(4,128)S(1)} %get-tuple-element.15, f32[3,384,12,64]{1,3,2,0:T(8,128)} %copy-done.2), kind=kOutput, calls=%fused_computation.30 | convolution fusion | flops 460652544 | bytes 15667200 | tf_op jit(solution)/shard_map/bkgqp,bpkd->bqkgd/dot_general | solution.py:46
  76.4 4.9 all-gather.7.cloned.1.call-done
  81.3 6.4 %convolution_convert_fusion.1 = bf16[3,384,2048]{2,1,0:T(8,128)(2,1)} fusion(bf16[3,384,512]{1,2,0:T(8,128)(2,1)S(1)} %bitcast.66, bf16[512,2048]{1,0:T(8,128)(2,1)} %all-gather.7.cloned.1.call-done), kind=kOutput, calls=%fused_computation.27 | convolution fusion | flops 2418278400 | bytes 7995392 | tf_op jit(solution)/shard_map/dot_general | solution.py:82
  87.8 0.5 all-gather.9.cloned.1.call-update
  88.4 0.5 all-gather.11.cloned.1.call-update
  89.2 110.3 %all-reduce.3.cloned.1.call-done = bf16[3,384,2048]{2,1,0:T(8,128)(2,1)} async-done(((bf16[3,384,2048]{2,1,0:T(8,128)(2,1)}), bf16[3,384,2048]{2,1,0:T(8,128)(2,1)}) %all-reduce.3.cloned.1.call-update) | async-done | bytes 4718608 | tf_op jit(solution)/shard_map/psum | solution.py:89
  199.5 6.5 %fusion.5 = (f32[3,384]{1,0:T(4,128)S(1)}, bf16[3,384,2048]{2,1,0:T(8,128)(2,1)S(1)}) fusion(bf16[3,384,2048]{2,1,0:T(8,128)(2,1)} %all-reduce.3.cloned.1.call-done, f32[3]{0:T(128)S(1)} %get-tuple-element.12, bf16[3,384,2048]{2,1,0:T(8,128)(2,1)} %param.6), kind=kLoop, calls=%fused_computation.14 | loop fusion | flops 18873216 | bytes 14160396 | tf_op jit(solution)/shard_map/reduce_sum | solution.py:13
  206.0 2.2 copy-done
  208.2 3.1 fusion.6
  211.3 140.8 %all-gather.9.cloned.1.call-done = bf16[2048,2,2048]{2,1,0:T(2,128)(2,1)} async-done(((bf16[256,2,2048]{2,1,0:T(2,128)(2,1)}), bf16[2048,2,2048]{2,1,0:T(2,128)(2,1)}) %all-gather.9.cloned.1.call-update) | async-done | bytes 16777232 | tf_op jit(solution)/shard_map/all_gather | solution.py:94
  352.1 12.7 %copy.18 = bf16[256,8,2,2048]{3,1,2,0:T(8,128)(2,1)S(1)} copy(bf16[256,8,2,2048]{3,2,1,0:T(2,128)(2,1)} %bitcast.58) | data formatting | bytes 33554432
  364.9 23.1 %fusion.36 = f32[1152,4096]{1,0:T(8,128)} fusion(bf16[1152,2048]{1,0:T(8,128)(2,1)S(1)} %bitcast.61, bf16[2048,4096]{1,0:T(8,128)(2,1)S(1)} %bitcast.59), kind=kOutput, calls=%fused_computation.55 | convolution fusion | flops 19327352832 | bytes 40370176 | tf_op jit(solution)/shard_map/dot_general | solution.py:97
  388.0 46.3 %all-gather.11.cloned.1.call-done = bf16[2048,2048]{1,0:T(8,128)(2,1)} async-done(((bf16[2048,256]{1,0:T(8,128)(2,1)}), bf16[2048,2048]{1,0:T(8,128)(2,1)}) %all-gather.11.cloned.1.call-update) | async-done | bytes 8388624 | tf_op jit(solution)/shard_map/all_gather | solution.py:103
  434.3 17.9 %convolution_convert_fusion = bf16[1152,2048]{1,0:T(8,128)(2,1)} fusion(bf16[2048,2048]{1,0:T(8,128)(2,1)} %all-gather.11.cloned.1.call-done, f32[1152,4096]{1,0:T(8,128)} %fusion.36), kind=kOutput, calls=%fused_computation.19 | convolution fusion | flops 9680191488 | bytes 31981568 | tf_op jit(solution)/shard_map/dot_general | solution.py:101
  452.3 110.8 %all-reduce.5.cloned.1.call-done = bf16[3,384,2048]{2,1,0:T(8,128)(2,1)} async-done(((bf16[3,384,2048]{2,1,0:T(8,128)(2,1)}), bf16[3,384,2048]{2,1,0:T(8,128)(2,1)}) %all-reduce.5.cloned.1.call-update) | async-done | bytes 4718608 | tf_op jit(solution)/shard_map/psum | solution.py:107
  563.1 8.9 %fusion.7 = bf16[3,384,2048]{2,1,0:T(8,128)(2,1)} fusion(bf16[3,384,2048]{2,1,0:T(8,128)(2,1)} %copy-done, bf16[3,384,2048]{2,1,0:T(8,128)(2,1)} %all-reduce.5.cloned.1.call-done, f32[3]{0:T(128)S(1)} %get-tuple-element.11), kind=kLoop, calls=%fused_computation.16 | loop fusion | flops 11796480 | bytes 14155788 | tf_op jit(solution)/shard_map/convert_element_type | solution.py:109
  (23 shorter events, 1.2 us)
Async XLA Ops:
  6.5 43.5 %all-gather.5.cloned.1.call-start = ((), (), s32[]{:S(2)}) async-start(), calls=%async_computation | async-start | bytes 3538944 | tf_op jit(solution)/shard_map/all_gather | solution.py:64
  7.3 74.1 %all-gather.7.cloned.1.call-start = ((), (), s32[]{:S(2)}) async-start(), calls=%async_computation.1 | async-start | bytes 2359296 | tf_op jit(solution)/shard_map/all_gather | solution.py:84
  8.0 191.5 %all-reduce.3.cloned.1.call-start = ((), (), s32[]{:S(2)}) async-start(), calls=%async_computation.2 | async-start | bytes 9437184 | tf_op jit(solution)/shard_map/psum | solution.py:89
  59.9 1.8 copy-start.2
  87.8 1.4 copy-start.3
  87.8 264.3 %all-gather.9.cloned.1.call-start = ((), (), s32[]{:S(2)}) async-start(), calls=%async_computation.3 | async-start | bytes 18874368 | tf_op jit(solution)/shard_map/all_gather | solution.py:94
  88.4 345.9 %all-gather.11.cloned.1.call-start = ((), (), s32[]{:S(2)}) async-start(), calls=%async_computation.4 | async-start | bytes 9437184 | tf_op jit(solution)/shard_map/all_gather | solution.py:103
  89.0 474.1 %all-reduce.5.cloned.1.call-start = ((), (), s32[]{:S(2)}) async-start(), calls=%async_computation.5 | async-start | bytes 9437184 | tf_op jit(solution)/shard_map/psum | solution.py:107
  206.0 2.2 copy-start
  352.1 12.7 %copy-start.1 = (bf16[3,384,2048]{2,1,0:T(8,128)(2,1)S(1)}, bf16[3,384,2048]{2,1,0:T(8,128)(2,1)}, u32[]{:S(2)}) copy-start(bf16[3,384,2048]{2,1,0:T(8,128)(2,1)} %fusion.6) | copy-start | bytes 14155780
Sparse Core Ops, SparseCore 0:
  9.0 40.9 all-gather.4
  51.6 29.6 all-gather.6
  87.9 111.5 all-reduce.2
  201.0 151.0 all-gather.8
  353.5 80.7 all-gather.10
  452.4 110.6 all-reduce.4
where the time goes:
time: 579 us
  waiting for transfers between devices  454 us (78%)
  matrix products  68.5 us (12%)
  other arithmetic  22.6 us (4%)
  local copies, waits for them, and re-layouts  19.8 us (3%)
  between operations  13.6 us (2%)
    all_gather x1, waiting for transfers between devices, shards(): block_piece = lax.all_gather(gate_up_weight, 'var', axis=0, tiled=True)  141 us
    psum x1, waiting for transfers between devices, shards(): mlp = lax.psum(mlp_terms.astype(jnp.bfloat16), 'tp').astype(jnp.float32)  111 us
    psum x1, waiting for transfers between devices, shards(): lax.psum(attn_terms.astype(jnp.bfloat16), 'tp').astype(jnp.float32)  110 us
    all_gather x1, waiting for transfers between devices, shards(): lax.all_gather(down_weight, 'var', axis=1, tiled=True)  46.3 us
    all_gather x1, waiting for transfers between devices, shards(): lax.all_gather(qkv_weight, 'var', axis=0, tiled=True)  38.3 us
    dot_general x1, matrix products, shards(): jnp.dot(columns, flat_piece, preferred_element_type=jnp.float32)  23.1 us
    dot_general x1, matrix products, shards(): jnp.dot(hidden, lax.all_gather(down_weight, 'var', axis=1, tiled=True), p...  17.9 us
    unnamed x9, local copies, waits for them, and re-layouts  16.6 us
  transfers between devices with their start and end apart: 6, of which 6 were waited for; matrix products, arithmetic and copies ran while one was open for 13% of the time, Pallas kernels for 0%

commit v1 on v0

v1 whole, which is shorter than its diff:
```python
import jax
import jax.numpy as jnp
from jax import lax
from jax.sharding import PartitionSpec as P

QUERY_HEADS = 32
KEY_VALUE_HEADS = 8
HEAD_SIZE = 64
CORES = 2


def rms_norm(tensor):
    widened = tensor.astype(jnp.float32)
    scaled = widened * lax.rsqrt(jnp.mean(widened * widened, axis=-1, keepdims=True) + 1e-05)
    return scaled.astype(jnp.bfloat16)


def rotary_embedding(tensor, token_positions):
    half_width = tensor.shape[-1] // 2
    exponent = jnp.arange(half_width, dtype=jnp.float32) * (2.0 / tensor.shape[-1])
    frequency = jnp.power(jnp.float32(500000.0), -exponent)
    angles = token_positions[:, None, None] * frequency[None, None, :]
    cosine = jnp.cos(angles)
    sine_part = jnp.sin(angles)
    first_half = tensor[..., :half_width]
    second_half = tensor[..., half_width:]
    return jnp.concatenate(
        [
            first_half * cosine - second_half * sine_part,
            second_half * cosine + first_half * sine_part,
        ],
        axis=-1,
    )


def attend(query_rows, keys_bfloat, values_bfloat, score_scale):
    scores = (
        jnp.einsum("bqkgd,bpkd->bkgqp", query_rows, keys_bfloat, preferred_element_type=jnp.float32)
        * score_scale
    )
    length = scores.shape[-1]
    causal = jnp.arange(length)[:, None] >= jnp.arange(length)[None, :]
    scores = jnp.where(causal, scores, jnp.float32(-1e30))
    row_max = jnp.max(scores, axis=-1, keepdims=True)
    exped = jnp.exp(scores - row_max)
    weights_bf = (exped / jnp.sum(exped, axis=-1, keepdims=True)).astype(jnp.bfloat16)
    head_outputs = jnp.einsum(
        "bkgqp,bpkd->bqkgd", weights_bf, values_bfloat, preferred_element_type=jnp.float32
    )
    return head_outputs.astype(jnp.bfloat16)


def after(tensor, earlier):
    return lax.optimization_barrier((tensor, earlier))[0]


def ring(shard, earlier):
    var_count = lax.axis_size("var")
    forward = [(i, (i + CORES) % var_count) for i in range(var_count)]
    if earlier is not None:
        shard = after(shard, earlier)
    held = [shard]
    for _ in range(var_count // CORES - 1):
        held.append(lax.ppermute(held[-1], "var", forward))
    return held


def swap(held):
    var_count = lax.axis_size("var")
    pairs = [(i, i + 1 - 2 * (i % CORES)) for i in range(var_count)]
    return [lax.ppermute(shard, "var", pairs) for shard in held]


def pairs_of(mine, other):
    return [block for pair in zip(mine, other) for block in pair]


def shards(hidden_in, run_table, qkv_weight, out_weight, gate_up_weight, down_weight):
    tensor_parallel_count = lax.axis_size("tp")
    var_count = lax.axis_size("var")
    seq_count, full_len, model_width = hidden_in.shape
    row_count = seq_count * full_len
    query_slice = QUERY_HEADS // tensor_parallel_count
    key_value_slice = KEY_VALUE_HEADS // tensor_parallel_count
    group_width = QUERY_HEADS // KEY_VALUE_HEADS
    switches = run_table.astype(jnp.float32)
    bf16 = jnp.bfloat16

    query_width = query_slice * HEAD_SIZE
    half_ff = down_weight.shape[0] // 2
    q_ring = ring(qkv_weight[:, :query_width], None)
    kv_ring = ring(qkv_weight[:, query_width:], None)
    out_ring = ring(out_weight, kv_ring[-1])
    gate_ring = ring(gate_up_weight[:, 0, :], q_ring[-1])
    up_ring = ring(gate_up_weight[:, 1, :], out_ring[-1])
    down_a_ring = ring(down_weight[:half_ff], gate_ring[-1])
    down_b_ring = ring(down_weight[half_ff:], up_ring[-1])

    q_weight = jnp.concatenate(pairs_of(q_ring, swap(q_ring)), axis=0)
    kv_weight = jnp.concatenate(pairs_of(kv_ring, swap(kv_ring)), axis=0)
    out_full = jnp.concatenate(pairs_of(out_ring, swap(out_ring)), axis=1)

    block = model_width // var_count
    me = lax.axis_index("var")
    chip, core = me // CORES, me % CORES
    chip_count = var_count // CORES
    order = []
    for step in range(chip_count):
        origin = (chip + chip_count - step) % chip_count
        order += [origin * CORES + core, origin * CORES + 1 - core]
    flat_in = hidden_in.reshape(row_count, model_width)
    ordered_in = jnp.concatenate(
        [lax.dynamic_slice_in_dim(flat_in, place * block, block, axis=1) for place in order], axis=1
    )

    columns = rms_norm(ordered_in)
    queries = jnp.dot(columns, q_weight, preferred_element_type=jnp.float32)
    keys_values = jnp.dot(columns, kv_weight, preferred_element_type=jnp.float32)
    queries = queries.reshape(seq_count, full_len, query_slice, HEAD_SIZE)
    keys_values = keys_values.reshape(seq_count, full_len, 2 * key_value_slice, HEAD_SIZE)
    token_positions = jnp.arange(full_len, dtype=jnp.float32)
    query_rows = rotary_embedding(queries, token_positions).astype(bf16)
    query_rows = query_rows.reshape(seq_count, full_len, key_value_slice, group_width, HEAD_SIZE)
    keys_bfloat = rotary_embedding(keys_values[:, :, :key_value_slice], token_positions).astype(bf16)
    values_bfloat = keys_values[:, :, key_value_slice:].astype(bf16)
    head_outputs = attend(query_rows, keys_bfloat, values_bfloat, HEAD_SIZE ** (-0.5))
    head_rows = head_outputs.reshape(row_count, query_width)
    attn_terms = jnp.dot(head_rows, out_full, preferred_element_type=jnp.float32)
    attention = lax.psum(attn_terms.astype(bf16), "tp").astype(jnp.float32)
    attn_switch = jnp.repeat(switches[:, 0], full_len)[:, None]
    whole_after = (ordered_in.astype(jnp.float32) + attn_switch * attention).astype(bf16)

    mlp_input = rms_norm(whole_after)
    gate_weight = jnp.concatenate(pairs_of(gate_ring, swap(gate_ring)), axis=0)
    up_weight = jnp.concatenate(pairs_of(up_ring, swap(up_ring)), axis=0)
    gate = jnp.dot(mlp_input, gate_weight, preferred_element_type=jnp.float32)
    up = jnp.dot(mlp_input, up_weight, preferred_element_type=jnp.float32)
    hidden = (jax.nn.silu(gate) * up).astype(bf16)

    mlp_switch = jnp.repeat(switches[:, 1], full_len)[:, None]
    down_a_swap, down_b_swap = swap(down_a_ring), swap(down_b_ring)
    layer_out = jnp.zeros((row_count, model_width), bf16)
    for step in range(chip_count):
        mine = jnp.concatenate([down_a_ring[step], down_b_ring[step]], axis=0)
        other = jnp.concatenate([down_a_swap[step], down_b_swap[step]], axis=0)
        down_pair = jnp.concatenate([mine, other], axis=1)
        terms = jnp.dot(hidden, down_pair, preferred_element_type=jnp.float32)
        terms = terms.astype(bf16)
        if step > 0:
            terms = after(terms, summed)
        summed = lax.psum(terms, "tp")
        mlp = summed.astype(jnp.float32)
        residual = whole_after[:, 2 * step * block : 2 * (step + 1) * block]
        result = (residual.astype(jnp.float32) + mlp_switch * mlp).astype(bf16)
        for half in range(2):
            layer_out = lax.dynamic_update_slice_in_dim(
                layer_out,
                result[:, half * block : (half + 1) * block],
                order[2 * step + half] * block,
                axis=1,
            )
    return layer_out.reshape(seq_count, full_len, model_width)


def solution(mesh):
    return jax.shard_map(
        shards,
        mesh=mesh,
        in_specs=(
            P("var", None, None),
            P("var", None),
            P("var", "tp"),
            P("tp", "var"),
            P("var", None, "tp"),
            P("tp", "var"),
        ),
        out_specs=P("var", None, None),
        check_vma=False,
    )
```

time: 579 us -> 547 us (0.945); the launches traced: 579 us -> 540 us
  waiting for transfers between devices: 454 us -> 345 us
  local copies, waits for them, and re-layouts: 19.8 us -> 69.2 us
  starting transfers between devices: 0.38 us -> 14.1 us
  matrix products: 68.5 us -> 82 us
  other arithmetic: 22.6 us -> 15.9 us
    all_gather x4 -> x0, waiting for transfers between devices: 230 us -> none  [the longest x1 141 us: shards(): block_piece = lax.all_gather(gate_up_weight, 'var', axis=0, tiled=True)]
    ppermute x0 -> x49, waiting for transfers between devices: none -> 145 us  [the longest x21 145 us: ring(): held.append(lax.ppermute(held[-1], 'var', forward))]
    unnamed x9 -> x82, local copies, waits for them, and re-layouts: 16.6 us -> 52.7 us
    psum x2 -> x5, waiting for transfers between devices: 221 us -> 200 us  [the longest x4 200 us: shards(): summed = lax.psum(terms, 'tp')]
    ppermute x0 -> x49, starting transfers between devices: none -> 13.9 us  [the longest x21 8.36 us: ring(): held.append(lax.ppermute(held[-1], 'var', forward))]
    dot_general x4 -> x9, matrix products: 54.1 us -> 64.9 us  [the longest x4 23.8 us: shards(): terms = jnp.dot(hidden, down_pair, preferred_element_type=jnp.float32)]
    convert_element_type x2 -> x1, other arithmetic: 12.1 us -> 3.91 us  [shards(): result = (residual.astype(jnp.float32) + mlp_switch * mlp).astype(bf16)]
    slice x0 -> x5, local copies, waits for them, and re-layouts: none -> 6.64 us  [the longest x1 2.97 us: shards(): up_ring = ring(gate_up_weight[:, 1, :], out_ring[-1])]
  transfers between devices with their start and end apart: 6 -> 54, of which waited for: 6 -> 20; matrix products, arithmetic and copies ran while one was open for 13% -> 29% of each run, Pallas kernels for 0% -> 0%
where the time goes in v1:
time: 547 us; the launch traced here: 540 us
  waiting for transfers between devices  345 us (63%)
  matrix products  82 us (15%)
  local copies, waits for them, and re-layouts  69.2 us (13%)
  other arithmetic  15.9 us (3%)
  starting transfers between devices  14.1 us (3%)
  between operations  14 us (3%)
    psum x4, waiting for transfers between devices, shards(): summed = lax.psum(terms, 'tp')  200 us
    ppermute x21, waiting for transfers between devices, ring(): held.append(lax.ppermute(held[-1], 'var', forward))  145 us
    unnamed x82, local copies, waits for them, and re-layouts  52.7 us
    dot_general x4, matrix products, shards(): terms = jnp.dot(hidden, down_pair, preferred_element_type=jnp.float32)  23.8 us
    dot_general x1, matrix products, shards(): up = jnp.dot(mlp_input, up_weight, preferred_element_type=jnp.float32)  14.9 us
    dot_general x1, matrix products, shards(): gate = jnp.dot(mlp_input, gate_weight, preferred_element_type=jnp.float32)  12.7 us
  transfers between devices with their start and end apart: 54, of which 20 were waited for; matrix products, arithmetic and copies ran while one was open for 29% of the time, Pallas kernels for 0%

profile of v1, /device:TPU:0, one launch (start us, length us, event | category | flops | bytes accessed | tf_op | source)
XLA Modules:
  0.0 540.1 jit_solution(9341613238529488840)
XLA Ops:
  43.4 4.9 collective-permute-done.3
  50.3 6.1 %collective-permute-done.5 = bf16[256,256]{1,0:T(8,128)(2,1)S(1)} collective-permute-done((bf16[256,256]{1,0:T(8,128)(2,1)S(1)}, bf16[256,256]{1,0:T(8,128)(2,1)S(1)}, u32[]{:S(2)}, u32[]{:S(2)}) %collective-permute-start.5) | collective-permute-done | bytes 131104 | tf_op jit(solution)/shard_map/ppermute | solution.py:64
  81.3 7.5 %fusion.45 = f32[1152,512]{0,1:T(8,128)} fusion(bf16[2048,512]{1,0:T(8,128)(2,1)} %constant_dynamic-update-slice_fusion.8, bf16[1152,2048]{1,0:T(8,128)(2,1)} %dynamic-slice_dynamic-update-slice_fusion, f32[1152]{0:T(1024)S(1)} %add_rsqrt_fusion.1), kind=kOutput, calls=%fused_computation.59 | convolution fusion | flops 2422996992 | bytes 9179648 | tf_op jit(solution)/shard_map/dot_general | solution.py:117
  92.6 10.6 %fusion.73 = (f32[3,2,4,384]{3,2,1,0:T(4,128)S(1)}, f32[3,2,4,384,384]{3,4,2,1,0:T(8,128)}) fusion(pred[384,384]{0,1:T(8,128)(4,1)} %iota_compare_fusion, bf16[3,384,2,4,32]{1,4,3,2,0:T(8,128)(2,1)S(1)} %bitcast.79, bf16[3,384,2,4,32]{1,4,3,2,0:T(8,128)(2,1)S(1)} %bitcast.78, bf16[3,384,2,32]{1,3,2,0:T(8,128)(2,1)} %get-tuple-element.36, ...), kind=kOutput, calls=%fused_computation.152 | convolution fusion | flops 470090112 | bytes 15814656 | tf_op jit(solution)/shard_map/sub | solution.py:45
  106.7 6.4 %fusion.52 = bf16[3,384,2,4,64]{1,4,3,2,0:T(8,128)(2,1)S(1)} fusion(f32[3,2,4,384,384]{3,4,2,1,0:T(8,128)} %get-tuple-element.46, f32[3,2,4,384]{3,2,1,0:T(4,128)S(1)} %get-tuple-element.45, bf16[3,384,2,64]{1,0,3,2:T(4,128)(2,1)S(1)} %copy-done.9), kind=kOutput, calls=%fused_computation.65 | convolution fusion | flops 460652544 | bytes 15667200 | tf_op jit(solution)/shard_map/bkgqp,bpkd->bqkgd/dot_general | solution.py:47
  124.7 17.9 %collective-permute-done.29 = bf16[256,2048]{1,0:T(8,128)(2,1)S(1)} collective-permute-done((bf16[256,2048]{1,0:T(8,128)(2,1)S(1)}, bf16[256,2048]{1,0:T(8,128)(2,1)S(1)}, u32[]{:S(2)}, u32[]{:S(2)}) %collective-permute-start.29) | collective-permute-done | bytes 1048608 | tf_op jit(solution)/shard_map/ppermute | solution.py:64
  148.2 17.0 %collective-permute-done.24 = bf16[256,2048]{1,0:T(8,128)(2,1)} collective-permute-done((bf16[256,2048]{1,0:T(8,128)(2,1)}, bf16[256,2048]{1,0:T(8,128)(2,1)}, u32[]{:S(2)}, u32[]{:S(2)}) %collective-permute-start.24) | collective-permute-done | bytes 1048608 | tf_op jit(solution)/shard_map/ppermute | solution.py:64
  167.5 20.0 %collective-permute-done.31 = bf16[256,2048]{1,0:T(8,128)(2,1)S(1)} collective-permute-done((bf16[256,2048]{1,0:T(8,128)(2,1)S(1)}, bf16[256,2048]{1,0:T(8,128)(2,1)S(1)}, u32[]{:S(2)}, u32[]{:S(2)}) %collective-permute-start.31) | collective-permute-done | bytes 1048608 | tf_op jit(solution)/shard_map/ppermute | solution.py:64
  191.2 18.8 %collective-permute-done.26 = bf16[256,2048]{1,0:T(8,128)(2,1)S(1)} collective-permute-done((bf16[256,2048]{1,0:T(8,128)(2,1)}, bf16[256,2048]{1,0:T(8,128)(2,1)S(1)}, u32[]{:S(2)}, u32[]{:S(2)}) %collective-permute-start.26) | collective-permute-done | bytes 1048608 | tf_op jit(solution)/shard_map/ppermute | solution.py:64
  211.6 20.9 %collective-permute-done.33 = bf16[256,2048]{1,0:T(8,128)(2,1)S(1)} collective-permute-done((bf16[256,2048]{1,0:T(8,128)(2,1)S(1)}, bf16[256,2048]{1,0:T(8,128)(2,1)S(1)}, u32[]{:S(2)}, u32[]{:S(2)}) %collective-permute-start.33) | collective-permute-done | bytes 1048608 | tf_op jit(solution)/shard_map/ppermute | solution.py:64
  234.9 8.8 %collective-permute-done.37 = bf16[1024,256]{1,0:T(8,128)(2,1)S(1)} collective-permute-done((bf16[1024,256]{1,0:T(8,128)(2,1)S(1)}, bf16[1024,256]{1,0:T(8,128)(2,1)S(1)}, u32[]{:S(2)}, u32[]{:S(2)}) %collective-permute-start.37) | collective-permute-done | bytes 524320 | tf_op jit(solution)/shard_map/ppermute | solution.py:64
  244.3 10.2 %collective-permute-done.38 = bf16[1024,256]{1,0:T(8,128)(2,1)S(1)} collective-permute-done((bf16[1024,256]{1,0:T(8,128)(2,1)S(1)}, bf16[1024,256]{1,0:T(8,128)(2,1)S(1)}, u32[]{:S(2)}, u32[]{:S(2)}) %collective-permute-start.38) | collective-permute-done | bytes 524320 | tf_op jit(solution)/shard_map/ppermute | solution.py:64
  255.8 6.0 %fusion.2 = (f32[1152]{0:T(1024)S(1)}, bf16[1152,2048]{1,0:T(8,128)(2,1)S(1)}) fusion(bf16[1152,2048]{1,0:T(8,128)(2,1)} %all-reduce.6.cloned.1.call-done, f32[1152]{0:T(1024)S(1)} %mul.294, bf16[1152,2048]{1,0:T(8,128)(2,1)} %dynamic-slice_dynamic-update-slice_fusion), kind=kLoop, calls=%fused_computation.10 | loop fusion | flops 18873216 | bytes 14164992 | tf_op jit(solution)/shard_map/reduce_sum | solution.py:14
  261.9 12.7 %fusion.41 = f32[1152,2048]{1,0:T(8,128)} fusion(bf16[2048,2048]{1,0:T(8,128)(2,1)S(1)} %copy-done.12, bf16[1152,2048]{1,0:T(8,128)(2,1)S(1)} %get-tuple-element.22, f32[1152]{0:T(1024)S(1)} %add_rsqrt_fusion), kind=kOutput, calls=%fused_computation.58 | convolution fusion | flops 9670754304 | bytes 22548992 | tf_op jit(solution)/shard_map/dot_general | solution.py:136
  274.6 14.9 %multiply_convert_fusion = bf16[1152,2048]{1,0:T(8,128)(2,1)S(1)} fusion(f32[1152,2048]{1,0:T(8,128)} %fusion.41, bf16[2048,2048]{1,0:T(8,128)(2,1)} %constant_dynamic-update-slice_fusion.32, bf16[1152,2048]{1,0:T(8,128)(2,1)S(1)} %get-tuple-element.22, f32[1152]{0:T(1024)S(1)} %add_rsqrt_fusion), kind=kOutput, calls=%fused_computation.15 | convolution fusion | flops 9684910080 | bytes 27267584 | tf_op jit(solution)/shard_map/dot_general | solution.py:137
  291.6 4.9 convolution_convert_fusion.4
  297.2 9.2 %collective-permute-done.42 = bf16[1024,256]{1,0:T(8,128)(2,1)} collective-permute-done((bf16[1024,256]{1,0:T(8,128)(2,1)S(1)}, bf16[1024,256]{1,0:T(8,128)(2,1)}, u32[]{:S(2)}, u32[]{:S(2)}) %collective-permute-start.42) | collective-permute-done | bytes 524320 | tf_op jit(solution)/shard_map/ppermute | solution.py:64
  306.4 6.1 %convolution_convert_fusion.3 = bf16[1152,512]{1,0:T(8,128)(2,1)} fusion(bf16[1152,2048]{1,0:T(8,128)(2,1)} %copy-done.16, bf16[1024,256]{1,0:T(8,128)(2,1)} %collective-permute-done.40, bf16[1024,256]{1,0:T(8,128)(2,1)S(1)} %collective-permute-done.39, bf16[1024,256]{1,0:T(8,128)(2,1)S(1)} %collective-permute-done.38, ...), kind=kOutput, calls=%fused_computation.23 | convolution fusion | flops 2424897536 | bytes 7995392 | tf_op jit(solution)/shard_map/dot_general | solution.py:147
  312.5 40.2 %all-reduce.8.cloned.1.call-done = bf16[1152,512]{1,0:T(8,128)(2,1)} async-done(((bf16[1152,512]{1,0:T(8,128)(2,1)}), bf16[1152,512]{1,0:T(8,128)(2,1)}) %all-reduce.8.cloned.1.call-update) | async-done | bytes 1179664 | tf_op jit(solution)/shard_map/psum | solution.py:151
  353.4 6.1 %convolution_convert_fusion.2 = bf16[1152,512]{1,0:T(8,128)(2,1)} fusion(bf16[1152,2048]{1,0:T(8,128)(2,1)} %copy-done.16, bf16[1024,256]{1,0:T(8,128)(2,1)S(1)} %collective-permute-done.44, bf16[1024,256]{1,0:T(8,128)(2,1)S(1)} %collective-permute-done.43, bf16[1024,256]{1,0:T(8,128)(2,1)} %collective-permute-done.42, ...), kind=kOutput, calls=%fused_computation.22 | convolution fusion | flops 2424897536 | bytes 7995392 | tf_op jit(solution)/shard_map/dot_general | solution.py:147
  359.5 51.1 %all-reduce.10.cloned.1.call-done = bf16[1152,512]{1,0:T(8,128)(2,1)} async-done(((bf16[1152,512]{1,0:T(8,128)(2,1)}), bf16[1152,512]{1,0:T(8,128)(2,1)}) %all-reduce.10.cloned.1.call-update) | async-done | bytes 1179664 | tf_op jit(solution)/shard_map/psum | solution.py:151
  410.8 6.7 %convolution_convert_fusion.1 = bf16[1152,512]{1,0:T(8,128)(2,1)} fusion(bf16[1152,2048]{1,0:T(8,128)(2,1)} %copy-done.16, bf16[1024,256]{1,0:T(8,128)(2,1)} %collective-permute-done.48, bf16[1024,256]{1,0:T(8,128)(2,1)} %collective-permute-done.47, bf16[1024,256]{1,0:T(8,128)(2,1)} %collective-permute-done.46, bf16[1024,256]{1,0:T(8,128)(2,1)} %collective-permute-done.45), kind=kOutput, calls=%fused_computation.21 | convolution fusion | flops 2424897536 | bytes 7995392 | tf_op jit(solution)/shard_map/dot_general | solution.py:147
  417.5 50.6 %all-reduce.12.cloned.1.call-done = bf16[1152,512]{1,0:T(8,128)(2,1)} async-done(((bf16[1152,512]{1,0:T(8,128)(2,1)}), bf16[1152,512]{1,0:T(8,128)(2,1)}) %all-reduce.12.cloned.1.call-update) | async-done | bytes 1179664 | tf_op jit(solution)/shard_map/psum | solution.py:151
  468.2 57.7 %all-reduce.14.cloned.1.call-done = bf16[1152,512]{1,0:T(8,128)(2,1)} async-done(((bf16[1152,512]{1,0:T(8,128)(2,1)}), bf16[1152,512]{1,0:T(8,128)(2,1)}) %all-reduce.14.cloned.1.call-update) | async-done | bytes 1179664 | tf_op jit(solution)/shard_map/psum | solution.py:151
  (224 shorter events, 110.7 us)
Async XLA Ops:
  6.5 249.2 %all-reduce.6.cloned.1.call-start = ((), (), s32[]{:S(2)}) async-start(), calls=%async_computation | async-start | bytes 9437184 | tf_op jit(solution)/shard_map/psum | solution.py:129
  73.2 50.9 %collective-permute-start.22 = (bf16[256,2048]{1,0:T(8,128)(2,1)}, bf16[256,2048]{1,0:T(8,128)(2,1)}, u32[]{:S(2)}, u32[]{:S(2)}) collective-permute-start(bf16[256,2048]{1,0:T(8,128)(2,1)} %bitcast.62), channel_id=1, source_target_pairs={{0,8},{4,12},{8,16},{12,20},{16,24},{20,28},{24,0},{28,4},{1,9},{5... | collective-permute-start | bytes 3145736 | tf_op jit(solution)/shard_map/ppermute | solution.py:64
  121.4 231.4 %all-reduce.8.cloned.1.call-start = ((), (), s32[]{:S(2)}) async-start(), calls=%async_computation.1 | async-start | bytes 2359296 | tf_op jit(solution)/shard_map/psum | solution.py:151
  142.6 44.9 %collective-permute-start.31 = (bf16[256,2048]{1,0:T(8,128)(2,1)S(1)}, bf16[256,2048]{1,0:T(8,128)(2,1)S(1)}, u32[]{:S(2)}, u32[]{:S(2)}) collective-permute-start(bf16[256,2048]{1,0:T(8,128)(2,1)S(1)} %collective-permute-done.29), channel_id=1, source_target_pairs={{0,8},{4,12},{8,16},{12,20},{16,24},{20,28},{24,0},{28,4},{1,9},{5... | collective-permute-start | bytes 3145736 | tf_op jit(solution)/shard_map/ppermute | solution.py:64
  143.9 44.8 %collective-permute-start.23 = (bf16[256,2048]{1,0:T(8,128)(2,1)}, bf16[256,2048]{1,0:T(8,128)(2,1)S(1)}, u32[]{:S(2)}, u32[]{:S(2)}) collective-permute-start(bf16[256,2048]{1,0:T(8,128)(2,1)} %collective-permute-done.22), channel_id=1, source_target_pairs={{0,4},{4,0},{8,12},{12,8},{16,20},{20,16},{24,28},{28,24},{1,5},{5... | collective-permute-start | bytes 3145736 | tf_op jit(solution)/shard_map/ppermute | solution.py:71
  146.3 43.8 %collective-permute-start.30 = (bf16[256,2048]{1,0:T(8,128)(2,1)S(1)}, bf16[256,2048]{1,0:T(8,128)(2,1)S(1)}, u32[]{:S(2)}, u32[]{:S(2)}) collective-permute-start(bf16[256,2048]{1,0:T(8,128)(2,1)S(1)} %collective-permute-done.29), channel_id=1, source_target_pairs={{0,4},{4,0},{8,12},{12,8},{16,20},{20,16},{24,28},{28,24},{1,5},{5... | collective-permute-start | bytes 3145736 | tf_op jit(solution)/shard_map/ppermute | solution.py:71
  165.2 44.8 %collective-permute-start.26 = (bf16[256,2048]{1,0:T(8,128)(2,1)}, bf16[256,2048]{1,0:T(8,128)(2,1)S(1)}, u32[]{:S(2)}, u32[]{:S(2)}) collective-permute-start(bf16[256,2048]{1,0:T(8,128)(2,1)} %collective-permute-done.24), channel_id=1, source_target_pairs={{0,8},{4,12},{8,16},{12,20},{16,24},{20,28},{24,0},{28,4},{1,9},{5... | collective-permute-start | bytes 3145736 | tf_op jit(solution)/shard_map/ppermute | solution.py:64
  167.5 44.1 %collective-permute-start.25 = (bf16[256,2048]{1,0:T(8,128)(2,1)}, bf16[256,2048]{1,0:T(8,128)(2,1)S(1)}, u32[]{:S(2)}, u32[]{:S(2)}) collective-permute-start(bf16[256,2048]{1,0:T(8,128)(2,1)} %collective-permute-done.24), channel_id=1, source_target_pairs={{0,4},{4,0},{8,12},{12,8},{16,20},{20,16},{24,28},{28,24},{1,5},{5... | collective-permute-start | bytes 3145736 | tf_op jit(solution)/shard_map/ppermute | solution.py:71
  187.5 44.9 %collective-permute-start.33 = (bf16[256,2048]{1,0:T(8,128)(2,1)S(1)}, bf16[256,2048]{1,0:T(8,128)(2,1)S(1)}, u32[]{:S(2)}, u32[]{:S(2)}) collective-permute-start(bf16[256,2048]{1,0:T(8,128)(2,1)S(1)} %collective-permute-done.31), channel_id=1, source_target_pairs={{0,8},{4,12},{8,16},{12,20},{16,24},{20,28},{24,0},{28,4},{1,9},{5... | collective-permute-start | bytes 3145736 | tf_op jit(solution)/shard_map/ppermute | solution.py:64
  188.8 43.9 %collective-permute-start.32 = (bf16[256,2048]{1,0:T(8,128)(2,1)S(1)}, bf16[256,2048]{1,0:T(8,128)(2,1)S(1)}, u32[]{:S(2)}, u32[]{:S(2)}) collective-permute-start(bf16[256,2048]{1,0:T(8,128)(2,1)S(1)} %collective-permute-done.31), channel_id=1, source_target_pairs={{0,4},{4,0},{8,12},{12,8},{16,20},{20,16},{24,28},{28,24},{1,5},{5... | collective-permute-start | bytes 3145736 | tf_op jit(solution)/shard_map/ppermute | solution.py:71
  211.1 78.4 %collective-permute-start.35 = (bf16[1024,256]{1,0:T(8,128)(2,1)S(1)}, bf16[1024,256]{1,0:T(8,128)(2,1)}, u32[]{:S(2)}, u32[]{:S(2)}) collective-permute-start(bf16[1024,256]{1,0:T(8,128)(2,1)S(1)} %copy-done.7), channel_id=1, source_target_pairs={{0,4},{4,0},{8,12},{12,8},{16,20},{20,16},{24,28},{28,24},{1,5},{5... | collective-permute-start | bytes 1572872 | tf_op jit(solution)/shard_map/ppermute | solution.py:71
  243.7 46.0 %collective-permute-start.36 = (bf16[1024,256]{1,0:T(8,128)(2,1)S(1)}, bf16[1024,256]{1,0:T(8,128)(2,1)}, u32[]{:S(2)}, u32[]{:S(2)}) collective-permute-start(bf16[1024,256]{1,0:T(8,128)(2,1)S(1)} %copy-done.8), channel_id=1, source_target_pairs={{0,4},{4,0},{8,12},{12,8},{16,20},{20,16},{24,28},{28,24},{1,5},{5... | collective-permute-start | bytes 1572872 | tf_op jit(solution)/shard_map/ppermute | solution.py:71
  243.7 62.7 %collective-permute-start.39 = (bf16[1024,256]{1,0:T(8,128)(2,1)S(1)}, bf16[1024,256]{1,0:T(8,128)(2,1)S(1)}, u32[]{:S(2)}, u32[]{:S(2)}) collective-permute-start(bf16[1024,256]{1,0:T(8,128)(2,1)S(1)} %collective-permute-done.37), channel_id=1, source_target_pairs={{0,4},{4,0},{8,12},{12,8},{16,20},{20,16},{24,28},{28,24},{1,5},{5... | collective-permute-start | bytes 1572872 | tf_op jit(solution)/shard_map/ppermute | solution.py:71
  254.5 42.0 %collective-permute-start.41 = (bf16[1024,256]{1,0:T(8,128)(2,1)S(1)}, bf16[1024,256]{1,0:T(8,128)(2,1)S(1)}, u32[]{:S(2)}, u32[]{:S(2)}) collective-permute-start(bf16[1024,256]{1,0:T(8,128)(2,1)S(1)} %collective-permute-done.37), channel_id=1, source_target_pairs={{0,8},{4,12},{8,16},{12,20},{16,24},{20,28},{24,0},{28,4},{1,9},{5... | collective-permute-start | bytes 1572872 | tf_op jit(solution)/shard_map/ppermute | solution.py:64
  254.6 51.9 %collective-permute-start.40 = (bf16[1024,256]{1,0:T(8,128)(2,1)S(1)}, bf16[1024,256]{1,0:T(8,128)(2,1)}, u32[]{:S(2)}, u32[]{:S(2)}) collective-permute-start(bf16[1024,256]{1,0:T(8,128)(2,1)S(1)} %collective-permute-done.38), channel_id=1, source_target_pairs={{0,4},{4,0},{8,12},{12,8},{16,20},{20,16},{24,28},{28,24},{1,5},{5... | collective-permute-start | bytes 1572872 | tf_op jit(solution)/shard_map/ppermute | solution.py:71
  296.5 114.1 %all-reduce.10.cloned.1.call-start = ((), (), s32[]{:S(2)}) async-start(), calls=%async_computation.2 | async-start | bytes 2359296 | tf_op jit(solution)/shard_map/psum | solution.py:151
  296.6 56.8 %collective-permute-start.43 = (bf16[1024,256]{1,0:T(8,128)(2,1)S(1)}, bf16[1024,256]{1,0:T(8,128)(2,1)S(1)}, u32[]{:S(2)}, u32[]{:S(2)}) collective-permute-start(bf16[1024,256]{1,0:T(8,128)(2,1)S(1)} %collective-permute-done.41), channel_id=1, source_target_pairs={{0,4},{4,0},{8,12},{12,8},{16,20},{20,16},{24,28},{28,24},{1,5},{5... | collective-permute-start | bytes 1572872 | tf_op jit(solution)/shard_map/ppermute | solution.py:71
  297.2 55.6 %collective-permute-start.45 = (bf16[1024,256]{1,0:T(8,128)(2,1)S(1)}, bf16[1024,256]{1,0:T(8,128)(2,1)}, u32[]{:S(2)}, u32[]{:S(2)}) collective-permute-start(bf16[1024,256]{1,0:T(8,128)(2,1)S(1)} %collective-permute-done.41), channel_id=1, source_target_pairs={{0,8},{4,12},{8,16},{12,20},{16,24},{20,28},{24,0},{28,4},{1,9},{5... | collective-permute-start | bytes 1572872 | tf_op jit(solution)/shard_map/ppermute | solution.py:64
  306.4 47.0 %collective-permute-start.44 = (bf16[1024,256]{1,0:T(8,128)(2,1)}, bf16[1024,256]{1,0:T(8,128)(2,1)S(1)}, u32[]{:S(2)}, u32[]{:S(2)}) collective-permute-start(bf16[1024,256]{1,0:T(8,128)(2,1)} %collective-permute-done.42), channel_id=1, source_target_pairs={{0,4},{4,0},{8,12},{12,8},{16,20},{20,16},{24,28},{28,24},{1,5},{5... | collective-permute-start | bytes 1572872 | tf_op jit(solution)/shard_map/ppermute | solution.py:71
  306.4 46.5 %collective-permute-start.46 = (bf16[1024,256]{1,0:T(8,128)(2,1)}, bf16[1024,256]{1,0:T(8,128)(2,1)}, u32[]{:S(2)}, u32[]{:S(2)}) collective-permute-start(bf16[1024,256]{1,0:T(8,128)(2,1)} %collective-permute-done.42), channel_id=1, source_target_pairs={{0,8},{4,12},{8,16},{12,20},{16,24},{20,28},{24,0},{28,4},{1,9},{5... | collective-permute-start | bytes 1572872 | tf_op jit(solution)/shard_map/ppermute | solution.py:64
  352.8 115.4 %all-reduce.12.cloned.1.call-start = ((), (), s32[]{:S(2)}) async-start(), calls=%async_computation.3 | async-start | bytes 2359296 | tf_op jit(solution)/shard_map/psum | solution.py:151
  352.8 57.9 %collective-permute-start.47 = (bf16[1024,256]{1,0:T(8,128)(2,1)}, bf16[1024,256]{1,0:T(8,128)(2,1)}, u32[]{:S(2)}, u32[]{:S(2)}) collective-permute-start(bf16[1024,256]{1,0:T(8,128)(2,1)} %collective-permute-done.45), channel_id=1, source_target_pairs={{0,4},{4,0},{8,12},{12,8},{16,20},{20,16},{24,28},{28,24},{1,5},{5... | collective-permute-start | bytes 1572872 | tf_op jit(solution)/shard_map/ppermute | solution.py:71
  352.9 57.9 %collective-permute-start.48 = (bf16[1024,256]{1,0:T(8,128)(2,1)}, bf16[1024,256]{1,0:T(8,128)(2,1)}, u32[]{:S(2)}, u32[]{:S(2)}) collective-permute-start(bf16[1024,256]{1,0:T(8,128)(2,1)} %collective-permute-done.46), channel_id=1, source_target_pairs={{0,4},{4,0},{8,12},{12,8},{16,20},{20,16},{24,28},{28,24},{1,5},{5... | collective-permute-start | bytes 1572872 | tf_op jit(solution)/shard_map/ppermute | solution.py:71
  410.7 115.2 %all-reduce.14.cloned.1.call-start = ((), (), s32[]{:S(2)}) async-start(), calls=%async_computation.4 | async-start | bytes 2359296 | tf_op jit(solution)/shard_map/psum | solution.py:151
  (49 other events, 1031.7 us)
Sparse Core Ops, SparseCore 0:
  121.5 113.7 all-reduce.5
  296.7 56.0 all-reduce.7
  356.1 54.4 all-reduce.9
  413.6 54.4 all-reduce.11
  471.4 54.4 all-reduce.13

commit v2 on v1

--- a/solution.py
+++ b/solution.py
@@ -71,13 +71,52 @@
     return [lax.ppermute(shard, "var", pairs) for shard in held]
 
 
-def pairs_of(mine, other):
-    return [block for pair in zip(mine, other) for block in pair]
+def assemble(held, order, axis):
+    block = held[0].shape[axis]
+    shape = list(held[0].shape)
+    shape[axis] = block * len(held)
+    whole = jnp.zeros(tuple(shape), held[0].dtype)
+    for shard, place in zip(held, order):
+        whole = lax.dynamic_update_slice_in_dim(whole, shard, place * block, axis=axis)
+    return whole
+
+
+def partner(tensor, bit):
+    pairs = [(i, i ^ (1 << bit)) for i in range(lax.axis_size("tp"))]
+    return lax.ppermute(tensor, "tp", pairs)
+
+
+def side(bit):
+    return (lax.axis_index("tp") >> bit) & 1
+
+
+def scatter_rows(terms, bits):
+    start = 0
+    for bit in bits:
+        half = terms.shape[0] // 2
+        mine = side(bit)
+        sent = lax.dynamic_slice_in_dim(terms, (1 - mine) * half, half, axis=0)
+        kept = lax.dynamic_slice_in_dim(terms, mine * half, half, axis=0)
+        total = kept.astype(jnp.float32) + partner(sent, bit).astype(jnp.float32)
+        terms = total.astype(jnp.bfloat16)
+        start = start + mine * half
+    return total, start
+
+
+def gather_rows(rows, bits):
+    for bit in bits[:0:-1]:
+        half = rows.shape[0]
+        mine = side(bit)
+        joined = jnp.zeros((2 * half,) + rows.shape[1:], rows.dtype)
+        joined = lax.dynamic_update_slice_in_dim(joined, rows, mine * half, axis=0)
+        rows = lax.dynamic_update_slice_in_dim(joined, partner(rows, bit), (1 - mine) * half, axis=0)
+    return rows, partner(rows, bits[0]), side(bits[0])
 
 
 def shards(hidden_in, run_table, qkv_weight, out_weight, gate_up_weight, down_weight):
     tensor_parallel_count = lax.axis_size("tp")
     var_count = lax.axis_size("var")
+    chip_count = var_count // CORES
     seq_count, full_len, model_width = hidden_in.shape
     row_count = seq_count * full_len
     query_slice = QUERY_HEADS // tensor_parallel_count
@@ -91,31 +130,22 @@
     q_ring = ring(qkv_weight[:, :query_width], None)
     kv_ring = ring(qkv_weight[:, query_width:], None)
     out_ring = ring(out_weight, kv_ring[-1])
-    gate_ring = ring(gate_up_weight[:, 0, :], q_ring[-1])
-    up_ring = ring(gate_up_weight[:, 1, :], out_ring[-1])
-    down_a_ring = ring(down_weight[:half_ff], gate_ring[-1])
-    down_b_ring = ring(down_weight[half_ff:], up_ring[-1])
-
-    q_weight = jnp.concatenate(pairs_of(q_ring, swap(q_ring)), axis=0)
-    kv_weight = jnp.concatenate(pairs_of(kv_ring, swap(kv_ring)), axis=0)
-    out_full = jnp.concatenate(pairs_of(out_ring, swap(out_ring)), axis=1)
-
-    block = model_width // var_count
+    gate_ring = ring(gate_up_weight[:, 0, :], q_ring[-2])
+    up_ring = ring(gate_up_weight[:, 1, :], out_ring[-2])
+    down_a_ring = ring(down_weight[:half_ff], gate_ring[-2])
+    down_b_ring = ring(down_weight[half_ff:], up_ring[-2])
+
     me = lax.axis_index("var")
     chip, core = me // CORES, me % CORES
-    chip_count = var_count // CORES
-    order = []
-    for step in range(chip_count):
-        origin = (chip + chip_count - step) % chip_count
-        order += [origin * CORES + core, origin * CORES + 1 - core]
-    flat_in = hidden_in.reshape(row_count, model_width)
-    ordered_in = jnp.concatenate(
-        [lax.dynamic_slice_in_dim(flat_in, place * block, block, axis=1) for place in order], axis=1
-    )
-
-    columns = rms_norm(ordered_in)
-    queries = jnp.dot(columns, q_weight, preferred_element_type=jnp.float32)
-    keys_values = jnp.dot(columns, kv_weight, preferred_element_type=jnp.float32)
+    origins = [(chip + chip_count - step) % chip_count for step in range(chip_count)]
+    order = [place for origin in origins for place in (origin * CORES + core, origin * CORES + 1 - core)]
+
+    def whole(held, axis):
+        return assemble([shard for pair in zip(held, swap(held)) for shard in pair], order, axis)
+
+    columns = rms_norm(hidden_in).reshape(row_count, model_width)
+    queries = jnp.dot(columns, whole(q_ring, 0), preferred_element_type=jnp.float32)
+    keys_values = jnp.dot(columns, whole(kv_ring, 0), preferred_element_type=jnp.float32)
     queries = queries.reshape(seq_count, full_len, query_slice, HEAD_SIZE)
     keys_values = keys_values.reshape(seq_count, full_len, 2 * key_value_slice, HEAD_SIZE)
     token_positions = jnp.arange(full_len, dtype=jnp.float32)
@@ -125,40 +155,59 @@
     values_bfloat = keys_values[:, :, key_value_slice:].astype(bf16)
     head_outputs = attend(query_rows, keys_bfloat, values_bfloat, HEAD_SIZE ** (-0.5))
     head_rows = head_outputs.reshape(row_count, query_width)
-    attn_terms = jnp.dot(head_rows, out_full, preferred_element_type=jnp.float32)
+    attn_terms = jnp.dot(head_rows, whole(out_ring, 1), preferred_element_type=jnp.float32)
     attention = lax.psum(attn_terms.astype(bf16), "tp").astype(jnp.float32)
     attn_switch = jnp.repeat(switches[:, 0], full_len)[:, None]
-    whole_after = (ordered_in.astype(jnp.float32) + attn_switch * attention).astype(bf16)
+    flat_in = hidden_in.reshape(row_count, model_width)
+    whole_after = (flat_in.astype(jnp.float32) + attn_switch * attention).astype(bf16)
 
     mlp_input = rms_norm(whole_after)
-    gate_weight = jnp.concatenate(pairs_of(gate_ring, swap(gate_ring)), axis=0)
-    up_weight = jnp.concatenate(pairs_of(up_ring, swap(up_ring)), axis=0)
-    gate = jnp.dot(mlp_input, gate_weight, preferred_element_type=jnp.float32)
-    up = jnp.dot(mlp_input, up_weight, preferred_element_type=jnp.float32)
+    gate = jnp.dot(mlp_input, whole(gate_ring, 0), preferred_element_type=jnp.float32)
+    up = jnp.dot(mlp_input, whole(up_ring, 0), preferred_element_type=jnp.float32)
     hidden = (jax.nn.silu(gate) * up).astype(bf16)
 
     mlp_switch = jnp.repeat(switches[:, 1], full_len)[:, None]
     down_a_swap, down_b_swap = swap(down_a_ring), swap(down_b_ring)
+    width = model_width // chip_count
+    forth = list(range(tensor_parallel_count.bit_length() - 1))
+    early = chip_count // 2
     layer_out = jnp.zeros((row_count, model_width), bf16)
-    for step in range(chip_count):
-        mine = jnp.concatenate([down_a_ring[step], down_b_ring[step]], axis=0)
-        other = jnp.concatenate([down_a_swap[step], down_b_swap[step]], axis=0)
-        down_pair = jnp.concatenate([mine, other], axis=1)
-        terms = jnp.dot(hidden, down_pair, preferred_element_type=jnp.float32)
-        terms = terms.astype(bf16)
-        if step > 0:
-            terms = after(terms, summed)
-        summed = lax.psum(terms, "tp")
-        mlp = summed.astype(jnp.float32)
-        residual = whole_after[:, 2 * step * block : 2 * (step + 1) * block]
-        result = (residual.astype(jnp.float32) + mlp_switch * mlp).astype(bf16)
-        for half in range(2):
-            layer_out = lax.dynamic_update_slice_in_dim(
-                layer_out,
-                result[:, half * block : (half + 1) * block],
-                order[2 * step + half] * block,
+    for steps in [list(range(early))] + [[step] for step in range(early, chip_count)]:
+        down_blocks = []
+        for step in steps:
+            pair = jnp.zeros((2 * half_ff, width), bf16)
+            for tensor, row, place in (
+                (down_a_ring, 0, core),
+                (down_b_ring, half_ff, core),
+                (down_a_swap, 0, 1 - core),
+                (down_b_swap, half_ff, 1 - core),
+            ):
+                pair = lax.dynamic_update_slice(pair, tensor[step], (row, place * (width // CORES)))
+            down_blocks.append(pair)
+        terms = jnp.dot(
+            hidden, jnp.concatenate(down_blocks, axis=1), preferred_element_type=jnp.float32
+        ).astype(bf16)
+        half_rows = row_count // 2
+        for row, bits in ((0, forth), (half_rows, forth[::-1])):
+            mlp, start = scatter_rows(terms[row : row + half_rows], bits)
+            count = mlp.shape[0]
+            residual = jnp.concatenate(
+                [
+                    lax.dynamic_slice(whole_after, (row + start, origins[step] * width), (count, width))
+                    for step in steps
+                ],
                 axis=1,
             )
+            switch = lax.dynamic_slice_in_dim(mlp_switch, row + start, count, axis=0)
+            result = (residual.astype(jnp.float32) + switch * mlp).astype(bf16)
+            near, far, first = gather_rows(result, bits)
+            for part, lower in ((near, first), (far, 1 - first)):
+                for number, step in enumerate(steps):
+                    layer_out = lax.dynamic_update_slice(
+                        layer_out,
+                        part[:, number * width : (number + 1) * width],
+                        (row + lower * part.shape[0], origins[step] * width),
+                    )
     return layer_out.reshape(seq_count, full_len, model_width)
 
 

time: 547 us -> 510 us (0.932)
  waiting for transfers between devices: 345 us -> 208 us
  local copies, waits for them, and re-layouts: 69.2 us -> 128 us
  starting transfers between devices: 14.1 us -> 55.3 us
    psum x4 -> x0, waiting for transfers between devices: 200 us -> none  [shards(): summed = lax.psum(terms, 'tp')]
    dynamic_update_slice x8 -> x78, local copies, waits for them, and re-layouts: 0.69 us -> 89.5 us  [the longest x40 47.2 us: assemble(): lax.dynamic_update_slice_in_dim(whole, shard, place * block, axis=axis)]
    ppermute x0 -> x24, waiting for transfers between devices: none -> 57.6 us  [partner(): return lax.ppermute(tensor, 'tp', pairs)]
    unnamed x82 -> x39, local copies, waits for them, and re-layouts: 52.7 us -> 7.01 us
    ppermute x0 -> x24, starting transfers between devices: none -> 26 us  [partner(): return lax.ppermute(tensor, 'tp', pairs)]
    ppermute x21, starting transfers between devices: 8.36 us -> 24.2 us  [ring(): held.append(lax.ppermute(held[-1], 'var', forward))]
    another operation x2 -> x13, local copies, waits for them, and re-layouts: 0.16 us -> 13.6 us
    ppermute x21, waiting for transfers between devices: 145 us -> 151 us  [ring(): held.append(lax.ppermute(held[-1], 'var', forward))]
  transfers between devices with their start and end apart: 54 -> 74, of which waited for: 20 -> 22; matrix products, arithmetic and copies ran while one was open for 29% -> 34% of each run, Pallas kernels for 0% -> 0%
where the time goes in v2:
time: 510 us; the launch traced here: 502 us
  waiting for transfers between devices  208 us (41%)
  local copies, waits for them, and re-layouts  128 us (25%)
  matrix products  81.4 us (16%)
  starting transfers between devices  55.3 us (11%)
  between operations  15 us (3%)
  other arithmetic  14 us (3%)
    ppermute x21, waiting for transfers between devices, ring(): held.append(lax.ppermute(held[-1], 'var', forward))  151 us
    ppermute x24, waiting for transfers between devices, partner(): return lax.ppermute(tensor, 'tp', pairs)  57.6 us
    dynamic_update_slice x40, local copies, waits for them, and re-layouts, assemble(): lax.dynamic_update_slice_in_dim(whole, shard, place * block, axis=axis)  47.2 us
    dynamic_update_slice x16, local copies, waits for them, and re-layouts, shards(): lax.dynamic_update_slice(layer_out, part[:, number * width:(number + 1) *...  34.8 us
    ppermute x24, starting transfers between devices, partner(): return lax.ppermute(tensor, 'tp', pairs)  26 us
    ppermute x21, starting transfers between devices, ring(): held.append(lax.ppermute(held[-1], 'var', forward))  24.2 us
    dot_general x3, matrix products, shards(): jnp.dot(hidden, jnp.concatenate(down_blocks, axis=1), preferred_element_t...  17.3 us
    dot_general x1, matrix products, shards(): jnp.dot(mlp_input, whole(up_ring, 0), preferred_element_type=jnp.float32)  15.1 us
  transfers between devices with their start and end apart: 74, of which 22 were waited for; matrix products, arithmetic and copies ran while one was open for 34% of the time, Pallas kernels for 0%

profile of v2, /device:TPU:0, one launch (start us, length us, event | category | flops | bytes accessed | tf_op | source)
XLA Modules:
  0.0 501.8 jit_solution(10455453533014282356)
XLA Ops:
  44.4 5.6 %collective-permute-done.5 = bf16[256,256]{1,0:T(8,128)(2,1)S(1)} collective-permute-done((bf16[256,256]{1,0:T(8,128)(2,1)S(1)}, bf16[256,256]{1,0:T(8,128)(2,1)S(1)}, u32[]{:S(2)}, u32[]{:S(2)}) %collective-permute-start.5) | collective-permute-done | bytes 131104 | tf_op jit(solution)/shard_map/ppermute | solution.py:64
  96.9 6.0 %fusion.17 = f32[3,384,8,64]{1,3,2,0:T(8,128)S(1)} fusion(bf16[8,64,2048,1]{2,1,0,3:T(8,128)(2,1)} %bitcast.93, bf16[3,384,2048]{2,1,0:T(8,128)(2,1)} %param.6, f32[3,384]{1,0:T(4,128)S(1)} %add_rsqrt_fusion.1), kind=kOutput, calls=%fused_computation.25 | convolution fusion | flops 2422996992 | bytes 9179648 | tf_op jit(solution)/shard_map/dot_general | solution.py:147
  104.3 10.9 %fusion.49 = (f32[3,2,4,384]{3,2,1,0:T(4,128)S(1)}, f32[3,2,4,384,384]{3,4,2,1,0:T(8,128)}) fusion(pred[384,384]{0,1:T(8,128)(4,1)} %iota_compare_fusion, bf16[3,384,2,4,32]{1,4,3,2,0:T(8,128)(2,1)} %bitcast.96, bf16[3,384,2,4,32]{1,4,3,2,0:T(8,128)(2,1)} %bitcast.95, bf16[3,384,2,32]{1,3,2,0:T(8,128)(2,1)} %get-tuple-element.40, ...), kind=kOutput, calls=%fused_computation.167 | convolution fusion | flops 470090112 | bytes 15814656 | tf_op jit(solution)/shard_map/sub | solution.py:45
  115.2 6.6 %fusion.30 = bf16[3,384,2,4,64]{1,4,3,2,0:T(8,128)(2,1)S(1)} fusion(f32[3,2,4,384,384]{3,4,2,1,0:T(8,128)} %get-tuple-element.56, f32[3,2,4,384]{3,2,1,0:T(4,128)S(1)} %get-tuple-element.55, f32[3,384,4,64]{1,3,2,0:T(8,128)} %copy-done.9), kind=kOutput, calls=%fused_computation.33 | convolution fusion | flops 460652544 | bytes 15667200 | tf_op jit(solution)/shard_map/bkgqp,bpkd->bqkgd/dot_general | solution.py:47
  129.2 6.4 %convolution_convert_fusion = bf16[1152,2048]{1,0:T(8,128)(2,1)} fusion(bf16[1152,512]{0,1:T(8,128)(2,1)S(1)} %bitcast.94, bf16[512,2048]{1,0:T(8,128)(2,1)} %constant_dynamic-update-slice_fusion.36), kind=kOutput, calls=%fused_computation.14 | convolution fusion | flops 2418278400 | bytes 7995392 | tf_op jit(solution)/shard_map/dot_general | solution.py:158
  139.2 11.9 %collective-permute-done.29 = bf16[256,2048]{1,0:T(8,128)(2,1)} collective-permute-done((bf16[256,2048]{1,0:T(8,128)(2,1)S(1)}, bf16[256,2048]{1,0:T(8,128)(2,1)}, u32[]{:S(2)}, u32[]{:S(2)}) %collective-permute-start.29) | collective-permute-done | bytes 1048608 | tf_op jit(solution)/shard_map/ppermute | solution.py:64
  156.0 17.6 %collective-permute-done.24 = bf16[256,2048]{1,0:T(8,128)(2,1)} collective-permute-done((bf16[256,2048]{1,0:T(8,128)(2,1)}, bf16[256,2048]{1,0:T(8,128)(2,1)}, u32[]{:S(2)}, u32[]{:S(2)}) %collective-permute-start.24) | collective-permute-done | bytes 1048608 | tf_op jit(solution)/shard_map/ppermute | solution.py:64
  177.8 18.2 %collective-permute-done.31 = bf16[256,2048]{1,0:T(8,128)(2,1)S(1)} collective-permute-done((bf16[256,2048]{1,0:T(8,128)(2,1)}, bf16[256,2048]{1,0:T(8,128)(2,1)S(1)}, u32[]{:S(2)}, u32[]{:S(2)}) %collective-permute-start.31) | collective-permute-done | bytes 1048608 | tf_op jit(solution)/shard_map/ppermute | solution.py:64
  198.0 9.2 %collective-permute-done.37 = bf16[1024,256]{1,0:T(8,128)(2,1)S(1)} collective-permute-done((bf16[1024,256]{1,0:T(8,128)(2,1)S(1)}, bf16[1024,256]{1,0:T(8,128)(2,1)S(1)}, u32[]{:S(2)}, u32[]{:S(2)}) %collective-permute-start.37) | collective-permute-done | bytes 524320 | tf_op jit(solution)/shard_map/ppermute | solution.py:64
  208.6 32.3 %collective-permute-done.38 = bf16[1024,256]{1,0:T(8,128)(2,1)S(1)} collective-permute-done((bf16[1024,256]{1,0:T(8,128)(2,1)S(1)}, bf16[1024,256]{1,0:T(8,128)(2,1)S(1)}, u32[]{:S(2)}, u32[]{:S(2)}) %collective-permute-start.38) | collective-permute-done | bytes 524320 | tf_op jit(solution)/shard_map/ppermute | solution.py:64
  243.4 8.7 %collective-permute-done.49 = bf16[1024,256]{1,0:T(8,128)(2,1)S(1)} collective-permute-done((bf16[1024,256]{1,0:T(8,128)(2,1)S(1)}, bf16[1024,256]{1,0:T(8,128)(2,1)S(1)}, u32[]{:S(2)}, u32[]{:S(2)}) %collective-permute-start.49) | collective-permute-done | bytes 524320 | tf_op jit(solution)/shard_map/ppermute | solution.py:64
  255.5 30.3 %collective-permute-done.50 = bf16[1024,256]{1,0:T(8,128)(2,1)S(1)} collective-permute-done((bf16[1024,256]{1,0:T(8,128)(2,1)S(1)}, bf16[1024,256]{1,0:T(8,128)(2,1)S(1)}, u32[]{:S(2)}, u32[]{:S(2)}) %collective-permute-start.50) | collective-permute-done | bytes 524320 | tf_op jit(solution)/shard_map/ppermute | solution.py:64
  287.3 8.4 %collective-permute-start.62 = (bf16[1024,256]{1,0:T(8,128)(2,1)S(1)}, bf16[1024,256]{1,0:T(8,128)(2,1)S(1)}, u32[]{:S(2)}, u32[]{:S(2)}) collective-permute-start(bf16[1024,256]{1,0:T(8,128)(2,1)S(1)} %collective-permute-done.50), channel_id=1, source_target_pairs={{0,8},{4,12},{8,16},{12,20},{16,24},{20,28},{24,0},{28,4},{1,9},{5... | collective-permute-start | bytes 1572872 | tf_op jit(solution)/shard_map/ppermute | solution.py:64
  301.6 9.8 %collective-permute-done.62 = bf16[1024,256]{1,0:T(8,128)(2,1)S(1)} collective-permute-done((bf16[1024,256]{1,0:T(8,128)(2,1)S(1)}, bf16[1024,256]{1,0:T(8,128)(2,1)S(1)}, u32[]{:S(2)}, u32[]{:S(2)}) %collective-permute-start.62) | collective-permute-done | bytes 524320 | tf_op jit(solution)/shard_map/ppermute | solution.py:64
  317.0 5.9 %fusion.2 = (f32[1152]{0:T(1024)S(1)}, bf16[1152,2048]{1,0:T(8,128)(2,1)S(1)}) fusion(bf16[1152,2048]{1,0:T(8,128)(2,1)} %all-reduce.2.cloned.1.call-done, f32[1152]{0:T(1024)S(1)} %mul.217, bf16[3,384,2048]{2,1,0:T(8,128)(2,1)} %param.6), kind=kLoop, calls=%fused_computation.7 | loop fusion | flops 18873216 | bytes 14164992 | tf_op jit(solution)/shard_map/reduce_sum | solution.py:14
  322.9 14.7 %fusion.23 = f32[1152,2048]{1,0:T(8,128)} fusion(bf16[2048,2048]{1,0:T(8,128)(2,1)} %constant_dynamic-update-slice_fusion.28, bf16[1152,2048]{1,0:T(8,128)(2,1)S(1)} %get-tuple-element.28, f32[1152]{0:T(1024)S(1)} %add_rsqrt_fusion), kind=kOutput, calls=%fused_computation.30 | convolution fusion | flops 9670754304 | bytes 22548992 | tf_op jit(solution)/shard_map/dot_general | solution.py:165
  337.7 15.1 %multiply_convert_fusion = bf16[1152,2048]{1,0:T(8,128)(2,1)S(1)} fusion(f32[1152,2048]{1,0:T(8,128)} %fusion.23, bf16[2048,2048]{1,0:T(8,128)(2,1)} %constant_dynamic-update-slice_fusion.20, bf16[1152,2048]{1,0:T(8,128)(2,1)S(1)} %get-tuple-element.28, f32[1152]{0:T(1024)S(1)} %add_rsqrt_fusion), kind=kOutput, calls=%fused_computation.11 | convolution fusion | flops 9684910080 | bytes 27267584 | tf_op jit(solution)/shard_map/dot_general | solution.py:166
  352.8 5.8 %convolution_convert_fusion.1 = bf16[1152,512]{1,0:T(8,128)(2,1)S(1)} fusion(bf16[1152,2048]{1,0:T(8,128)(2,1)S(1)} %multiply_convert_fusion, bf16[2048,512]{1,0:T(8,128)(2,1)} %constant_dynamic-update-slice_fusion.60), kind=kOutput, calls=%fused_computation.27 | convolution fusion | flops 2416508928 | bytes 7995392 | tf_op jit(solution)/shard_map/dot_general | solution.py:187
  361.9 6.0 %convolution_convert_fusion.2 = bf16[1152,512]{1,0:T(8,128)(2,1)S(1)} fusion(bf16[1152,2048]{1,0:T(8,128)(2,1)} %copy-done.14, bf16[2048,512]{1,0:T(8,128)(2,1)} %constant_dynamic-update-slice_fusion.62), kind=kOutput, calls=%fused_computation.28 | convolution fusion | flops 2416508928 | bytes 7995392 | tf_op jit(solution)/shard_map/dot_general | solution.py:187
  369.3 5.5 %fusion.14 = bf16[1152,1024]{1,0:T(8,128)(2,1)S(1)} fusion(bf16[1152,2048]{1,0:T(8,128)(2,1)S(1)} %bitcast.105, bf16[2048,512]{1,0:T(8,128)(2,1)S(1)} %copy-done.5, bf16[2048,512]{1,0:T(8,128)(2,1)S(1)} %constant_dynamic-update-slice_fusion.66), kind=kOutput, calls=%fused_computation.24 | convolution fusion | flops 4841406464 | bytes 11272192 | tf_op jit(solution)/shard_map/dot_general | solution.py:187
  381.5 14.4 %collective-permute-done.70 = bf16[144,512]{1,0:T(8,128)(2,1)S(1)} collective-permute-done((bf16[144,512]{1,0:T(8,128)(2,1)S(1)}, bf16[144,512]{1,0:T(8,128)(2,1)S(1)}, u32[]{:S(2)}, u32[]{:S(2)}) %collective-permute-start.70) | collective-permute-done | bytes 147488 | tf_op jit(solution)/shard_map/ppermute | solution.py:86
  428.9 6.4 %collective-permute-done.43 = bf16[144,1024]{1,0:T(8,128)(2,1)S(1)} collective-permute-done((bf16[144,1024]{1,0:T(8,128)(2,1)S(1)}, bf16[144,1024]{1,0:T(8,128)(2,1)S(1)}, u32[]{:S(2)}, u32[]{:S(2)}) %collective-permute-start.43) | collective-permute-done | bytes 294944 | tf_op jit(solution)/shard_map/ppermute | solution.py:86
  438.9 8.7 %collective-permute-done.44 = bf16[288,1024]{1,0:T(8,128)(2,1)S(1)} collective-permute-done((bf16[288,1024]{1,0:T(8,128)(2,1)S(1)}, bf16[288,1024]{1,0:T(8,128)(2,1)S(1)}, u32[]{:S(2)}, u32[]{:S(2)}) %collective-permute-start.44) | collective-permute-done | bytes 589856 | tf_op jit(solution)/shard_map/ppermute | solution.py:86
  448.8 8.7 %collective-permute-done.48 = bf16[288,1024]{1,0:T(8,128)(2,1)S(1)} collective-permute-done((bf16[288,1024]{1,0:T(8,128)(2,1)S(1)}, bf16[288,1024]{1,0:T(8,128)(2,1)S(1)}, u32[]{:S(2)}, u32[]{:S(2)}) %collective-permute-start.48) | collective-permute-done | bytes 589856 | tf_op jit(solution)/shard_map/ppermute | solution.py:86
  (323 shorter events, 213.6 us)
Async XLA Ops:
  6.5 310.5 %all-reduce.2.cloned.1.call-start = ((), (), s32[]{:S(2)}) async-start(), calls=%async_computation | async-start | bytes 9437184 | tf_op jit(solution)/shard_map/psum | solution.py:159
  55.1 80.7 %collective-permute-start.21 = (bf16[256,2048]{1,0:T(8,128)(2,1)S(1)}, bf16[256,2048]{1,0:T(8,128)(2,1)S(1)}, u32[]{:S(2)}, u32[]{:S(2)}) collective-permute-start(bf16[256,2048]{1,0:T(8,128)(2,1)S(1)} %bitcast.90), channel_id=1, source_target_pairs={{0,4},{4,0},{8,12},{12,8},{16,20},{20,16},{24,28},{28,24},{1,5},{5... | collective-permute-start | bytes 3145736 | tf_op jit(solution)/shard_map/ppermute | solution.py:71
  74.1 52.7 %collective-permute-start.22 = (bf16[256,2048]{1,0:T(8,128)(2,1)S(1)}, bf16[256,2048]{1,0:T(8,128)(2,1)}, u32[]{:S(2)}, u32[]{:S(2)}) collective-permute-start(bf16[256,2048]{1,0:T(8,128)(2,1)S(1)} %bitcast.92), channel_id=1, source_target_pairs={{0,8},{4,12},{8,16},{12,20},{16,24},{20,28},{24,0},{28,4},{1,9},{5... | collective-permute-start | bytes 3145736 | tf_op jit(solution)/shard_map/ppermute | solution.py:64
  83.5 67.6 %collective-permute-start.28 = (bf16[256,2048]{1,0:T(8,128)(2,1)S(1)}, bf16[256,2048]{1,0:T(8,128)(2,1)}, u32[]{:S(2)}, u32[]{:S(2)}) collective-permute-start(bf16[256,2048]{1,0:T(8,128)(2,1)S(1)} %bitcast.87), channel_id=1, source_target_pairs={{0,4},{4,0},{8,12},{12,8},{16,20},{20,16},{24,28},{28,24},{1,5},{5... | collective-permute-start | bytes 3145736 | tf_op jit(solution)/shard_map/ppermute | solution.py:71
  83.6 39.5 %collective-permute-start.18 = (bf16[512,256]{1,0:T(8,128)(2,1)}, bf16[512,256]{1,0:T(8,128)(2,1)S(1)}, u32[]{:S(2)}, u32[]{:S(2)}) collective-permute-start(bf16[512,256]{1,0:T(8,128)(2,1)} %collective-permute-done.17), channel_id=1, source_target_pairs={{0,4},{4,0},{8,12},{12,8},{16,20},{20,16},{24,28},{28,24},{1,5},{5... | collective-permute-start | bytes 786440 | tf_op jit(solution)/shard_map/ppermute | solution.py:71
  126.7 46.8 %collective-permute-start.24 = (bf16[256,2048]{1,0:T(8,128)(2,1)}, bf16[256,2048]{1,0:T(8,128)(2,1)}, u32[]{:S(2)}, u32[]{:S(2)}) collective-permute-start(bf16[256,2048]{1,0:T(8,128)(2,1)} %collective-permute-done.22), channel_id=1, source_target_pairs={{0,8},{4,12},{8,16},{12,20},{16,24},{20,28},{24,0},{28,4},{1,9},{5... | collective-permute-start | bytes 3145736 | tf_op jit(solution)/shard_map/ppermute | solution.py:64
  135.7 38.1 %collective-permute-start.23 = (bf16[256,2048]{1,0:T(8,128)(2,1)}, bf16[256,2048]{1,0:T(8,128)(2,1)S(1)}, u32[]{:S(2)}, u32[]{:S(2)}) collective-permute-start(bf16[256,2048]{1,0:T(8,128)(2,1)} %collective-permute-done.22), channel_id=1, source_target_pairs={{0,4},{4,0},{8,12},{12,8},{16,20},{20,16},{24,28},{28,24},{1,5},{5... | collective-permute-start | bytes 3145736 | tf_op jit(solution)/shard_map/ppermute | solution.py:71
  151.1 44.8 %collective-permute-start.30 = (bf16[256,2048]{1,0:T(8,128)(2,1)}, bf16[256,2048]{1,0:T(8,128)(2,1)S(1)}, u32[]{:S(2)}, u32[]{:S(2)}) collective-permute-start(bf16[256,2048]{1,0:T(8,128)(2,1)} %collective-permute-done.29), channel_id=1, source_target_pairs={{0,4},{4,0},{8,12},{12,8},{16,20},{20,16},{24,28},{28,24},{1,5},{5... | collective-permute-start | bytes 3145736 | tf_op jit(solution)/shard_map/ppermute | solution.py:71
  151.1 44.8 %collective-permute-start.31 = (bf16[256,2048]{1,0:T(8,128)(2,1)}, bf16[256,2048]{1,0:T(8,128)(2,1)S(1)}, u32[]{:S(2)}, u32[]{:S(2)}) collective-permute-start(bf16[256,2048]{1,0:T(8,128)(2,1)} %collective-permute-done.29), channel_id=1, source_target_pairs={{0,8},{4,12},{8,16},{12,20},{16,24},{20,28},{24,0},{28,4},{1,9},{5... | collective-permute-start | bytes 3145736 | tf_op jit(solution)/shard_map/ppermute | solution.py:64
  173.6 34.9 %collective-permute-start.35 = (bf16[1024,256]{1,0:T(8,128)(2,1)S(1)}, bf16[1024,256]{1,0:T(8,128)(2,1)S(1)}, u32[]{:S(2)}, u32[]{:S(2)}) collective-permute-start(bf16[1024,256]{1,0:T(8,128)(2,1)S(1)} %copy-done.7), channel_id=1, source_target_pairs={{0,4},{4,0},{8,12},{12,8},{16,20},{20,16},{24,28},{28,24},{1,5},{5... | collective-permute-start | bytes 1572872 | tf_op jit(solution)/shard_map/ppermute | solution.py:71
  173.8 67.3 %collective-permute-start.25 = (bf16[256,2048]{1,0:T(8,128)(2,1)}, bf16[256,2048]{1,0:T(8,128)(2,1)S(1)}, u32[]{:S(2)}, u32[]{:S(2)}) collective-permute-start(bf16[256,2048]{1,0:T(8,128)(2,1)} %collective-permute-done.24), channel_id=1, source_target_pairs={{0,4},{4,0},{8,12},{12,8},{16,20},{20,16},{24,28},{28,24},{1,5},{5... | collective-permute-start | bytes 3145736 | tf_op jit(solution)/shard_map/ppermute | solution.py:71
  195.9 45.7 %collective-permute-start.26 = (bf16[256,2048]{1,0:T(8,128)(2,1)}, bf16[256,2048]{1,0:T(8,128)(2,1)S(1)}, u32[]{:S(2)}, u32[]{:S(2)}) collective-permute-start(bf16[256,2048]{1,0:T(8,128)(2,1)} %collective-permute-done.24), channel_id=1, source_target_pairs={{0,8},{4,12},{8,16},{12,20},{16,24},{20,28},{24,0},{28,4},{1,9},{5... | collective-permute-start | bytes 3145736 | tf_op jit(solution)/shard_map/ppermute | solution.py:64
  195.9 44.9 %collective-permute-start.38 = (bf16[1024,256]{1,0:T(8,128)(2,1)S(1)}, bf16[1024,256]{1,0:T(8,128)(2,1)S(1)}, u32[]{:S(2)}, u32[]{:S(2)}) collective-permute-start(bf16[1024,256]{1,0:T(8,128)(2,1)S(1)} %copy-done.6), channel_id=1, source_target_pairs={{0,8},{4,12},{8,16},{12,20},{16,24},{20,28},{24,0},{28,4},{1,9},{5... | collective-permute-start | bytes 1572872 | tf_op jit(solution)/shard_map/ppermute | solution.py:64
  208.5 43.6 %collective-permute-start.49 = (bf16[1024,256]{1,0:T(8,128)(2,1)S(1)}, bf16[1024,256]{1,0:T(8,128)(2,1)S(1)}, u32[]{:S(2)}, u32[]{:S(2)}) collective-permute-start(bf16[1024,256]{1,0:T(8,128)(2,1)S(1)} %collective-permute-done.37), channel_id=1, source_target_pairs={{0,8},{4,12},{8,16},{12,20},{16,24},{20,28},{24,0},{28,4},{1,9},{5... | collective-permute-start | bytes 1572872 | tf_op jit(solution)/shard_map/ppermute | solution.py:64
  240.9 46.5 %collective-permute-start.32 = (bf16[256,2048]{1,0:T(8,128)(2,1)S(1)}, bf16[256,2048]{1,0:T(8,128)(2,1)S(1)}, u32[]{:S(2)}, u32[]{:S(2)}) collective-permute-start(bf16[256,2048]{1,0:T(8,128)(2,1)S(1)} %collective-permute-done.31), channel_id=1, source_target_pairs={{0,4},{4,0},{8,12},{12,8},{16,20},{20,16},{24,28},{28,24},{1,5},{5... | collective-permute-start | bytes 3145736 | tf_op jit(solution)/shard_map/ppermute | solution.py:71
  240.9 55.9 %collective-permute-start.33 = (bf16[256,2048]{1,0:T(8,128)(2,1)S(1)}, bf16[256,2048]{1,0:T(8,128)(2,1)S(1)}, u32[]{:S(2)}, u32[]{:S(2)}) collective-permute-start(bf16[256,2048]{1,0:T(8,128)(2,1)S(1)} %collective-permute-done.31), channel_id=1, source_target_pairs={{0,8},{4,12},{8,16},{12,20},{16,24},{20,28},{24,0},{28,4},{1,9},{5... | collective-permute-start | bytes 3145736 | tf_op jit(solution)/shard_map/ppermute | solution.py:64
  241.6 44.2 %collective-permute-start.50 = (bf16[1024,256]{1,0:T(8,128)(2,1)S(1)}, bf16[1024,256]{1,0:T(8,128)(2,1)S(1)}, u32[]{:S(2)}, u32[]{:S(2)}) collective-permute-start(bf16[1024,256]{1,0:T(8,128)(2,1)S(1)} %collective-permute-done.38), channel_id=1, source_target_pairs={{0,8},{4,12},{8,16},{12,20},{16,24},{20,28},{24,0},{28,4},{1,9},{5... | collective-permute-start | bytes 1572872 | tf_op jit(solution)/shard_map/ppermute | solution.py:64
  255.5 41.4 %collective-permute-start.61 = (bf16[1024,256]{1,0:T(8,128)(2,1)S(1)}, bf16[1024,256]{1,0:T(8,128)(2,1)S(1)}, u32[]{:S(2)}, u32[]{:S(2)}) collective-permute-start(bf16[1024,256]{1,0:T(8,128)(2,1)S(1)} %collective-permute-done.49), channel_id=1, source_target_pairs={{0,8},{4,12},{8,16},{12,20},{16,24},{20,28},{24,0},{28,4},{1,9},{5... | collective-permute-start | bytes 1572872 | tf_op jit(solution)/shard_map/ppermute | solution.py:64
  375.0 37.3 %collective-permute-start.45 = (bf16[288,1024]{1,0:T(8,128)(2,1)S(1)}, bf16[288,1024]{1,0:T(8,128)(2,1)S(1)}, u32[]{:S(2)}, u32[]{:S(2)}) collective-permute-start(bf16[288,1024]{1,0:T(8,128)(2,1)S(1)} %constant_dynamic-slice_fusion.9), channel_id=1, source_target_pairs={{0,2},{1,3},{2,0},{3,1},{4,6},{5,7},{6,4},{7,5},{8,10},{9,11},{10,... | collective-permute-start | bytes 1769480 | tf_op jit(solution)/shard_map/ppermute | solution.py:86
  376.6 35.0 %collective-permute-start.41 = (bf16[288,1024]{1,0:T(8,128)(2,1)S(1)}, bf16[288,1024]{1,0:T(8,128)(2,1)S(1)}, u32[]{:S(2)}, u32[]{:S(2)}) collective-permute-start(bf16[288,1024]{1,0:T(8,128)(2,1)S(1)} %constant_dynamic-slice_fusion.12), channel_id=1, source_target_pairs={{0,1},{1,0},{2,3},{3,2},{4,5},{5,4},{6,7},{7,6},{8,9},{9,8},{10,11... | collective-permute-start | bytes 1769480 | tf_op jit(solution)/shard_map/ppermute | solution.py:86
  411.6 50.5 %collective-permute-start.56 = (bf16[288,512]{1,0:T(8,128)(2,1)S(1)}, bf16[288,512]{1,0:T(8,128)(2,1)S(1)}, u32[]{:S(2)}, u32[]{:S(2)}) collective-permute-start(bf16[288,512]{1,0:T(8,128)(2,1)S(1)} %constant_dynamic-update-slice_fusion.8), channel_id=1, source_target_pairs={{0,1},{1,0},{2,3},{3,2},{4,5},{5,4},{6,7},{7,6},{8,9},{9,8},{10,11... | collective-permute-start | bytes 884744 | tf_op jit(solution)/shard_map/ppermute | solution.py:86
  422.3 48.9 %collective-permute-start.60 = (bf16[288,512]{1,0:T(8,128)(2,1)S(1)}, bf16[288,512]{1,0:T(8,128)(2,1)S(1)}, u32[]{:S(2)}, u32[]{:S(2)}) collective-permute-start(bf16[288,512]{1,0:T(8,128)(2,1)S(1)} %constant_dynamic-update-slice_fusion.6), channel_id=1, source_target_pairs={{0,2},{1,3},{2,0},{3,1},{4,6},{5,7},{6,4},{7,5},{8,10},{9,11},{10,... | collective-permute-start | bytes 884744 | tf_op jit(solution)/shard_map/ppermute | solution.py:86
  428.3 51.3 %collective-permute-start.68 = (bf16[288,512]{1,0:T(8,128)(2,1)S(1)}, bf16[288,512]{1,0:T(8,128)(2,1)S(1)}, u32[]{:S(2)}, u32[]{:S(2)}) collective-permute-start(bf16[288,512]{1,0:T(8,128)(2,1)S(1)} %constant_dynamic-update-slice_fusion.2), channel_id=1, source_target_pairs={{0,1},{1,0},{2,3},{3,2},{4,5},{5,4},{6,7},{7,6},{8,9},{9,8},{10,11... | collective-permute-start | bytes 884744 | tf_op jit(solution)/shard_map/ppermute | solution.py:86
  435.4 53.1 %collective-permute-start.72 = (bf16[288,512]{1,0:T(8,128)(2,1)S(1)}, bf16[288,512]{1,0:T(8,128)(2,1)S(1)}, u32[]{:S(2)}, u32[]{:S(2)}) collective-permute-start(bf16[288,512]{1,0:T(8,128)(2,1)S(1)} %constant_dynamic-update-slice_fusion), channel_id=1, source_target_pairs={{0,2},{1,3},{2,0},{3,1},{4,6},{5,7},{6,4},{7,5},{8,10},{9,11},{10,... | collective-permute-start | bytes 884744 | tf_op jit(solution)/shard_map/ppermute | solution.py:86
  (67 other events, 1053.7 us)
Sparse Core Ops, SparseCore 0:
  135.8 112.1 all-reduce.1

commit v3 on v2

--- a/solution.py
+++ b/solution.py
@@ -54,14 +54,15 @@
     return lax.optimization_barrier((tensor, earlier))[0]
 
 
-def ring(shard, earlier):
+def ring(shard, earlier=None, gates=()):
     var_count = lax.axis_size("var")
     forward = [(i, (i + CORES) % var_count) for i in range(var_count)]
-    if earlier is not None:
-        shard = after(shard, earlier)
-    held = [shard]
-    for _ in range(var_count // CORES - 1):
-        held.append(lax.ppermute(held[-1], "var", forward))
+    hops = var_count // CORES - 1
+    held = [shard if earlier is None else after(shard, earlier)]
+    for hop in range(hops):
+        gate = hop - (hops - len(gates))
+        sent = held[-1] if gate < 0 else after(held[-1], gates[gate])
+        held.append(lax.ppermute(sent, "var", forward))
     return held
 
 
@@ -104,13 +105,19 @@
 
 
 def gather_rows(rows, bits):
-    for bit in bits[:0:-1]:
-        half = rows.shape[0]
-        mine = side(bit)
-        joined = jnp.zeros((2 * half,) + rows.shape[1:], rows.dtype)
-        joined = lax.dynamic_update_slice_in_dim(joined, rows, mine * half, axis=0)
-        rows = lax.dynamic_update_slice_in_dim(joined, partner(rows, bit), (1 - mine) * half, axis=0)
-    return rows, partner(rows, bits[0]), side(bits[0])
+    for bit in bits[::-1]:
+        other = partner(rows, bit)
+        lower = side(bit) == 0
+        rows = jnp.concatenate([jnp.where(lower, rows, other), jnp.where(lower, other, rows)], axis=0)
+    return rows
+
+
+def add_sum(terms, base, switch, bits):
+    total, start = scatter_rows(terms, bits)
+    count = total.shape[0]
+    own = lax.dynamic_slice_in_dim(base, start, count, axis=0).astype(jnp.float32)
+    own_switch = lax.dynamic_slice_in_dim(switch, start, count, axis=0)
+    return gather_rows((own + own_switch * total).astype(jnp.bfloat16), bits)
 
 
 def shards(hidden_in, run_table, qkv_weight, out_weight, gate_up_weight, down_weight):
@@ -126,14 +133,11 @@
     bf16 = jnp.bfloat16
 
     query_width = query_slice * HEAD_SIZE
-    half_ff = down_weight.shape[0] // 2
-    q_ring = ring(qkv_weight[:, :query_width], None)
-    kv_ring = ring(qkv_weight[:, query_width:], None)
-    out_ring = ring(out_weight, kv_ring[-1])
+    q_ring = ring(qkv_weight[:, :query_width])
+    kv_ring = ring(qkv_weight[:, query_width:])
+    out_ring = ring(out_weight, kv_ring[-2])
     gate_ring = ring(gate_up_weight[:, 0, :], q_ring[-2])
-    up_ring = ring(gate_up_weight[:, 1, :], out_ring[-2])
-    down_a_ring = ring(down_weight[:half_ff], gate_ring[-2])
-    down_b_ring = ring(down_weight[half_ff:], up_ring[-2])
+    up_ring = ring(gate_up_weight[:, 1, :], kv_ring[-1])
 
     me = lax.axis_index("var")
     chip, core = me // CORES, me % CORES
@@ -155,59 +159,64 @@
     values_bfloat = keys_values[:, :, key_value_slice:].astype(bf16)
     head_outputs = attend(query_rows, keys_bfloat, values_bfloat, HEAD_SIZE ** (-0.5))
     head_rows = head_outputs.reshape(row_count, query_width)
-    attn_terms = jnp.dot(head_rows, whole(out_ring, 1), preferred_element_type=jnp.float32)
-    attention = lax.psum(attn_terms.astype(bf16), "tp").astype(jnp.float32)
+    attn_terms = jnp.dot(head_rows, whole(out_ring, 1), preferred_element_type=jnp.float32).astype(bf16)
     attn_switch = jnp.repeat(switches[:, 0], full_len)[:, None]
     flat_in = hidden_in.reshape(row_count, model_width)
-    whole_after = (flat_in.astype(jnp.float32) + attn_switch * attention).astype(bf16)
+    forth = list(range(tensor_parallel_count.bit_length() - 1))
+    half_width = model_width // 2
+    whole_after = jnp.concatenate(
+        [
+            add_sum(attn_terms[:, :half_width], flat_in[:, :half_width], attn_switch, forth),
+            add_sum(attn_terms[:, half_width:], flat_in[:, half_width:], attn_switch, forth[::-1]),
+        ],
+        axis=1,
+    )
 
     mlp_input = rms_norm(whole_after)
     gate = jnp.dot(mlp_input, whole(gate_ring, 0), preferred_element_type=jnp.float32)
     up = jnp.dot(mlp_input, whole(up_ring, 0), preferred_element_type=jnp.float32)
     hidden = (jax.nn.silu(gate) * up).astype(bf16)
 
+    half_ff = down_weight.shape[0] // 2
+    gates = (whole_after, gate)
+    down_a_ring = ring(down_weight[:half_ff], gate_ring[-2], gates)
+    down_b_ring = ring(down_weight[half_ff:], up_ring[-2], gates)
+    down_a_swap, down_b_swap = swap(down_a_ring), swap(down_b_ring)
     mlp_switch = jnp.repeat(switches[:, 1], full_len)[:, None]
-    down_a_swap, down_b_swap = swap(down_a_ring), swap(down_b_ring)
     width = model_width // chip_count
-    forth = list(range(tensor_parallel_count.bit_length() - 1))
+    half_rows = row_count // 2
     early = chip_count // 2
+    first_core = core == 0
     layer_out = jnp.zeros((row_count, model_width), bf16)
-    for steps in [list(range(early))] + [[step] for step in range(early, chip_count)]:
+    for steps in (range(early), range(early, chip_count)):
         down_blocks = []
         for step in steps:
-            pair = jnp.zeros((2 * half_ff, width), bf16)
-            for tensor, row, place in (
-                (down_a_ring, 0, core),
-                (down_b_ring, half_ff, core),
-                (down_a_swap, 0, 1 - core),
-                (down_b_swap, half_ff, 1 - core),
-            ):
-                pair = lax.dynamic_update_slice(pair, tensor[step], (row, place * (width // CORES)))
-            down_blocks.append(pair)
-        terms = jnp.dot(
-            hidden, jnp.concatenate(down_blocks, axis=1), preferred_element_type=jnp.float32
-        ).astype(bf16)
-        half_rows = row_count // 2
-        for row, bits in ((0, forth), (half_rows, forth[::-1])):
-            mlp, start = scatter_rows(terms[row : row + half_rows], bits)
-            count = mlp.shape[0]
-            residual = jnp.concatenate(
-                [
-                    lax.dynamic_slice(whole_after, (row + start, origins[step] * width), (count, width))
-                    for step in steps
-                ],
+            mine = jnp.concatenate([down_a_ring[step], down_b_ring[step]], axis=0)
+            other = jnp.concatenate([down_a_swap[step], down_b_swap[step]], axis=0)
+            down_blocks += [jnp.where(first_core, mine, other), jnp.where(first_core, other, mine)]
+        down_blocks = jnp.concatenate(down_blocks, axis=1)
+        terms = jnp.dot(hidden, down_blocks, preferred_element_type=jnp.float32).astype(bf16)
+        base = jnp.concatenate(
+            [
+                lax.dynamic_slice_in_dim(whole_after, origins[step] * width, width, axis=1)
+                for step in steps
+            ],
+            axis=1,
+        )
+        result = jnp.concatenate(
+            [
+                add_sum(terms[:half_rows], base[:half_rows], mlp_switch[:half_rows], forth),
+                add_sum(terms[half_rows:], base[half_rows:], mlp_switch[half_rows:], forth[::-1]),
+            ],
+            axis=0,
+        )
+        for number, step in enumerate(steps):
+            layer_out = lax.dynamic_update_slice_in_dim(
+                layer_out,
+                result[:, number * width : (number + 1) * width],
+                origins[step] * width,
                 axis=1,
             )
-            switch = lax.dynamic_slice_in_dim(mlp_switch, row + start, count, axis=0)
-            result = (residual.astype(jnp.float32) + switch * mlp).astype(bf16)
-            near, far, first = gather_rows(result, bits)
-            for part, lower in ((near, first), (far, 1 - first)):
-                for number, step in enumerate(steps):
-                    layer_out = lax.dynamic_update_slice(
-                        layer_out,
-                        part[:, number * width : (number + 1) * width],
-                        (row + lower * part.shape[0], origins[step] * width),
-                    )
     return layer_out.reshape(seq_count, full_len, model_width)
 
 

time: 510 us -> 482 us (0.945)
  local copies, waits for them, and re-layouts: 128 us -> 89.5 us
  other arithmetic: 14 us -> 37.6 us
  waiting for transfers between devices: 208 us -> 223 us
  between operations: 15 us -> 1.86 us
  matrix products: 81.4 us -> 71.3 us
  starting transfers between devices: 55.3 us -> 49.8 us
    dynamic_update_slice x38 -> x4, local copies, waits for them, and re-layouts: 42.3 us -> 0.87 us  [shards(): lax.dynamic_update_slice_in_dim(layer_out, result[:, number * width:(numb...]
    ppermute x21, starting transfers between devices: 24.2 us -> 12.2 us  [ring(): held.append(lax.ppermute(sent, 'var', forward))]
    reduce_sum x2, other arithmetic: 9.25 us -> 20.3 us  [rms_norm(): jnp.mean(widened * widened, axis=-1, keepdims=True) + 1e-05]
    dynamic_update_slice x40, local copies, waits for them, and re-layouts: 47.2 us -> 37 us  [assemble(): lax.dynamic_update_slice_in_dim(whole, shard, place * block, axis=axis)]
    slice x7 -> x15, local copies, waits for them, and re-layouts: 6.58 us -> 16.2 us  [the longest x1 5.27 us: shards(): flat_in[:, :half_width]]
    ppermute x24, waiting for transfers between devices: 57.6 us -> 65.8 us  [partner(): return lax.ppermute(tensor, 'tp', pairs)]
    another operation x13 -> x2, local copies, waits for them, and re-layouts: 13.6 us -> 5.37 us
    ppermute x24, starting transfers between devices: 26 us -> 33.1 us  [partner(): return lax.ppermute(tensor, 'tp', pairs)]
  transfers between devices with their start and end apart: 74 -> 73, of which waited for: 22 -> 26; matrix products, arithmetic and copies ran while one was open for 34% -> 30% of each run, Pallas kernels for 0% -> 0%
where the time goes in v3:
time: 482 us; the launch traced here: 473 us
  waiting for transfers between devices  223 us (46%)
  local copies, waits for them, and re-layouts  89.5 us (19%)
  matrix products  71.3 us (15%)
  starting transfers between devices  49.8 us (10%)
  other arithmetic  37.6 us (8%)
    ppermute x21, waiting for transfers between devices, ring(): held.append(lax.ppermute(sent, 'var', forward))  154 us
    ppermute x24, waiting for transfers between devices, partner(): return lax.ppermute(tensor, 'tp', pairs)  65.8 us
    dynamic_update_slice x40, local copies, waits for them, and re-layouts, assemble(): lax.dynamic_update_slice_in_dim(whole, shard, place * block, axis=axis)  37 us
    ppermute x24, starting transfers between devices, partner(): return lax.ppermute(tensor, 'tp', pairs)  33.1 us
    reduce_sum x2, other arithmetic, rms_norm(): jnp.mean(widened * widened, axis=-1, keepdims=True) + 1e-05  20.3 us
    dot_general x1, matrix products, shards(): jnp.dot(mlp_input, whole(up_ring, 0), preferred_element_type=jnp.float32)  15.1 us
    dot_general x1, matrix products, shards(): jnp.dot(mlp_input, whole(gate_ring, 0), preferred_element_type=jnp.float32)  12.7 us
    ppermute x21, starting transfers between devices, ring(): held.append(lax.ppermute(sent, 'var', forward))  12.2 us
  transfers between devices with their start and end apart: 73, of which 26 were waited for; matrix products, arithmetic and copies ran while one was open for 30% of the time, Pallas kernels for 0%

profile of v3, /device:TPU:0, one launch (start us, length us, event | category | flops | bytes accessed | tf_op | source)
XLA Modules:
  0.0 473.1 jit_solution(10571859916301035002)
XLA Ops:
  13.2 5.3 %fusion.64 = (bf16[1152,1024]{1,0:T(8,128)(2,1)}, bf16[1152,1024]{1,0:T(8,128)(2,1)}) fusion(bf16[1152,2048]{1,0:T(8,128)(2,1)} %bitcast.85), kind=kLoop, calls=%fused_computation.220 | loop fusion | bytes 9437184 | tf_op jit(solution)/shard_map/slice | solution.py:169
  53.7 4.3 broadcast.78.clone.1
  94.2 6.0 %fusion.33 = f32[3,384,8,64]{1,3,2,0:T(8,128)S(1)} fusion(bf16[8,64,2048,1]{2,1,0,3:T(8,128)(2,1)} %bitcast.93, bf16[3,384,2048]{2,1,0:T(8,128)(2,1)} %param.6, f32[3,384]{1,0:T(4,128)S(1)} %copy-done.15), kind=kOutput, calls=%fused_computation.39 | convolution fusion | flops 2422996992 | bytes 9179648 | tf_op jit(solution)/shard_map/dot_general | solution.py:151
  101.6 10.9 %fusion.71 = (f32[3,2,4,384]{3,2,1,0:T(4,128)S(1)}, f32[3,2,4,384,384]{3,4,2,1,0:T(8,128)}) fusion(pred[384,384]{0,1:T(8,128)(4,1)S(1)} %copy-done.14, bf16[3,384,2,4,32]{1,4,3,2,0:T(8,128)(2,1)} %bitcast.96, bf16[3,384,2,4,32]{1,4,3,2,0:T(8,128)(2,1)} %bitcast.95, bf16[3,384,2,32]{1,3,2,0:T(8,128)(2,1)} %get-tuple-element.56, ...), kind=kOutput, calls=%fused_computation.227 | convolution fusion | flops 470090112 | bytes 15814656 | tf_op jit(solution)/shard_map/sub | solution.py:45
  114.1 6.6 %fusion.46 = bf16[3,384,2,4,64]{1,4,3,2,0:T(8,128)(2,1)S(1)} fusion(f32[3,2,4,384,384]{3,4,2,1,0:T(8,128)} %get-tuple-element.90, f32[3,2,4,384]{3,2,1,0:T(4,128)S(1)} %get-tuple-element.89, f32[3,384,4,64]{1,3,2,0:T(8,128)} %copy-done.13), kind=kOutput, calls=%fused_computation.53 | convolution fusion | flops 460652544 | bytes 15667200 | tf_op jit(solution)/shard_map/bkgqp,bpkd->bqkgd/dot_general | solution.py:47
  141.2 9.1 %collective-permute-done.30 = bf16[256,2048]{1,0:T(8,128)(2,1)} collective-permute-done((bf16[256,2048]{1,0:T(8,128)(2,1)S(1)}, bf16[256,2048]{1,0:T(8,128)(2,1)}, u32[]{:S(2)}, u32[]{:S(2)}) %collective-permute-start.30) | collective-permute-done | bytes 1048608 | tf_op jit(solution)/shard_map/ppermute | solution.py:65
  153.0 19.3 %collective-permute-done.39 = bf16[256,2048]{1,0:T(8,128)(2,1)S(1)} collective-permute-done((bf16[256,2048]{1,0:T(8,128)(2,1)}, bf16[256,2048]{1,0:T(8,128)(2,1)S(1)}, u32[]{:S(2)}, u32[]{:S(2)}) %collective-permute-start.39) | collective-permute-done | bytes 1048608 | tf_op jit(solution)/shard_map/ppermute | solution.py:65
  177.3 23.1 %collective-permute-done.32 = bf16[256,2048]{1,0:T(8,128)(2,1)S(1)} collective-permute-done((bf16[256,2048]{1,0:T(8,128)(2,1)}, bf16[256,2048]{1,0:T(8,128)(2,1)S(1)}, u32[]{:S(2)}, u32[]{:S(2)}) %collective-permute-start.32) | collective-permute-done | bytes 1048608 | tf_op jit(solution)/shard_map/ppermute | solution.py:65
  203.7 9.5 %collective-permute-done.26 = bf16[288,1024]{1,0:T(8,128)(2,1)S(1)} collective-permute-done((bf16[288,1024]{1,0:T(8,128)(2,1)S(1)}, bf16[288,1024]{1,0:T(8,128)(2,1)S(1)}, u32[]{:S(2)}, u32[]{:S(2)}) %collective-permute-start.26) | collective-permute-done | bytes 589856 | tf_op jit(solution)/shard_map/ppermute | solution.py:87
  214.5 7.0 %collective-permute-done.45 = bf16[1024,256]{1,0:T(8,128)(2,1)S(1)} collective-permute-done((bf16[1024,256]{1,0:T(8,128)(2,1)S(1)}, bf16[1024,256]{1,0:T(8,128)(2,1)S(1)}, u32[]{:S(2)}, u32[]{:S(2)}) %collective-permute-start.45) | collective-permute-done | bytes 524320 | tf_op jit(solution)/shard_map/ppermute | solution.py:65
  226.3 23.2 %collective-permute-done.41 = bf16[256,2048]{1,0:T(8,128)(2,1)S(1)} collective-permute-done((bf16[256,2048]{1,0:T(8,128)(2,1)S(1)}, bf16[256,2048]{1,0:T(8,128)(2,1)S(1)}, u32[]{:S(2)}, u32[]{:S(2)}) %collective-permute-start.41) | collective-permute-done | bytes 1048608 | tf_op jit(solution)/shard_map/ppermute | solution.py:65
  255.0 14.8 %collective-permute-done.34 = bf16[256,2048]{1,0:T(8,128)(2,1)S(1)} collective-permute-done((bf16[256,2048]{1,0:T(8,128)(2,1)S(1)}, bf16[256,2048]{1,0:T(8,128)(2,1)S(1)}, u32[]{:S(2)}, u32[]{:S(2)}) %collective-permute-start.34) | collective-permute-done | bytes 1048608 | tf_op jit(solution)/shard_map/ppermute | solution.py:65
  272.5 7.3 %collective-permute-done.24 = bf16[576,1024]{1,0:T(8,128)(2,1)S(1)} collective-permute-done((bf16[576,1024]{1,0:T(8,128)(2,1)S(1)}, bf16[576,1024]{1,0:T(8,128)(2,1)S(1)}, u32[]{:S(2)}, u32[]{:S(2)}) %collective-permute-start.24) | collective-permute-done | bytes 1179680 | tf_op jit(solution)/shard_map/ppermute | solution.py:87
  282.0 16.9 %fusion.4 = (f32[1152]{0:T(1024)S(1)}, bf16[1152,2048]{1,0:T(8,128)(2,1)S(1)}) fusion(bf16[576,1024]{1,0:T(8,128)(2,1)S(1)} %get-tuple-element.44, bf16[576,1024]{1,0:T(8,128)(2,1)S(1)} %get-tuple-element.43, bf16[576,1024]{1,0:T(8,128)(2,1)S(1)} %get-tuple-element.42, bf16[576,1024]{1,0:T(8,128)(2,1)S(1)} %get-tuple-element.41), kind=kLoop, calls=%fused_computation.11 | loop fusion | flops 25951104 | bytes 9441792 | tf_op jit(solution)/shard_map/reduce_sum | solution.py:14
  299.0 12.7 %fusion.39 = f32[1152,2048]{1,0:T(8,128)} fusion(bf16[2048,2048]{1,0:T(8,128)(2,1)S(1)} %constant_dynamic-update-slice_fusion.24, bf16[1152,2048]{1,0:T(8,128)(2,1)S(1)} %get-tuple-element.26, f32[1152]{0:T(1024)S(1)} %add_rsqrt_fusion), kind=kOutput, calls=%fused_computation.50 | convolution fusion | flops 9670754304 | bytes 22548992 | tf_op jit(solution)/shard_map/dot_general | solution.py:176
  311.7 15.1 %multiply_convert_fusion = bf16[1152,2048]{1,0:T(8,128)(2,1)S(1)} fusion(f32[1152,2048]{1,0:T(8,128)} %fusion.39, bf16[2048,2048]{1,0:T(8,128)(2,1)} %constant_dynamic-update-slice_fusion.16, bf16[1152,2048]{1,0:T(8,128)(2,1)S(1)} %get-tuple-element.26, f32[1152]{0:T(1024)S(1)} %add_rsqrt_fusion), kind=kOutput, calls=%fused_computation.13 | convolution fusion | flops 9684910080 | bytes 27267584 | tf_op jit(solution)/shard_map/dot_general | solution.py:177
  326.8 5.6 %fusion.30 = bf16[1152,1024]{1,0:T(8,128)(2,1)S(1)} fusion(bf16[1152,2048]{1,0:T(8,128)(2,1)S(1)} %multiply_convert_fusion, bf16[2048,256]{1,0:T(8,128)(2,1)S(1)} %get-tuple-element.52, bf16[2048,256]{1,0:T(8,128)(2,1)S(1)} %get-tuple-element.51, bf16[2048,256]{1,0:T(8,128)(2,1)S(1)} %get-tuple-element.50, bf16[2048,256]{1,0:T(8,128)(2,1)S(1)} %get-tuple-element.49), kind=kOutput, calls=%fused_computation.38 | convolution fusion | flops 4849795072 | bytes 11272192 | tf_op jit(solution)/shard_map/dot_general | solution.py:198
  335.6 24.2 %collective-permute-done.58 = bf16[1024,256]{1,0:T(8,128)(2,1)S(1)} collective-permute-done((bf16[1024,256]{1,0:T(8,128)(2,1)S(1)}, bf16[1024,256]{1,0:T(8,128)(2,1)S(1)}, u32[]{:S(2)}, u32[]{:S(2)}) %collective-permute-start.58) | collective-permute-done | bytes 524320 | tf_op jit(solution)/shard_map/ppermute | solution.py:65
  362.4 14.1 %collective-permute-done.62 = bf16[1024,256]{1,0:T(8,128)(2,1)S(1)} collective-permute-done((bf16[1024,256]{1,0:T(8,128)(2,1)S(1)}, bf16[1024,256]{1,0:T(8,128)(2,1)S(1)}, u32[]{:S(2)}, u32[]{:S(2)}) %collective-permute-start.62) | collective-permute-done | bytes 524320 | tf_op jit(solution)/shard_map/ppermute | solution.py:65
  376.5 8.5 %collective-permute-done.61 = bf16[1024,256]{1,0:T(8,128)(2,1)S(1)} collective-permute-done((bf16[1024,256]{1,0:T(8,128)(2,1)S(1)}, bf16[1024,256]{1,0:T(8,128)(2,1)S(1)}, u32[]{:S(2)}, u32[]{:S(2)}) %collective-permute-start.61) | collective-permute-done | bytes 524320 | tf_op jit(solution)/shard_map/ppermute | solution.py:65
  387.4 5.8 %fusion.27 = bf16[1152,1024]{1,0:T(8,128)(2,1)S(1)} fusion(bf16[1152,2048]{1,0:T(8,128)(2,1)S(1)} %bitcast.102, bf16[2048,256]{1,0:T(8,128)(2,1)S(1)} %get-tuple-element.48, bf16[2048,256]{1,0:T(8,128)(2,1)S(1)} %get-tuple-element.47, bf16[2048,256]{1,0:T(8,128)(2,1)S(1)} %get-tuple-element.46, bf16[2048,256]{1,0:T(8,128)(2,1)S(1)} %get-tuple-element.45), kind=kOutput, calls=%fused_computation.37 | convolution fusion | flops 4849795072 | bytes 11272192 | tf_op jit(solution)/shard_map/dot_general | solution.py:198
  398.9 10.8 %collective-permute-done.65 = bf16[288,1024]{1,0:T(8,128)(2,1)S(1)} collective-permute-done((bf16[288,1024]{1,0:T(8,128)(2,1)S(1)}, bf16[288,1024]{1,0:T(8,128)(2,1)S(1)}, u32[]{:S(2)}, u32[]{:S(2)}) %collective-permute-start.65) | collective-permute-done | bytes 589856 | tf_op jit(solution)/shard_map/ppermute | solution.py:87
  411.6 5.1 %collective-permute-done.69 = bf16[288,1024]{1,0:T(8,128)(2,1)S(1)} collective-permute-done((bf16[288,1024]{1,0:T(8,128)(2,1)S(1)}, bf16[288,1024]{1,0:T(8,128)(2,1)S(1)}, u32[]{:S(2)}, u32[]{:S(2)}) %collective-permute-start.69) | collective-permute-done | bytes 589856 | tf_op jit(solution)/shard_map/ppermute | solution.py:87
  446.3 21.0 %collective-permute-done.52 = bf16[288,1024]{1,0:T(8,128)(2,1)S(1)} collective-permute-done((bf16[288,1024]{1,0:T(8,128)(2,1)S(1)}, bf16[288,1024]{1,0:T(8,128)(2,1)S(1)}, u32[]{:S(2)}, u32[]{:S(2)}) %collective-permute-start.52) | collective-permute-done | bytes 589856 | tf_op jit(solution)/shard_map/ppermute | solution.py:87
  (337 shorter events, 184.8 us)
Async XLA Ops:
  1.7 43.6 %collective-permute-start.7 = (bf16[256,512]{1,0:T(8,128)(2,1)}, bf16[256,512]{1,0:T(8,128)(2,1)}, u32[]{:S(2)}, u32[]{:S(2)}) collective-permute-start(bf16[256,512]{1,0:T(8,128)(2,1)} %slice.105), channel_id=1, source_target_pairs={{0,4},{4,0},{8,12},{12,8},{16,20},{20,16},{24,28},{28,24},{1,5},{5... | collective-permute-start | bytes 786440 | tf_op jit(solution)/shard_map/ppermute | solution.py:72
  2.1 45.0 %collective-permute-start.8 = (bf16[256,512]{1,0:T(8,128)(2,1)}, bf16[256,512]{1,0:T(8,128)(2,1)}, u32[]{:S(2)}, u32[]{:S(2)}) collective-permute-start(bf16[256,512]{1,0:T(8,128)(2,1)} %slice.105), channel_id=1, source_target_pairs={{0,8},{4,12},{8,16},{12,20},{16,24},{20,28},{24,0},{28,4},{1,9},{5... | collective-permute-start | bytes 786440 | tf_op jit(solution)/shard_map/ppermute | solution.py:65
  40.0 34.8 %collective-permute-start.14 = (bf16[512,256]{1,0:T(8,128)(2,1)}, bf16[512,256]{1,0:T(8,128)(2,1)}, u32[]{:S(2)}, u32[]{:S(2)}) collective-permute-start(bf16[512,256]{1,0:T(8,128)(2,1)} %param.9), channel_id=1, source_target_pairs={{0,4},{4,0},{8,12},{12,8},{16,20},{20,16},{24,28},{28,24},{1,5},{5... | collective-permute-start | bytes 786440 | tf_op jit(solution)/shard_map/ppermute | solution.py:72
  40.0 34.7 %collective-permute-start.15 = (bf16[512,256]{1,0:T(8,128)(2,1)}, bf16[512,256]{1,0:T(8,128)(2,1)}, u32[]{:S(2)}, u32[]{:S(2)}) collective-permute-start(bf16[512,256]{1,0:T(8,128)(2,1)} %param.9), channel_id=1, source_target_pairs={{0,8},{4,12},{8,16},{12,20},{16,24},{20,28},{24,0},{28,4},{1,9},{5... | collective-permute-start | bytes 786440 | tf_op jit(solution)/shard_map/ppermute | solution.py:65
  62.1 74.1 %collective-permute-start.36 = (bf16[256,2048]{1,0:T(8,128)(2,1)S(1)}, bf16[256,2048]{1,0:T(8,128)(2,1)S(1)}, u32[]{:S(2)}, u32[]{:S(2)}) collective-permute-start(bf16[256,2048]{1,0:T(8,128)(2,1)S(1)} %bitcast.91), channel_id=1, source_target_pairs={{0,4},{4,0},{8,12},{12,8},{16,20},{20,16},{24,28},{28,24},{1,5},{5... | collective-permute-start | bytes 3145736 | tf_op jit(solution)/shard_map/ppermute | solution.py:72
  80.8 53.6 %collective-permute-start.37 = (bf16[256,2048]{1,0:T(8,128)(2,1)S(1)}, bf16[256,2048]{1,0:T(8,128)(2,1)}, u32[]{:S(2)}, u32[]{:S(2)}) collective-permute-start(bf16[256,2048]{1,0:T(8,128)(2,1)S(1)} %bitcast.92), channel_id=1, source_target_pairs={{0,8},{4,12},{8,16},{12,20},{16,24},{20,28},{24,0},{28,4},{1,9},{5... | collective-permute-start | bytes 3145736 | tf_op jit(solution)/shard_map/ppermute | solution.py:65
  86.2 55.0 %collective-permute-start.29 = (bf16[256,2048]{1,0:T(8,128)(2,1)S(1)}, bf16[256,2048]{1,0:T(8,128)(2,1)}, u32[]{:S(2)}, u32[]{:S(2)}) collective-permute-start(bf16[256,2048]{1,0:T(8,128)(2,1)S(1)} %bitcast.87), channel_id=1, source_target_pairs={{0,4},{4,0},{8,12},{12,8},{16,20},{20,16},{24,28},{28,24},{1,5},{5... | collective-permute-start | bytes 3145736 | tf_op jit(solution)/shard_map/ppermute | solution.py:72
  86.7 35.2 %collective-permute-start.18 = (bf16[512,256]{1,0:T(8,128)(2,1)}, bf16[512,256]{1,0:T(8,128)(2,1)}, u32[]{:S(2)}, u32[]{:S(2)}) collective-permute-start(bf16[512,256]{1,0:T(8,128)(2,1)} %collective-permute-done.17), channel_id=1, source_target_pairs={{0,4},{4,0},{8,12},{12,8},{16,20},{20,16},{24,28},{28,24},{1,5},{5... | collective-permute-start | bytes 786440 | tf_op jit(solution)/shard_map/ppermute | solution.py:72
  131.7 40.6 %collective-permute-start.21 = (bf16[576,1024]{1,0:T(8,128)(2,1)S(1)}, bf16[576,1024]{1,0:T(8,128)(2,1)S(1)}, u32[]{:S(2)}, u32[]{:S(2)}) collective-permute-start(bf16[576,1024]{1,0:T(8,128)(2,1)S(1)} %constant_dynamic-slice_fusion.18), channel_id=1, source_target_pairs={{0,1},{1,0},{2,3},{3,2},{4,5},{5,4},{6,7},{7,6},{8,9},{9,8},{10,11... | collective-permute-start | bytes 3538952 | tf_op jit(solution)/shard_map/ppermute | solution.py:87
  134.4 37.9 %collective-permute-start.39 = (bf16[256,2048]{1,0:T(8,128)(2,1)}, bf16[256,2048]{1,0:T(8,128)(2,1)S(1)}, u32[]{:S(2)}, u32[]{:S(2)}) collective-permute-start(bf16[256,2048]{1,0:T(8,128)(2,1)} %collective-permute-done.37), channel_id=1, source_target_pairs={{0,8},{4,12},{8,16},{12,20},{16,24},{20,28},{24,0},{28,4},{1,9},{5... | collective-permute-start | bytes 3145736 | tf_op jit(solution)/shard_map/ppermute | solution.py:65
  136.2 36.7 %collective-permute-start.25 = (bf16[576,1024]{1,0:T(8,128)(2,1)S(1)}, bf16[576,1024]{1,0:T(8,128)(2,1)S(1)}, u32[]{:S(2)}, u32[]{:S(2)}) collective-permute-start(bf16[576,1024]{1,0:T(8,128)(2,1)S(1)} %constant_dynamic-slice_fusion.15), channel_id=1, source_target_pairs={{0,2},{1,3},{2,0},{3,1},{4,6},{5,7},{6,4},{7,5},{8,10},{9,11},{10,... | collective-permute-start | bytes 3538952 | tf_op jit(solution)/shard_map/ppermute | solution.py:87
  141.2 32.4 %collective-permute-start.38 = (bf16[256,2048]{1,0:T(8,128)(2,1)}, bf16[256,2048]{1,0:T(8,128)(2,1)S(1)}, u32[]{:S(2)}, u32[]{:S(2)}) collective-permute-start(bf16[256,2048]{1,0:T(8,128)(2,1)} %collective-permute-done.37), channel_id=1, source_target_pairs={{0,4},{4,0},{8,12},{12,8},{16,20},{20,16},{24,28},{28,24},{1,5},{5... | collective-permute-start | bytes 3145736 | tf_op jit(solution)/shard_map/ppermute | solution.py:72
  150.3 51.6 %collective-permute-start.31 = (bf16[256,2048]{1,0:T(8,128)(2,1)}, bf16[256,2048]{1,0:T(8,128)(2,1)S(1)}, u32[]{:S(2)}, u32[]{:S(2)}) collective-permute-start(bf16[256,2048]{1,0:T(8,128)(2,1)} %collective-permute-done.30), channel_id=1, source_target_pairs={{0,4},{4,0},{8,12},{12,8},{16,20},{20,16},{24,28},{28,24},{1,5},{5... | collective-permute-start | bytes 3145736 | tf_op jit(solution)/shard_map/ppermute | solution.py:72
  172.3 49.7 %collective-permute-start.46 = (bf16[1024,256]{1,0:T(8,128)(2,1)S(1)}, bf16[1024,256]{1,0:T(8,128)(2,1)S(1)}, u32[]{:S(2)}, u32[]{:S(2)}) collective-permute-start(bf16[1024,256]{1,0:T(8,128)(2,1)S(1)} %copy-done.7), channel_id=1, source_target_pairs={{0,8},{4,12},{8,16},{12,20},{16,24},{20,28},{24,0},{28,4},{1,9},{5... | collective-permute-start | bytes 1572872 | tf_op jit(solution)/shard_map/ppermute | solution.py:65
  172.9 48.8 %collective-permute-start.44 = (bf16[1024,256]{1,0:T(8,128)(2,1)S(1)}, bf16[1024,256]{1,0:T(8,128)(2,1)S(1)}, u32[]{:S(2)}, u32[]{:S(2)}) collective-permute-start(bf16[1024,256]{1,0:T(8,128)(2,1)S(1)} %copy-done.7), channel_id=1, source_target_pairs={{0,4},{4,0},{8,12},{12,8},{16,20},{20,16},{24,28},{28,24},{1,5},{5... | collective-permute-start | bytes 1572872 | tf_op jit(solution)/shard_map/ppermute | solution.py:72
  173.6 28.7 %collective-permute-start.22 = (bf16[288,1024]{1,0:T(8,128)(2,1)S(1)}, bf16[288,1024]{1,0:T(8,128)(2,1)S(1)}, u32[]{:S(2)}, u32[]{:S(2)}) collective-permute-start(bf16[288,1024]{1,0:T(8,128)(2,1)S(1)} %constant_dynamic-slice_fusion.17), channel_id=1, source_target_pairs={{0,2},{1,3},{2,0},{3,1},{4,6},{5,7},{6,4},{7,5},{8,10},{9,11},{10,... | collective-permute-start | bytes 1769480 | tf_op jit(solution)/shard_map/ppermute | solution.py:87
  221.6 48.3 %collective-permute-start.33 = (bf16[256,2048]{1,0:T(8,128)(2,1)S(1)}, bf16[256,2048]{1,0:T(8,128)(2,1)S(1)}, u32[]{:S(2)}, u32[]{:S(2)}) collective-permute-start(bf16[256,2048]{1,0:T(8,128)(2,1)S(1)} %collective-permute-done.32), channel_id=1, source_target_pairs={{0,4},{4,0},{8,12},{12,8},{16,20},{20,16},{24,28},{28,24},{1,5},{5... | collective-permute-start | bytes 3145736 | tf_op jit(solution)/shard_map/ppermute | solution.py:72
  221.8 48.0 %collective-permute-start.34 = (bf16[256,2048]{1,0:T(8,128)(2,1)S(1)}, bf16[256,2048]{1,0:T(8,128)(2,1)S(1)}, u32[]{:S(2)}, u32[]{:S(2)}) collective-permute-start(bf16[256,2048]{1,0:T(8,128)(2,1)S(1)} %collective-permute-done.32), channel_id=1, source_target_pairs={{0,8},{4,12},{8,16},{12,20},{16,24},{20,28},{24,0},{28,4},{1,9},{5... | collective-permute-start | bytes 3145736 | tf_op jit(solution)/shard_map/ppermute | solution.py:65
  222.0 28.5 %collective-permute-start.23 = (bf16[288,1024]{1,0:T(8,128)(2,1)S(1)}, bf16[288,1024]{1,0:T(8,128)(2,1)S(1)}, u32[]{:S(2)}, u32[]{:S(2)}) collective-permute-start(bf16[288,1024]{1,0:T(8,128)(2,1)S(1)} %add_convert_fusion.7), channel_id=1, source_target_pairs={{0,2},{1,3},{2,0},{3,1},{4,6},{5,7},{6,4},{7,5},{8,10},{9,11},{10,... | collective-permute-start | bytes 1769480 | tf_op jit(solution)/shard_map/ppermute | solution.py:87
  332.7 28.9 %collective-permute-start.49 = (bf16[288,1024]{1,0:T(8,128)(2,1)S(1)}, bf16[288,1024]{1,0:T(8,128)(2,1)S(1)}, u32[]{:S(2)}, u32[]{:S(2)}) collective-permute-start(bf16[288,1024]{1,0:T(8,128)(2,1)S(1)} %constant_dynamic-slice_fusion.10), channel_id=1, source_target_pairs={{0,1},{1,0},{2,3},{3,2},{4,5},{5,4},{6,7},{7,6},{8,9},{9,8},{10,11... | collective-permute-start | bytes 1769480 | tf_op jit(solution)/shard_map/ppermute | solution.py:87
  359.9 36.4 %collective-permute-start.53 = (bf16[288,1024]{1,0:T(8,128)(2,1)S(1)}, bf16[288,1024]{1,0:T(8,128)(2,1)S(1)}, u32[]{:S(2)}, u32[]{:S(2)}) collective-permute-start(bf16[288,1024]{1,0:T(8,128)(2,1)S(1)} %constant_dynamic-slice_fusion.7), channel_id=1, source_target_pairs={{0,2},{1,3},{2,0},{3,1},{4,6},{5,7},{6,4},{7,5},{8,10},{9,11},{10,... | collective-permute-start | bytes 1769480 | tf_op jit(solution)/shard_map/ppermute | solution.py:87
  397.4 28.5 %collective-permute-start.54 = (bf16[144,1024]{1,0:T(8,128)(2,1)}, bf16[144,1024]{1,0:T(8,128)(2,1)}, u32[]{:S(2)}, u32[]{:S(2)}) collective-permute-start(bf16[144,1024]{1,0:T(8,128)(2,1)} %constant_dynamic-slice_fusion.5), channel_id=1, source_target_pairs={{0,1},{1,0},{2,3},{3,2},{4,5},{5,4},{6,7},{7,6},{8,9},{9,8},{10,11... | collective-permute-start | bytes 884744 | tf_op jit(solution)/shard_map/ppermute | solution.py:87
  434.9 34.1 %collective-permute-start.68 = (bf16[288,1024]{1,0:T(8,128)(2,1)S(1)}, bf16[288,1024]{1,0:T(8,128)(2,1)S(1)}, u32[]{:S(2)}, u32[]{:S(2)}) collective-permute-start(bf16[288,1024]{1,0:T(8,128)(2,1)S(1)} %pad_maximum_fusion.13), channel_id=1, source_target_pairs={{0,1},{1,0},{2,3},{3,2},{4,5},{5,4},{6,7},{7,6},{8,9},{9,8},{10,11... | collective-permute-start | bytes 1769480 | tf_op jit(solution)/shard_map/ppermute | solution.py:87
  438.6 28.7 %collective-permute-start.52 = (bf16[288,1024]{1,0:T(8,128)(2,1)S(1)}, bf16[288,1024]{1,0:T(8,128)(2,1)S(1)}, u32[]{:S(2)}, u32[]{:S(2)}) collective-permute-start(bf16[288,1024]{1,0:T(8,128)(2,1)S(1)} %pad_maximum_fusion.11), channel_id=1, source_target_pairs={{0,1},{1,0},{2,3},{3,2},{4,5},{5,4},{6,7},{7,6},{8,9},{9,8},{10,11... | collective-permute-start | bytes 1769480 | tf_op jit(solution)/shard_map/ppermute | solution.py:87
  (70 other events, 971.3 us)

commit v4 on v3

v4 whole, which is shorter than its diff:
```python
import jax
import jax.numpy as jnp
from jax import lax
from jax.sharding import PartitionSpec as P

QUERY_HEADS = 32
KEY_VALUE_HEADS = 8
HEAD_SIZE = 64


def rms_norm(tensor):
    widened = tensor.astype(jnp.float32)
    scaled = widened * lax.rsqrt(jnp.mean(widened * widened, axis=-1, keepdims=True) + 1e-05)
    return scaled.astype(jnp.bfloat16)


def rotary_embedding(tensor, token_positions):
    half_width = tensor.shape[-1] // 2
    exponent = jnp.arange(half_width, dtype=jnp.float32) * (2.0 / tensor.shape[-1])
    frequency = jnp.power(jnp.float32(500000.0), -exponent)
    angles = token_positions[:, None, None] * frequency[None, None, :]
    cosine = jnp.cos(angles)
    sine_part = jnp.sin(angles)
    first_half = tensor[..., :half_width]
    second_half = tensor[..., half_width:]
    return jnp.concatenate(
        [
            first_half * cosine - second_half * sine_part,
            second_half * cosine + first_half * sine_part,
        ],
        axis=-1,
    )


def attend(query_rows, keys_bfloat, values_bfloat, score_scale):
    scores = (
        jnp.einsum("bqkgd,bpkd->bkgqp", query_rows, keys_bfloat, preferred_element_type=jnp.float32)
        * score_scale
    )
    length = scores.shape[-1]
    causal = jnp.arange(length)[:, None] >= jnp.arange(length)[None, :]
    scores = jnp.where(causal, scores, jnp.float32(-1e30))
    row_max = jnp.max(scores, axis=-1, keepdims=True)
    exped = jnp.exp(scores - row_max)
    weights_bf = (exped / jnp.sum(exped, axis=-1, keepdims=True)).astype(jnp.bfloat16)
    head_outputs = jnp.einsum(
        "bkgqp,bpkd->bqkgd", weights_bf, values_bfloat, preferred_element_type=jnp.float32
    )
    return head_outputs.astype(jnp.bfloat16)


def after(tensor, earlier):
    return lax.optimization_barrier((tensor, earlier))[0]


def gather(shard, axis, *earlier):
    shard = after(shard, earlier) if earlier else shard
    return lax.all_gather(shard, "var", axis=axis, tiled=True)


def partner(tensor, bit):
    pairs = [(i, i ^ (1 << bit)) for i in range(lax.axis_size("tp"))]
    return lax.ppermute(tensor, "tp", pairs)


def side(bit):
    return (lax.axis_index("tp") >> bit) & 1


def scatter_rows(terms, bits):
    start = 0
    for bit in bits:
        half = terms.shape[0] // 2
        mine = side(bit)
        sent = lax.dynamic_slice_in_dim(terms, (1 - mine) * half, half, axis=0)
        kept = lax.dynamic_slice_in_dim(terms, mine * half, half, axis=0)
        total = kept.astype(jnp.float32) + partner(sent, bit).astype(jnp.float32)
        terms = total.astype(jnp.bfloat16)
        start = start + mine * half
    return total, start


def gather_rows(rows, bits):
    for bit in bits[::-1]:
        other = partner(rows, bit)
        lower = side(bit) == 0
        rows = jnp.concatenate([jnp.where(lower, rows, other), jnp.where(lower, other, rows)], axis=0)
    return rows


def add_sum(terms, base, switch, bits):
    total, start = scatter_rows(terms, bits)
    count = total.shape[0]
    own = lax.dynamic_slice_in_dim(base, start, count, axis=0).astype(jnp.float32)
    own_switch = lax.dynamic_slice_in_dim(switch, start, count, axis=0)
    return gather_rows((own + own_switch * total).astype(jnp.bfloat16), bits)


def shards(hidden_in, run_table, qkv_weight, out_weight, gate_up_weight, down_weight):
    tensor_parallel_count = lax.axis_size("tp")
    var_count = lax.axis_size("var")
    seq_count, full_len, model_width = hidden_in.shape
    row_count = seq_count * full_len
    query_slice = QUERY_HEADS // tensor_parallel_count
    key_value_slice = KEY_VALUE_HEADS // tensor_parallel_count
    group_width = QUERY_HEADS // KEY_VALUE_HEADS
    switches = run_table.astype(jnp.float32)
    bf16 = jnp.bfloat16

    block = down_weight.shape[1]
    half_block = block // 2
    ff_local = gate_up_weight.shape[2]
    qkv_full = gather(qkv_weight, 0)
    out_full = gather(out_weight, 1, qkv_full)

    columns = rms_norm(hidden_in).reshape(row_count, model_width)
    projected = jnp.dot(columns, qkv_full, preferred_element_type=jnp.float32)
    projected = projected.reshape(seq_count, full_len, query_slice + 2 * key_value_slice, HEAD_SIZE)
    queries, keys_values = projected[:, :, :query_slice], projected[:, :, query_slice:]
    token_positions = jnp.arange(full_len, dtype=jnp.float32)
    query_rows = rotary_embedding(queries, token_positions).astype(bf16)
    query_rows = query_rows.reshape(seq_count, full_len, key_value_slice, group_width, HEAD_SIZE)
    keys_bfloat = rotary_embedding(keys_values[:, :, :key_value_slice], token_positions).astype(bf16)
    values_bfloat = keys_values[:, :, key_value_slice:].astype(bf16)
    head_outputs = attend(query_rows, keys_bfloat, values_bfloat, HEAD_SIZE ** (-0.5))
    head_rows = head_outputs.reshape(row_count, query_slice * HEAD_SIZE)
    gate_up_full = gather(gate_up_weight.reshape(-1, 2 * ff_local), 0, out_full, head_rows)
    attn_terms = jnp.dot(head_rows, out_full, preferred_element_type=jnp.float32).astype(bf16)
    attn_switch = jnp.repeat(switches[:, 0], full_len)[:, None]
    flat_in = hidden_in.reshape(row_count, model_width)
    forth = list(range(tensor_parallel_count.bit_length() - 1))
    half_width = model_width // 2
    whole_after = jnp.concatenate(
        [
            add_sum(attn_terms[:, :half_width], flat_in[:, :half_width], attn_switch, forth),
            add_sum(attn_terms[:, half_width:], flat_in[:, half_width:], attn_switch, forth[::-1]),
        ],
        axis=1,
    )

    mlp_input = rms_norm(whole_after)
    down_a_full = gather(down_weight[:, :half_block], 1, gate_up_full, mlp_input)
    gate_and_up = jnp.dot(mlp_input, gate_up_full, preferred_element_type=jnp.float32)
    hidden = (jax.nn.silu(gate_and_up[:, :ff_local]) * gate_and_up[:, ff_local:]).astype(bf16)
    down_b_full = gather(down_weight[:, half_block:], 1, down_a_full, hidden)

    mlp_switch = jnp.repeat(switches[:, 1], full_len)[:, None]
    half_rows = row_count // 2
    results = []
    for number, down_full in enumerate((down_a_full, down_b_full)):
        if results:
            down_full = after(down_full, results[0])
        terms = jnp.dot(hidden, down_full, preferred_element_type=jnp.float32).astype(bf16)
        places = [var * block + number * half_block for var in range(var_count)]
        base = jnp.concatenate([whole_after[:, at : at + half_block] for at in places], axis=1)
        result = [
            add_sum(terms[:half_rows], base[:half_rows], mlp_switch[:half_rows], forth),
            add_sum(terms[half_rows:], base[half_rows:], mlp_switch[half_rows:], forth[::-1]),
        ]
        results.append(jnp.concatenate(result, axis=0))
    layer_out = jnp.concatenate(
        [
            result[:, at : at + half_block]
            for at in range(0, var_count * half_block, half_block)
            for result in results
        ],
        axis=1,
    )
    return layer_out.reshape(seq_count, full_len, model_width)


def solution(mesh):
    return jax.shard_map(
        shards,
        mesh=mesh,
        in_specs=(
            P("var", None, None),
            P("var", None),
            P("var", "tp"),
            P("tp", "var"),
            P("var", None, "tp"),
            P("tp", "var"),
        ),
        out_specs=P("var", None, None),
        check_vma=False,
    )
```

time: 482 us -> 414 us (0.86)
  local copies, waits for them, and re-layouts: 89.5 us -> 32.2 us
  other arithmetic: 37.6 us -> 69.7 us
  waiting for transfers between devices: 223 us -> 200 us
  starting transfers between devices: 49.8 us -> 27.4 us
  between operations: 1.86 us -> 14.4 us
  matrix products: 71.3 us -> 62 us
    ppermute x49 -> x0, waiting for transfers between devices: 157 us -> none  [the longest x21 154 us: ring(): held.append(lax.ppermute(sent, 'var', forward))]
    all_gather x0 -> x5, waiting for transfers between devices: none -> 67.3 us  [gather(): return lax.all_gather(shard, 'var', axis=axis, tiled=True)]
    ppermute x24, waiting for transfers between devices: 65.8 us -> 132 us  [partner(): return lax.ppermute(tensor, 'tp', pairs)]
    dynamic_update_slice x44 -> x0, local copies, waits for them, and re-layouts: 37.8 us -> none  [the longest x40 37 us: assemble(): lax.dynamic_update_slice_in_dim(whole, shard, place * block, axis=axis)]
    convert_element_type x0 -> x2, other arithmetic: none -> 25.7 us  [the longest x1 21.4 us: rms_norm(): return scaled.astype(jnp.bfloat16)]
    ppermute x49 -> x0, starting transfers between devices: 16.7 us -> none  [the longest x21 12.2 us: ring(): held.append(lax.ppermute(sent, 'var', forward))]
    ppermute x14 -> x0, local copies, waits for them, and re-layouts: 13.3 us -> none  [the longest x8 7.03 us: swap(): return [lax.ppermute(shard, 'var', pairs) for shard in held]]
    unnamed x1 -> x14, other arithmetic: 0.01 us -> 7.7 us
  transfers between devices with their start and end apart: 73 -> 29, of which waited for: 26 -> 23; matrix products, arithmetic and copies ran while one was open for 30% -> 36% of each run, Pallas kernels for 0% -> 0%
where the time goes in v4:
time: 414 us; the launch traced here: 406 us
  waiting for transfers between devices  200 us (48%)
  other arithmetic  69.7 us (17%)
  matrix products  62 us (15%)
  local copies, waits for them, and re-layouts  32.2 us (8%)
  starting transfers between devices  27.4 us (7%)
  between operations  14.4 us (3%)
    ppermute x24, waiting for transfers between devices, partner(): return lax.ppermute(tensor, 'tp', pairs)  132 us
    all_gather x5, waiting for transfers between devices, gather(): return lax.all_gather(shard, 'var', axis=axis, tiled=True)  67.3 us
    ppermute x24, starting transfers between devices, partner(): return lax.ppermute(tensor, 'tp', pairs)  27.1 us
    dot_general x1, matrix products, shards(): jnp.dot(mlp_input, gate_up_full, preferred_element_type=jnp.float32)  23.1 us
    reduce_sum x2, other arithmetic, rms_norm(): jnp.mean(widened * widened, axis=-1, keepdims=True) + 1e-05  22.8 us
    convert_element_type x1, other arithmetic, rms_norm(): return scaled.astype(jnp.bfloat16)  21.4 us
    unnamed x52, local copies, waits for them, and re-layouts  14.7 us
    dot_general x2, matrix products, shards(): jnp.dot(hidden, down_full, preferred_element_type=jnp.float32).astype(bf16)  13.7 us
  transfers between devices with their start and end apart: 29, of which 23 were waited for; matrix products, arithmetic and copies ran while one was open for 36% of the time, Pallas kernels for 0%

profile of v4, /device:TPU:0, one launch (start us, length us, event | category | flops | bytes accessed | tf_op | source)
XLA Modules:
  0.0 405.5 jit_solution(5009564643495568629)
XLA Ops:
  14.8 35.3 %all-gather.6.cloned.1.call-done = bf16[2048,768]{1,0:T(8,128)(2,1)} async-done(((bf16[256,768]{1,0:T(8,128)(2,1)}), bf16[2048,768]{1,0:T(8,128)(2,1)}) %all-gather.6.cloned.1.call-update) | async-done | bytes 3145744 | tf_op jit(solution)/shard_map/all_gather | solution.py:58
  53.3 6.7 %fusion.12 = f32[3,384,12,64]{1,3,2,0:T(8,128)S(1)} fusion(bf16[12,64,2048,1]{2,1,0,3:T(8,128)(2,1)S(1)} %bitcast.83, bf16[3,384,2048]{2,1,0:T(8,128)(2,1)} %param.6, f32[3,384]{1,0:T(4,128)S(1)} %add_rsqrt_fusion.1), kind=kOutput, calls=%fused_computation.21 | convolution fusion | flops 3630956544 | bytes 11407872 | tf_op jit(solution)/shard_map/dot_general | solution.py:117
  62.1 7.6 %fusion.70 = (f32[3,2,4,384]{3,2,1,0:T(4,128)S(1)}, f32[3,2,4,384,384]{3,4,2,1,0:T(8,128)}) fusion(pred[384,384]{0,1:T(8,128)(4,1)S(1)} %iota_compare_fusion, bf16[3,384,2,4,32]{1,4,3,2,0:T(8,128)(2,1)S(1)} %bitcast.87, bf16[3,384,2,4,32]{1,4,3,2,0:T(8,128)(2,1)S(1)} %bitcast.86, bf16[3,384,2,32]{1,3,2,0:T(8,128)(2,1)S(1)} %get-tuple-element.22, ...), kind=kOutput, calls=%fused_computation.199 | convolution fusion | flops 470090112 | bytes 15814656 | tf_op jit(solution)/shard_map/sub | solution.py:44
  69.7 6.7 %fusion.18 = bf16[3,384,2,4,64]{1,4,3,2,0:T(8,128)(2,1)S(1)} fusion(f32[3,2,4,384,384]{3,4,2,1,0:T(8,128)} %get-tuple-element.70, f32[3,2,4,384]{3,2,1,0:T(4,128)S(1)} %get-tuple-element.69, f32[3,384,12,64]{1,3,2,0:T(8,128)} %copy-done.7), kind=kOutput, calls=%fused_computation.60 | convolution fusion | flops 460652544 | bytes 15667200 | tf_op jit(solution)/shard_map/bkgqp,bpkd->bqkgd/dot_general | solution.py:46
  91.8 6.2 %fusion.62 = (bf16[1152,1024]{1,0:T(8,128)(2,1)}, bf16[1152,1024]{1,0:T(8,128)(2,1)}) fusion(bf16[1152,2048]{1,0:T(8,128)(2,1)} %bitcast.75), kind=kLoop, calls=%fused_computation.191 | loop fusion | bytes 9437184 | tf_op jit(solution)/shard_map/slice | solution.py:135
  98.1 18.1 %collective-permute-done.4 = bf16[576,1024]{1,0:T(8,128)(2,1)} collective-permute-done((bf16[576,1024]{1,0:T(8,128)(2,1)S(1)}, bf16[576,1024]{1,0:T(8,128)(2,1)}, u32[]{:S(2)}, u32[]{:S(2)}) %collective-permute-start.4) | collective-permute-done | bytes 1179680 | tf_op jit(solution)/shard_map/ppermute | solution.py:63
  123.6 10.3 %collective-permute-done.5 = bf16[288,1024]{1,0:T(8,128)(2,1)} collective-permute-done((bf16[288,1024]{1,0:T(8,128)(2,1)}, bf16[288,1024]{1,0:T(8,128)(2,1)}, u32[]{:S(2)}, u32[]{:S(2)}) %collective-permute-start.5) | collective-permute-done | bytes 589856 | tf_op jit(solution)/shard_map/ppermute | solution.py:63
  139.7 9.7 %collective-permute-done.6 = bf16[288,1024]{1,0:T(8,128)(2,1)S(1)} collective-permute-done((bf16[288,1024]{1,0:T(8,128)(2,1)S(1)}, bf16[288,1024]{1,0:T(8,128)(2,1)S(1)}, u32[]{:S(2)}, u32[]{:S(2)}) %collective-permute-start.6) | collective-permute-done | bytes 589856 | tf_op jit(solution)/shard_map/ppermute | solution.py:63
  155.2 21.8 %collective-permute-done.7 = bf16[576,1024]{1,0:T(8,128)(2,1)S(1)} collective-permute-done((bf16[576,1024]{1,0:T(8,128)(2,1)S(1)}, bf16[576,1024]{1,0:T(8,128)(2,1)S(1)}, u32[]{:S(2)}, u32[]{:S(2)}) %collective-permute-start.7) | collective-permute-done | bytes 1179680 | tf_op jit(solution)/shard_map/ppermute | solution.py:63
  178.3 19.5 %fusion.4 = f32[1152]{0:T(1024)S(1)} fusion(bf16[576,1024]{1,0:T(8,128)(2,1)S(1)} %get-tuple-element.40, bf16[576,1024]{1,0:T(8,128)(2,1)S(1)} %get-tuple-element.39, bf16[576,1024]{1,0:T(8,128)(2,1)S(1)} %get-tuple-element.38, bf16[576,1024]{1,0:T(8,128)(2,1)S(1)} %get-tuple-element.37), kind=kLoop, calls=%fused_computation.11 | loop fusion | flops 23591808 | bytes 4723200 | tf_op jit(solution)/shard_map/reduce_sum | solution.py:13
  197.9 21.4 %fusion.5 = bf16[1152,2048]{1,0:T(8,128)(2,1)} fusion(f32[1152]{0:T(1024)S(1)} %add_rsqrt_fusion, bf16[576,1024]{1,0:T(8,128)(2,1)S(1)} %get-tuple-element.40, bf16[576,1024]{1,0:T(8,128)(2,1)S(1)} %get-tuple-element.39, bf16[576,1024]{1,0:T(8,128)(2,1)S(1)} %get-tuple-element.38, bf16[576,1024]{1,0:T(8,128)(2,1)S(1)} %get-tuple-element.37), kind=kLoop, calls=%fused_computation.12 | loop fusion | flops 23592960 | bytes 9441792 | tf_op jit(solution)/shard_map/convert_element_type | solution.py:14
  219.3 13.8 %all-gather.10.cloned.1.call-done = bf16[2048,4096]{1,0:T(8,128)(2,1)} async-done(((bf16[256,4096]{1,0:T(8,128)(2,1)}), bf16[2048,4096]{1,0:T(8,128)(2,1)}) %all-gather.10.cloned.1.call-update) | async-done | bytes 16777232 | tf_op jit(solution)/shard_map/all_gather | solution.py:58
  238.8 23.1 %fusion.71 = f32[1152,4096]{1,0:T(8,128)S(1)} fusion(bf16[1152,2048]{1,0:T(8,128)(2,1)S(1)} %bitcast.79, bf16[2048,4096]{1,0:T(8,128)(2,1)} %all-gather.10.cloned.1.call-done), kind=kOutput, calls=%fused_computation.200 | convolution fusion | flops 19327352832 | bytes 40370176 | tf_op jit(solution)/shard_map/dot_general | solution.py:143
  266.1 14.5 %all-gather.12.cloned.1.call-done = bf16[2048,1024]{1,0:T(8,128)(2,1)} async-done(((bf16[2048,128]{1,0:T(8,128)(2,1)}), bf16[2048,1024]{1,0:T(8,128)(2,1)}) %all-gather.12.cloned.1.call-update) | async-done | bytes 4194320 | tf_op jit(solution)/shard_map/all_gather | solution.py:58
  287.2 5.3 %convolution_convert_fusion.2 = bf16[1152,1024]{1,0:T(8,128)(2,1)S(1)} fusion(bf16[1152,2048]{1,0:T(8,128)(2,1)S(1)} %bitcast.81, bf16[2048,1024]{1,0:T(8,128)(2,1)S(1)} %copy-done.11), kind=kOutput, calls=%fused_computation.53 | convolution fusion | flops 4833017856 | bytes 11272192 | tf_op jit(solution)/shard_map/dot_general | solution.py:153
  296.3 12.1 %collective-permute-done.12 = bf16[288,1024]{1,0:T(8,128)(2,1)S(1)} collective-permute-done((bf16[288,1024]{1,0:T(8,128)(2,1)S(1)}, bf16[288,1024]{1,0:T(8,128)(2,1)S(1)}, u32[]{:S(2)}, u32[]{:S(2)}) %collective-permute-start.12) | collective-permute-done | bytes 589856 | tf_op jit(solution)/shard_map/ppermute | solution.py:63
  312.0 5.2 %collective-permute-done.13 = bf16[144,1024]{1,0:T(8,128)(2,1)S(1)} collective-permute-done((bf16[144,1024]{1,0:T(8,128)(2,1)S(1)}, bf16[144,1024]{1,0:T(8,128)(2,1)S(1)}, u32[]{:S(2)}, u32[]{:S(2)}) %collective-permute-start.13) | collective-permute-done | bytes 294944 | tf_op jit(solution)/shard_map/ppermute | solution.py:63
  320.6 4.4 %collective-permute-done.14 = bf16[144,1024]{1,0:T(8,128)(2,1)S(1)} collective-permute-done((bf16[144,1024]{1,0:T(8,128)(2,1)S(1)}, bf16[144,1024]{1,0:T(8,128)(2,1)S(1)}, u32[]{:S(2)}, u32[]{:S(2)}) %collective-permute-start.14) | collective-permute-done | bytes 294944 | tf_op jit(solution)/shard_map/ppermute | solution.py:63
  328.3 10.9 %collective-permute-done.15 = bf16[288,1024]{1,0:T(8,128)(2,1)S(1)} collective-permute-done((bf16[288,1024]{1,0:T(8,128)(2,1)S(1)}, bf16[288,1024]{1,0:T(8,128)(2,1)S(1)}, u32[]{:S(2)}, u32[]{:S(2)}) %collective-permute-start.15) | collective-permute-done | bytes 589856 | tf_op jit(solution)/shard_map/ppermute | solution.py:63
  340.2 8.4 %convolution_convert_fusion.1 = bf16[1152,1024]{1,0:T(8,128)(2,1)S(1)} fusion(bf16[1152,2048]{1,0:T(8,128)(2,1)} %fusion.6, bf16[2048,1024]{1,0:T(8,128)(2,1)} %all-gather.14.cloned.1.call-done), kind=kOutput, calls=%fused_computation.52 | convolution fusion | flops 4833017856 | bytes 11272192 | tf_op jit(solution)/shard_map/dot_general | solution.py:153
  353.0 8.9 %collective-permute-done.20 = bf16[288,1024]{1,0:T(8,128)(2,1)S(1)} collective-permute-done((bf16[288,1024]{1,0:T(8,128)(2,1)S(1)}, bf16[288,1024]{1,0:T(8,128)(2,1)S(1)}, u32[]{:S(2)}, u32[]{:S(2)}) %collective-permute-start.20) | collective-permute-done | bytes 589856 | tf_op jit(solution)/shard_map/ppermute | solution.py:63
  365.0 4.4 %collective-permute-done.21 = bf16[144,1024]{1,0:T(8,128)(2,1)S(1)} collective-permute-done((bf16[144,1024]{1,0:T(8,128)(2,1)S(1)}, bf16[144,1024]{1,0:T(8,128)(2,1)S(1)}, u32[]{:S(2)}, u32[]{:S(2)}) %collective-permute-start.21) | collective-permute-done | bytes 294944 | tf_op jit(solution)/shard_map/ppermute | solution.py:63
  378.6 5.0 %collective-permute-done.18 = bf16[144,1024]{1,0:T(8,128)(2,1)S(1)} collective-permute-done((bf16[144,1024]{1,0:T(8,128)(2,1)S(1)}, bf16[144,1024]{1,0:T(8,128)(2,1)S(1)}, u32[]{:S(2)}, u32[]{:S(2)}) %collective-permute-start.18) | collective-permute-done | bytes 294944 | tf_op jit(solution)/shard_map/ppermute | solution.py:63
  383.8 7.6 %collective-permute-done.23 = bf16[288,1024]{1,0:T(8,128)(2,1)S(1)} collective-permute-done((bf16[288,1024]{1,0:T(8,128)(2,1)S(1)}, bf16[288,1024]{1,0:T(8,128)(2,1)S(1)}, u32[]{:S(2)}, u32[]{:S(2)}) %collective-permute-start.23) | collective-permute-done | bytes 589856 | tf_op jit(solution)/shard_map/ppermute | solution.py:63
  (185 shorter events, 104.2 us)
Async XLA Ops:
  6.5 43.5 %all-gather.6.cloned.1.call-start = ((), (), s32[]{:S(2)}) async-start(), calls=%async_computation | async-start | bytes 3538944 | tf_op jit(solution)/shard_map/all_gather | solution.py:58
  7.3 74.1 %all-gather.8.cloned.1.call-start = ((), (), s32[]{:S(2)}) async-start(), calls=%async_computation.1 | async-start | bytes 2359296 | tf_op jit(solution)/shard_map/all_gather | solution.py:58
  50.0 183.1 %all-gather.10.cloned.1.call-start = ((), (), s32[]{:S(2)}) async-start(), calls=%async_computation.2 | async-start | bytes 18874368 | tf_op jit(solution)/shard_map/all_gather | solution.py:58
  81.4 199.3 %all-gather.12.cloned.1.call-start = ((), (), s32[]{:S(2)}) async-start(), calls=%async_computation.3 | async-start | bytes 4718592 | tf_op jit(solution)/shard_map/all_gather | solution.py:58
  87.9 28.3 %collective-permute-start.4 = (bf16[576,1024]{1,0:T(8,128)(2,1)S(1)}, bf16[576,1024]{1,0:T(8,128)(2,1)}, u32[]{:S(2)}, u32[]{:S(2)}) collective-permute-start(bf16[576,1024]{1,0:T(8,128)(2,1)S(1)} %constant_dynamic-slice_fusion.10), channel_id=1, source_target_pairs={{0,2},{1,3},{2,0},{3,1},{4,6},{5,7},{6,4},{7,5},{8,10},{9,11},{10,... | collective-permute-start | bytes 3538952 | tf_op jit(solution)/shard_map/ppermute | solution.py:63
  90.3 29.8 %collective-permute-start = (bf16[576,1024]{1,0:T(8,128)(2,1)}, bf16[576,1024]{1,0:T(8,128)(2,1)}, u32[]{:S(2)}, u32[]{:S(2)}) collective-permute-start(bf16[576,1024]{1,0:T(8,128)(2,1)} %constant_dynamic-slice_fusion.14), channel_id=1, source_target_pairs={{0,1},{1,0},{2,3},{3,2},{4,5},{5,4},{6,7},{7,6},{8,9},{9,8},{10,11... | collective-permute-start | bytes 3538952 | tf_op jit(solution)/shard_map/ppermute | solution.py:63
  118.9 15.0 %collective-permute-start.5 = (bf16[288,1024]{1,0:T(8,128)(2,1)}, bf16[288,1024]{1,0:T(8,128)(2,1)}, u32[]{:S(2)}, u32[]{:S(2)}) collective-permute-start(bf16[288,1024]{1,0:T(8,128)(2,1)} %constant_dynamic-slice_fusion.9), channel_id=1, source_target_pairs={{0,1},{1,0},{2,3},{3,2},{4,5},{5,4},{6,7},{7,6},{8,9},{9,8},{10,11... | collective-permute-start | bytes 1769480 | tf_op jit(solution)/shard_map/ppermute | solution.py:63
  121.9 14.9 %collective-permute-start.1 = (bf16[288,1024]{1,0:T(8,128)(2,1)S(1)}, bf16[288,1024]{1,0:T(8,128)(2,1)S(1)}, u32[]{:S(2)}, u32[]{:S(2)}) collective-permute-start(bf16[288,1024]{1,0:T(8,128)(2,1)S(1)} %constant_dynamic-slice_fusion.13), channel_id=1, source_target_pairs={{0,2},{1,3},{2,0},{3,1},{4,6},{5,7},{6,4},{7,5},{8,10},{9,11},{10,... | collective-permute-start | bytes 1769480 | tf_op jit(solution)/shard_map/ppermute | solution.py:63
  135.6 13.8 %collective-permute-start.6 = (bf16[288,1024]{1,0:T(8,128)(2,1)S(1)}, bf16[288,1024]{1,0:T(8,128)(2,1)S(1)}, u32[]{:S(2)}, u32[]{:S(2)}) collective-permute-start(bf16[288,1024]{1,0:T(8,128)(2,1)S(1)} %add_convert_fusion.6), channel_id=1, source_target_pairs={{0,1},{1,0},{2,3},{3,2},{4,5},{5,4},{6,7},{7,6},{8,9},{9,8},{10,11... | collective-permute-start | bytes 1769480 | tf_op jit(solution)/shard_map/ppermute | solution.py:63
  138.2 15.3 %collective-permute-start.2 = (bf16[288,1024]{1,0:T(8,128)(2,1)S(1)}, bf16[288,1024]{1,0:T(8,128)(2,1)S(1)}, u32[]{:S(2)}, u32[]{:S(2)}) collective-permute-start(bf16[288,1024]{1,0:T(8,128)(2,1)S(1)} %add_convert_fusion.7), channel_id=1, source_target_pairs={{0,2},{1,3},{2,0},{3,1},{4,6},{5,7},{6,4},{7,5},{8,10},{9,11},{10,... | collective-permute-start | bytes 1769480 | tf_op jit(solution)/shard_map/ppermute | solution.py:63
  149.6 27.4 %collective-permute-start.7 = (bf16[576,1024]{1,0:T(8,128)(2,1)S(1)}, bf16[576,1024]{1,0:T(8,128)(2,1)S(1)}, u32[]{:S(2)}, u32[]{:S(2)}) collective-permute-start(bf16[576,1024]{1,0:T(8,128)(2,1)S(1)} %pad_maximum_fusion.4), channel_id=1, source_target_pairs={{0,2},{1,3},{2,0},{3,1},{4,6},{5,7},{6,4},{7,5},{8,10},{9,11},{10,... | collective-permute-start | bytes 3538952 | tf_op jit(solution)/shard_map/ppermute | solution.py:63
  153.7 24.0 %collective-permute-start.3 = (bf16[576,1024]{1,0:T(8,128)(2,1)S(1)}, bf16[576,1024]{1,0:T(8,128)(2,1)S(1)}, u32[]{:S(2)}, u32[]{:S(2)}) collective-permute-start(bf16[576,1024]{1,0:T(8,128)(2,1)S(1)} %pad_maximum_fusion.3), channel_id=1, source_target_pairs={{0,1},{1,0},{2,3},{3,2},{4,5},{5,4},{6,7},{7,6},{8,9},{9,8},{10,11... | collective-permute-start | bytes 3538952 | tf_op jit(solution)/shard_map/ppermute | solution.py:63
  233.2 107.1 %all-gather.14.cloned.1.call-start = ((), (), s32[]{:S(2)}) async-start(), calls=%async_computation.4 | async-start | bytes 4718592 | tf_op jit(solution)/shard_map/all_gather | solution.py:58
  292.8 15.5 %collective-permute-start.12 = (bf16[288,1024]{1,0:T(8,128)(2,1)S(1)}, bf16[288,1024]{1,0:T(8,128)(2,1)S(1)}, u32[]{:S(2)}, u32[]{:S(2)}) collective-permute-start(bf16[288,1024]{1,0:T(8,128)(2,1)S(1)} %constant_dynamic-slice_fusion.2), channel_id=1, source_target_pairs={{0,2},{1,3},{2,0},{3,1},{4,6},{5,7},{6,4},{7,5},{8,10},{9,11},{10,... | collective-permute-start | bytes 1769480 | tf_op jit(solution)/shard_map/ppermute | solution.py:63
  294.5 15.6 %collective-permute-start.8 = (bf16[288,1024]{1,0:T(8,128)(2,1)S(1)}, bf16[288,1024]{1,0:T(8,128)(2,1)S(1)}, u32[]{:S(2)}, u32[]{:S(2)}) collective-permute-start(bf16[288,1024]{1,0:T(8,128)(2,1)S(1)} %constant_dynamic-slice_fusion.6), channel_id=1, source_target_pairs={{0,1},{1,0},{2,3},{3,2},{4,5},{5,4},{6,7},{7,6},{8,9},{9,8},{10,11... | collective-permute-start | bytes 1769480 | tf_op jit(solution)/shard_map/ppermute | solution.py:63
  308.6 8.5 %collective-permute-start.13 = (bf16[144,1024]{1,0:T(8,128)(2,1)S(1)}, bf16[144,1024]{1,0:T(8,128)(2,1)S(1)}, u32[]{:S(2)}, u32[]{:S(2)}) collective-permute-start(bf16[144,1024]{1,0:T(8,128)(2,1)S(1)} %constant_dynamic-slice_fusion.1), channel_id=1, source_target_pairs={{0,1},{1,0},{2,3},{3,2},{4,5},{5,4},{6,7},{7,6},{8,9},{9,8},{10,11... | collective-permute-start | bytes 884744 | tf_op jit(solution)/shard_map/ppermute | solution.py:63
  310.4 8.5 %collective-permute-start.9 = (bf16[144,1024]{1,0:T(8,128)(2,1)S(1)}, bf16[144,1024]{1,0:T(8,128)(2,1)S(1)}, u32[]{:S(2)}, u32[]{:S(2)}) collective-permute-start(bf16[144,1024]{1,0:T(8,128)(2,1)S(1)} %constant_dynamic-slice_fusion.5), channel_id=1, source_target_pairs={{0,2},{1,3},{2,0},{3,1},{4,6},{5,7},{6,4},{7,5},{8,10},{9,11},{10,... | collective-permute-start | bytes 884744 | tf_op jit(solution)/shard_map/ppermute | solution.py:63
  325.1 14.1 %collective-permute-start.15 = (bf16[288,1024]{1,0:T(8,128)(2,1)S(1)}, bf16[288,1024]{1,0:T(8,128)(2,1)S(1)}, u32[]{:S(2)}, u32[]{:S(2)}) collective-permute-start(bf16[288,1024]{1,0:T(8,128)(2,1)S(1)} %pad_maximum_fusion.12), channel_id=1, source_target_pairs={{0,2},{1,3},{2,0},{3,1},{4,6},{5,7},{6,4},{7,5},{8,10},{9,11},{10,... | collective-permute-start | bytes 1769480 | tf_op jit(solution)/shard_map/ppermute | solution.py:63
  327.4 12.3 %collective-permute-start.11 = (bf16[288,1024]{1,0:T(8,128)(2,1)S(1)}, bf16[288,1024]{1,0:T(8,128)(2,1)S(1)}, u32[]{:S(2)}, u32[]{:S(2)}) collective-permute-start(bf16[288,1024]{1,0:T(8,128)(2,1)S(1)} %pad_maximum_fusion.11), channel_id=1, source_target_pairs={{0,1},{1,0},{2,3},{3,2},{4,5},{5,4},{6,7},{7,6},{8,9},{9,8},{10,11... | collective-permute-start | bytes 1769480 | tf_op jit(solution)/shard_map/ppermute | solution.py:63
  348.9 12.9 %collective-permute-start.20 = (bf16[288,1024]{1,0:T(8,128)(2,1)S(1)}, bf16[288,1024]{1,0:T(8,128)(2,1)S(1)}, u32[]{:S(2)}, u32[]{:S(2)}) collective-permute-start(bf16[288,1024]{1,0:T(8,128)(2,1)S(1)} %constant_dynamic-slice_fusion.4), channel_id=1, source_target_pairs={{0,2},{1,3},{2,0},{3,1},{4,6},{5,7},{6,4},{7,5},{8,10},{9,11},{10,... | collective-permute-start | bytes 1769480 | tf_op jit(solution)/shard_map/ppermute | solution.py:63
  350.3 14.3 %collective-permute-start.16 = (bf16[288,1024]{1,0:T(8,128)(2,1)S(1)}, bf16[288,1024]{1,0:T(8,128)(2,1)S(1)}, u32[]{:S(2)}, u32[]{:S(2)}) collective-permute-start(bf16[288,1024]{1,0:T(8,128)(2,1)S(1)} %constant_dynamic-slice_fusion), channel_id=1, source_target_pairs={{0,1},{1,0},{2,3},{3,2},{4,5},{5,4},{6,7},{7,6},{8,9},{9,8},{10,11... | collective-permute-start | bytes 1769480 | tf_op jit(solution)/shard_map/ppermute | solution.py:63
  373.6 10.0 %collective-permute-start.18 = (bf16[144,1024]{1,0:T(8,128)(2,1)S(1)}, bf16[144,1024]{1,0:T(8,128)(2,1)S(1)}, u32[]{:S(2)}, u32[]{:S(2)}) collective-permute-start(bf16[144,1024]{1,0:T(8,128)(2,1)S(1)} %add_convert_fusion.10), channel_id=1, source_target_pairs={{0,2},{1,3},{2,0},{3,1},{4,6},{5,7},{6,4},{7,5},{8,10},{9,11},{10,... | collective-permute-start | bytes 884744 | tf_op jit(solution)/shard_map/ppermute | solution.py:63
  376.5 15.0 %collective-permute-start.23 = (bf16[288,1024]{1,0:T(8,128)(2,1)S(1)}, bf16[288,1024]{1,0:T(8,128)(2,1)S(1)}, u32[]{:S(2)}, u32[]{:S(2)}) collective-permute-start(bf16[288,1024]{1,0:T(8,128)(2,1)S(1)} %pad_maximum_fusion.14), channel_id=1, source_target_pairs={{0,2},{1,3},{2,0},{3,1},{4,6},{5,7},{6,4},{7,5},{8,10},{9,11},{10,... | collective-permute-start | bytes 1769480 | tf_op jit(solution)/shard_map/ppermute | solution.py:63
  383.7 9.9 %collective-permute-start.19 = (bf16[288,1024]{1,0:T(8,128)(2,1)S(1)}, bf16[288,1024]{1,0:T(8,128)(2,1)S(1)}, u32[]{:S(2)}, u32[]{:S(2)}) collective-permute-start(bf16[288,1024]{1,0:T(8,128)(2,1)S(1)} %pad_maximum_fusion.13), channel_id=1, source_target_pairs={{0,1},{1,0},{2,3},{3,2},{4,5},{5,4},{6,7},{7,6},{8,9},{9,8},{10,11... | collective-permute-start | bytes 1769480 | tf_op jit(solution)/shard_map/ppermute | solution.py:63
  (21 other events, 120.6 us)
Sparse Core Ops, SparseCore 0:
  9.0 40.9 all-gather.5
  51.6 29.6 all-gather.7
  82.9 150.1 all-gather.9
  234.6 46.0 all-gather.11
  282.1 46.0 all-gather.13

commit v5 on v4

--- a/solution.py
+++ b/solution.py
@@ -6,6 +6,7 @@
 QUERY_HEADS = 32
 KEY_VALUE_HEADS = 8
 HEAD_SIZE = 64
+CORES = 2
 
 
 def rms_norm(tensor):
@@ -56,6 +57,34 @@
 def gather(shard, axis, *earlier):
     shard = after(shard, earlier) if earlier else shard
     return lax.all_gather(shard, "var", axis=axis, tiled=True)
+
+
+def ring(shard, gates):
+    var_count = lax.axis_size("var")
+    forward = [(i, (i + CORES) % var_count) for i in range(var_count)]
+    held = [shard]
+    for hop in range(var_count // CORES - 1):
+        sent = after(held[-1], gates[min(hop, len(gates) - 1)])
+        held.append(lax.ppermute(sent, "var", forward))
+    return held
+
+
+def assemble_columns(held):
+    var_count = lax.axis_size("var")
+    chip_count = var_count // CORES
+    pairs = [(i, i + 1 - 2 * (i % CORES)) for i in range(var_count)]
+    me = lax.axis_index("var")
+    chip, core = me // CORES, me % CORES
+    rows, block = held[0].shape
+    whole = jnp.zeros((rows, block * var_count), held[0].dtype)
+    for step, shard in enumerate(held):
+        other = lax.ppermute(shard, "var", pairs)
+        pair = jnp.concatenate(
+            [jnp.where(core == 0, shard, other), jnp.where(core == 0, other, shard)], axis=1
+        )
+        origin = (chip + chip_count - step) % chip_count
+        whole = lax.dynamic_update_slice_in_dim(whole, pair, origin * CORES * block, axis=1)
+    return whole
 
 
 def partner(tensor, bit):
@@ -139,17 +168,16 @@
     )
 
     mlp_input = rms_norm(whole_after)
-    down_a_full = gather(down_weight[:, :half_block], 1, gate_up_full, mlp_input)
+    down_a_ring = ring(down_weight[:, :half_block], (qkv_full, head_rows, whole_after))
+    down_a_full = assemble_columns(down_a_ring)
+    down_b_full = gather(down_weight[:, half_block:], 1, gate_up_full, mlp_input, down_a_ring[-1])
     gate_and_up = jnp.dot(mlp_input, gate_up_full, preferred_element_type=jnp.float32)
     hidden = (jax.nn.silu(gate_and_up[:, :ff_local]) * gate_and_up[:, ff_local:]).astype(bf16)
-    down_b_full = gather(down_weight[:, half_block:], 1, down_a_full, hidden)
 
     mlp_switch = jnp.repeat(switches[:, 1], full_len)[:, None]
     half_rows = row_count // 2
     results = []
     for number, down_full in enumerate((down_a_full, down_b_full)):
-        if results:
-            down_full = after(down_full, results[0])
         terms = jnp.dot(hidden, down_full, preferred_element_type=jnp.float32).astype(bf16)
         places = [var * block + number * half_block for var in range(var_count)]
         base = jnp.concatenate([whole_after[:, at : at + half_block] for at in places], axis=1)

time: 414 us -> 421 us (1.017)
  starting transfers between devices: 27.4 us -> 48.1 us
  other arithmetic: 69.7 us -> 49.2 us
  matrix products: 62 us -> 67 us
  waiting for transfers between devices: 200 us -> 205 us
    ppermute x0 -> x7, waiting for transfers between devices: none -> 42.4 us  [the longest x3 42.4 us: ring(): held.append(lax.ppermute(sent, 'var', forward))]
    ppermute x24, waiting for transfers between devices: 132 us -> 110 us  [partner(): return lax.ppermute(tensor, 'tp', pairs)]
    ppermute x0 -> x7, starting transfers between devices: none -> 20.8 us  [the longest x3 20.6 us: ring(): held.append(lax.ppermute(sent, 'var', forward))]
    convert_element_type x1, other arithmetic: 21.4 us -> 3.02 us  [rms_norm(): return scaled.astype(jnp.bfloat16)]
    all_gather x5 -> x4, waiting for transfers between devices: 67.3 us -> 51.7 us  [gather(): return lax.all_gather(shard, 'var', axis=axis, tiled=True)]
    unnamed x14 -> x12, other arithmetic: 7.7 us -> 1.64 us
    dynamic_update_slice x0 -> x4, other arithmetic: none -> 4.74 us  [assemble_columns(): lax.dynamic_update_slice_in_dim(whole, pair, origin * CORES * block, axis=1)]
    unnamed x52 -> x38, local copies, waits for them, and re-layouts: 14.7 us -> 10.4 us
  transfers between devices with their start and end apart: 29 -> 35, of which waited for: 23 -> 17; matrix products, arithmetic and copies ran while one was open for 36% -> 34% of each run, Pallas kernels for 0% -> 0%
where the time goes in v5:
time: 421 us; the launch traced here: 413 us
  waiting for transfers between devices  205 us (49%)
  matrix products  67 us (16%)
  other arithmetic  49.2 us (12%)
  starting transfers between devices  48.1 us (11%)
  local copies, waits for them, and re-layouts  29.4 us (7%)
  between operations  14.2 us (3%)
    ppermute x24, waiting for transfers between devices, partner(): return lax.ppermute(tensor, 'tp', pairs)  110 us
    all_gather x4, waiting for transfers between devices, gather(): return lax.all_gather(shard, 'var', axis=axis, tiled=True)  51.7 us
    ppermute x3, waiting for transfers between devices, ring(): held.append(lax.ppermute(sent, 'var', forward))  42.4 us
    ppermute x24, starting transfers between devices, partner(): return lax.ppermute(tensor, 'tp', pairs)  26.8 us
    dot_general x1, matrix products, shards(): jnp.dot(mlp_input, gate_up_full, preferred_element_type=jnp.float32)  24.3 us
    ppermute x3, starting transfers between devices, ring(): held.append(lax.ppermute(sent, 'var', forward))  20.6 us
    reduce_sum x2, other arithmetic, rms_norm(): jnp.mean(widened * widened, axis=-1, keepdims=True) + 1e-05  20.1 us
    dot_general x2, matrix products, shards(): jnp.dot(hidden, down_full, preferred_element_type=jnp.float32).astype(bf16)  17.5 us
  transfers between devices with their start and end apart: 35, of which 17 were waited for; matrix products, arithmetic and copies ran while one was open for 34% of the time, Pallas kernels for 0%

profile of v5, /device:TPU:0, one launch (start us, length us, event | category | flops | bytes accessed | tf_op | source)
XLA Modules:
  0.0 413.1 jit_solution(9741780134461377931)
XLA Ops:
  7.3 3.8 copy.19
  14.8 35.2 %all-gather.5.cloned.1.call-done = bf16[2048,768]{1,0:T(8,128)(2,1)} async-done(((bf16[256,768]{1,0:T(8,128)(2,1)}), bf16[2048,768]{1,0:T(8,128)(2,1)}) %all-gather.5.cloned.1.call-update) | async-done | bytes 3145744 | tf_op jit(solution)/shard_map/all_gather | solution.py:59
  53.3 6.7 %fusion.12 = f32[3,384,12,64]{1,3,2,0:T(8,128)S(1)} fusion(bf16[12,64,2048,1]{2,1,0,3:T(8,128)(2,1)S(1)} %bitcast.79, bf16[3,384,2048]{2,1,0:T(8,128)(2,1)} %param.6, f32[3,384]{1,0:T(4,128)S(1)} %add_rsqrt_fusion.1), kind=kOutput, calls=%fused_computation.21 | convolution fusion | flops 3630956544 | bytes 11407872 | tf_op jit(solution)/shard_map/dot_general | solution.py:146
  62.1 7.6 %fusion.69 = (f32[3,2,4,384]{3,2,1,0:T(4,128)S(1)}, f32[3,2,4,384,384]{3,4,2,1,0:T(8,128)}) fusion(pred[384,384]{0,1:T(8,128)(4,1)S(1)} %iota_compare_fusion, bf16[3,384,2,4,32]{1,4,3,2,0:T(8,128)(2,1)S(1)} %bitcast.83, bf16[3,384,2,4,32]{1,4,3,2,0:T(8,128)(2,1)S(1)} %bitcast.82, bf16[3,384,2,32]{1,3,2,0:T(8,128)(2,1)S(1)} %get-tuple-element.26, ...), kind=kOutput, calls=%fused_computation.210 | convolution fusion | flops 470090112 | bytes 15814656 | tf_op jit(solution)/shard_map/sub | solution.py:45
  69.7 6.7 %fusion.18 = bf16[3,384,2,4,64]{1,4,3,2,0:T(8,128)(2,1)S(1)} fusion(f32[3,2,4,384,384]{3,4,2,1,0:T(8,128)} %get-tuple-element.85, f32[3,2,4,384]{3,2,1,0:T(4,128)S(1)} %get-tuple-element.84, f32[3,384,12,64]{1,3,2,0:T(8,128)} %copy-done.5), kind=kOutput, calls=%fused_computation.60 | convolution fusion | flops 460652544 | bytes 15667200 | tf_op jit(solution)/shard_map/bkgqp,bpkd->bqkgd/dot_general | solution.py:47
  77.6 3.7 all-gather.7.cloned.1.call-done
  83.0 4.2 %convolution_convert_fusion = bf16[1152,2048]{1,0:T(8,128)(2,1)S(1)} fusion(bf16[1152,512]{0,1:T(8,128)(2,1)S(1)} %bitcast.81, bf16[512,2048]{1,0:T(8,128)(2,1)} %all-gather.7.cloned.1.call-done), kind=kOutput, calls=%fused_computation.15 | convolution fusion | flops 2418278400 | bytes 7995392 | tf_op jit(solution)/shard_map/dot_general | solution.py:157
  93.1 3.7 fusion.62
  97.9 19.5 %collective-permute-done.4 = bf16[576,1024]{1,0:T(8,128)(2,1)} collective-permute-done((bf16[576,1024]{1,0:T(8,128)(2,1)}, bf16[576,1024]{1,0:T(8,128)(2,1)}, u32[]{:S(2)}, u32[]{:S(2)}) %collective-permute-start.4) | collective-permute-done | bytes 1179680 | tf_op jit(solution)/shard_map/ppermute | solution.py:92
  138.7 24.2 %collective-permute-done.11 = bf16[2048,128]{1,0:T(8,128)(2,1)S(1)} collective-permute-done((bf16[2048,128]{1,0:T(8,128)(2,1)S(1)}, bf16[2048,128]{1,0:T(8,128)(2,1)S(1)}, u32[]{:S(2)}, u32[]{:S(2)}) %collective-permute-start.11) | collective-permute-done | bytes 524320 | tf_op jit(solution)/shard_map/ppermute | solution.py:68
  167.1 24.5 %collective-permute-done.7 = bf16[576,1024]{1,0:T(8,128)(2,1)S(1)} collective-permute-done((bf16[576,1024]{1,0:T(8,128)(2,1)S(1)}, bf16[576,1024]{1,0:T(8,128)(2,1)S(1)}, u32[]{:S(2)}, u32[]{:S(2)}) %collective-permute-start.7) | collective-permute-done | bytes 1179680 | tf_op jit(solution)/shard_map/ppermute | solution.py:92
  192.9 16.8 %fusion.4 = (f32[1152]{0:T(1024)S(1)}, bf16[1152,2048]{1,0:T(8,128)(2,1)S(1)}) fusion(bf16[576,1024]{1,0:T(8,128)(2,1)S(1)} %get-tuple-element.44, bf16[576,1024]{1,0:T(8,128)(2,1)S(1)} %get-tuple-element.43, bf16[576,1024]{1,0:T(8,128)(2,1)S(1)} %get-tuple-element.42, bf16[576,1024]{1,0:T(8,128)(2,1)S(1)} %get-tuple-element.41), kind=kLoop, calls=%fused_computation.11 | loop fusion | flops 25951104 | bytes 9441792 | tf_op jit(solution)/shard_map/reduce_sum | solution.py:14
  209.6 17.7 %collective-permute-start.13 = (bf16[2048,128]{1,0:T(8,128)(2,1)S(1)}, bf16[2048,128]{1,0:T(8,128)(2,1)S(1)}, u32[]{:S(2)}, u32[]{:S(2)}) collective-permute-start(bf16[2048,128]{1,0:T(8,128)(2,1)S(1)} %collective-permute-done.11), channel_id=1, source_target_pairs={{0,8},{4,12},{8,16},{12,20},{16,24},{20,28},{24,0},{28,4},{1,9},{5... | collective-permute-start | bytes 1572872 | tf_op jit(solution)/shard_map/ppermute | solution.py:68
  232.2 18.1 %collective-permute-done.13 = bf16[2048,128]{1,0:T(8,128)(2,1)S(1)} collective-permute-done((bf16[2048,128]{1,0:T(8,128)(2,1)S(1)}, bf16[2048,128]{1,0:T(8,128)(2,1)S(1)}, u32[]{:S(2)}, u32[]{:S(2)}) %collective-permute-start.13) | collective-permute-done | bytes 524320 | tf_op jit(solution)/shard_map/ppermute | solution.py:68
  253.9 12.8 %all-gather.9.cloned.1.call-done = bf16[2048,4096]{1,0:T(8,128)(2,1)} async-done(((bf16[256,4096]{1,0:T(8,128)(2,1)}), bf16[2048,4096]{1,0:T(8,128)(2,1)}) %all-gather.9.cloned.1.call-update) | async-done | bytes 16777232 | tf_op jit(solution)/shard_map/all_gather | solution.py:59
  266.7 24.3 %fusion.70 = f32[1152,4096]{1,0:T(8,128)S(1)} fusion(bf16[1152,2048]{1,0:T(8,128)(2,1)} %fusion.5, bf16[2048,4096]{1,0:T(8,128)(2,1)} %all-gather.9.cloned.1.call-done), kind=kOutput, calls=%fused_computation.211 | convolution fusion | flops 19327352832 | bytes 40370176 | tf_op jit(solution)/shard_map/dot_general | solution.py:174
  294.0 9.1 %convolution_convert_fusion.2 = bf16[1152,1024]{1,0:T(8,128)(2,1)S(1)} fusion(bf16[1152,2048]{1,0:T(8,128)(2,1)S(1)} %fusion.6, bf16[2048,1024]{1,0:T(8,128)(2,1)} %maximum_dynamic-update-slice_fusion.3), kind=kOutput, calls=%fused_computation.53 | convolution fusion | flops 4833017856 | bytes 11272192 | tf_op jit(solution)/shard_map/dot_general | solution.py:181
  308.5 10.6 %collective-permute-done.19 = bf16[288,1024]{1,0:T(8,128)(2,1)S(1)} collective-permute-done((bf16[288,1024]{1,0:T(8,128)(2,1)S(1)}, bf16[288,1024]{1,0:T(8,128)(2,1)S(1)}, u32[]{:S(2)}, u32[]{:S(2)}) %collective-permute-start.19) | collective-permute-done | bytes 589856 | tf_op jit(solution)/shard_map/ppermute | solution.py:92
  319.3 8.4 %convolution_convert_fusion.1 = bf16[1152,1024]{1,0:T(8,128)(2,1)S(1)} fusion(bf16[1152,2048]{1,0:T(8,128)(2,1)} %copy-done.2, bf16[2048,1024]{1,0:T(8,128)(2,1)} %all-gather.11.cloned.1.call-done), kind=kOutput, calls=%fused_computation.52 | convolution fusion | flops 4833017856 | bytes 11272192 | tf_op jit(solution)/shard_map/dot_general | solution.py:181
  333.6 10.6 %collective-permute-done.27 = bf16[288,1024]{1,0:T(8,128)(2,1)S(1)} collective-permute-done((bf16[288,1024]{1,0:T(8,128)(2,1)S(1)}, bf16[288,1024]{1,0:T(8,128)(2,1)S(1)}, u32[]{:S(2)}, u32[]{:S(2)}) %collective-permute-start.27) | collective-permute-done | bytes 589856 | tf_op jit(solution)/shard_map/ppermute | solution.py:92
  346.1 6.1 %collective-permute-done.23 = bf16[288,1024]{1,0:T(8,128)(2,1)S(1)} collective-permute-done((bf16[288,1024]{1,0:T(8,128)(2,1)S(1)}, bf16[288,1024]{1,0:T(8,128)(2,1)S(1)}, u32[]{:S(2)}, u32[]{:S(2)}) %collective-permute-start.23) | collective-permute-done | bytes 589856 | tf_op jit(solution)/shard_map/ppermute | solution.py:92
  363.9 4.4 %collective-permute-done.29 = bf16[144,1024]{1,0:T(8,128)(2,1)} collective-permute-done((bf16[144,1024]{1,0:T(8,128)(2,1)S(1)}, bf16[144,1024]{1,0:T(8,128)(2,1)}, u32[]{:S(2)}, u32[]{:S(2)}) %collective-permute-start.29) | collective-permute-done | bytes 294944 | tf_op jit(solution)/shard_map/ppermute | solution.py:92
  372.5 5.6 %collective-permute-done.17 = bf16[144,1024]{1,0:T(8,128)(2,1)S(1)} collective-permute-done((bf16[144,1024]{1,0:T(8,128)(2,1)S(1)}, bf16[144,1024]{1,0:T(8,128)(2,1)S(1)}, u32[]{:S(2)}, u32[]{:S(2)}) %collective-permute-start.17) | collective-permute-done | bytes 294944 | tf_op jit(solution)/shard_map/ppermute | solution.py:92
  380.5 19.7 %collective-permute-done.22 = bf16[288,1024]{1,0:T(8,128)(2,1)S(1)} collective-permute-done((bf16[288,1024]{1,0:T(8,128)(2,1)S(1)}, bf16[288,1024]{1,0:T(8,128)(2,1)S(1)}, u32[]{:S(2)}, u32[]{:S(2)}) %collective-permute-start.22) | collective-permute-done | bytes 589856 | tf_op jit(solution)/shard_map/ppermute | solution.py:92
  (187 shorter events, 95.0 us)
Async XLA Ops:
  6.5 43.5 %all-gather.5.cloned.1.call-start = ((), (), s32[]{:S(2)}) async-start(), calls=%async_computation | async-start | bytes 3538944 | tf_op jit(solution)/shard_map/all_gather | solution.py:59
  7.3 74.1 %all-gather.7.cloned.1.call-start = ((), (), s32[]{:S(2)}) async-start(), calls=%async_computation.1 | async-start | bytes 2359296 | tf_op jit(solution)/shard_map/all_gather | solution.py:59
  50.0 216.6 %all-gather.9.cloned.1.call-start = ((), (), s32[]{:S(2)}) async-start(), calls=%async_computation.2 | async-start | bytes 18874368 | tf_op jit(solution)/shard_map/all_gather | solution.py:59
  81.4 237.9 %all-gather.11.cloned.1.call-start = ((), (), s32[]{:S(2)}) async-start(), calls=%async_computation.3 | async-start | bytes 4718592 | tf_op jit(solution)/shard_map/all_gather | solution.py:59
  82.6 41.2 %collective-permute-start.8 = (bf16[2048,128]{1,0:T(8,128)(2,1)}, bf16[2048,128]{1,0:T(8,128)(2,1)}, u32[]{:S(2)}, u32[]{:S(2)}) collective-permute-start(bf16[2048,128]{1,0:T(8,128)(2,1)} %slice.206), channel_id=1, source_target_pairs={{0,4},{4,0},{8,12},{12,8},{16,20},{20,16},{24,28},{28,24},{1,5},{5... | collective-permute-start | bytes 1572872 | tf_op jit(solution)/shard_map/ppermute | solution.py:81
  89.0 28.5 %collective-permute-start.4 = (bf16[576,1024]{1,0:T(8,128)(2,1)}, bf16[576,1024]{1,0:T(8,128)(2,1)}, u32[]{:S(2)}, u32[]{:S(2)}) collective-permute-start(bf16[576,1024]{1,0:T(8,128)(2,1)} %constant_dynamic-slice_fusion.10), channel_id=1, source_target_pairs={{0,2},{1,3},{2,0},{3,1},{4,6},{5,7},{6,4},{7,5},{8,10},{9,11},{10,... | collective-permute-start | bytes 3538952 | tf_op jit(solution)/shard_map/ppermute | solution.py:92
  91.5 29.0 %collective-permute-start = (bf16[576,1024]{1,0:T(8,128)(2,1)}, bf16[576,1024]{1,0:T(8,128)(2,1)}, u32[]{:S(2)}, u32[]{:S(2)}) collective-permute-start(bf16[576,1024]{1,0:T(8,128)(2,1)} %constant_dynamic-slice_fusion.14), channel_id=1, source_target_pairs={{0,1},{1,0},{2,3},{3,2},{4,5},{5,4},{6,7},{7,6},{8,9},{9,8},{10,11... | collective-permute-start | bytes 3538952 | tf_op jit(solution)/shard_map/ppermute | solution.py:92
  96.8 29.0 %collective-permute-start.9 = (bf16[2048,128]{1,0:T(8,128)(2,1)}, bf16[2048,128]{1,0:T(8,128)(2,1)S(1)}, u32[]{:S(2)}, u32[]{:S(2)}) collective-permute-start(bf16[2048,128]{1,0:T(8,128)(2,1)} %slice.206), channel_id=1, source_target_pairs={{0,8},{4,12},{8,16},{12,20},{16,24},{20,28},{24,0},{28,4},{1,9},{5... | collective-permute-start | bytes 1572872 | tf_op jit(solution)/shard_map/ppermute | solution.py:68
  129.5 33.4 %collective-permute-start.11 = (bf16[2048,128]{1,0:T(8,128)(2,1)S(1)}, bf16[2048,128]{1,0:T(8,128)(2,1)S(1)}, u32[]{:S(2)}, u32[]{:S(2)}) collective-permute-start(bf16[2048,128]{1,0:T(8,128)(2,1)S(1)} %collective-permute-done.9), channel_id=1, source_target_pairs={{0,8},{4,12},{8,16},{12,20},{16,24},{20,28},{24,0},{28,4},{1,9},{5... | collective-permute-start | bytes 1572872 | tf_op jit(solution)/shard_map/ppermute | solution.py:68
  134.3 28.6 %collective-permute-start.6 = (bf16[288,1024]{1,0:T(8,128)(2,1)S(1)}, bf16[288,1024]{1,0:T(8,128)(2,1)S(1)}, u32[]{:S(2)}, u32[]{:S(2)}) collective-permute-start(bf16[288,1024]{1,0:T(8,128)(2,1)S(1)} %add_convert_fusion.6), channel_id=1, source_target_pairs={{0,1},{1,0},{2,3},{3,2},{4,5},{5,4},{6,7},{7,6},{8,9},{9,8},{10,11... | collective-permute-start | bytes 1769480 | tf_op jit(solution)/shard_map/ppermute | solution.py:92
  137.1 26.8 %collective-permute-start.2 = (bf16[288,1024]{1,0:T(8,128)(2,1)S(1)}, bf16[288,1024]{1,0:T(8,128)(2,1)S(1)}, u32[]{:S(2)}, u32[]{:S(2)}) collective-permute-start(bf16[288,1024]{1,0:T(8,128)(2,1)S(1)} %add_convert_fusion.7), channel_id=1, source_target_pairs={{0,2},{1,3},{2,0},{3,1},{4,6},{5,7},{6,4},{7,5},{8,10},{9,11},{10,... | collective-permute-start | bytes 1769480 | tf_op jit(solution)/shard_map/ppermute | solution.py:92
  163.1 28.4 %collective-permute-start.7 = (bf16[576,1024]{1,0:T(8,128)(2,1)S(1)}, bf16[576,1024]{1,0:T(8,128)(2,1)S(1)}, u32[]{:S(2)}, u32[]{:S(2)}) collective-permute-start(bf16[576,1024]{1,0:T(8,128)(2,1)S(1)} %pad_maximum_fusion.4), channel_id=1, source_target_pairs={{0,2},{1,3},{2,0},{3,1},{4,6},{5,7},{6,4},{7,5},{8,10},{9,11},{10,... | collective-permute-start | bytes 3538952 | tf_op jit(solution)/shard_map/ppermute | solution.py:92
  164.0 28.2 %collective-permute-start.3 = (bf16[576,1024]{1,0:T(8,128)(2,1)S(1)}, bf16[576,1024]{1,0:T(8,128)(2,1)S(1)}, u32[]{:S(2)}, u32[]{:S(2)}) collective-permute-start(bf16[576,1024]{1,0:T(8,128)(2,1)S(1)} %pad_maximum_fusion.3), channel_id=1, source_target_pairs={{0,1},{1,0},{2,3},{3,2},{4,5},{5,4},{6,7},{7,6},{8,9},{9,8},{10,11... | collective-permute-start | bytes 3538952 | tf_op jit(solution)/shard_map/ppermute | solution.py:92
  209.6 40.7 %collective-permute-start.13 = (bf16[2048,128]{1,0:T(8,128)(2,1)S(1)}, bf16[2048,128]{1,0:T(8,128)(2,1)S(1)}, u32[]{:S(2)}, u32[]{:S(2)}) collective-permute-start(bf16[2048,128]{1,0:T(8,128)(2,1)S(1)} %collective-permute-done.11), channel_id=1, source_target_pairs={{0,8},{4,12},{8,16},{12,20},{16,24},{20,28},{24,0},{28,4},{1,9},{5... | collective-permute-start | bytes 1572872 | tf_op jit(solution)/shard_map/ppermute | solution.py:68
  306.9 24.8 %collective-permute-start.15 = (bf16[288,1024]{1,0:T(8,128)(2,1)S(1)}, bf16[288,1024]{1,0:T(8,128)(2,1)}, u32[]{:S(2)}, u32[]{:S(2)}) collective-permute-start(bf16[288,1024]{1,0:T(8,128)(2,1)S(1)} %constant_dynamic-slice_fusion.6), channel_id=1, source_target_pairs={{0,1},{1,0},{2,3},{3,2},{4,5},{5,4},{6,7},{7,6},{8,9},{9,8},{10,11... | collective-permute-start | bytes 1769480 | tf_op jit(solution)/shard_map/ppermute | solution.py:92
  327.9 16.3 %collective-permute-start.27 = (bf16[288,1024]{1,0:T(8,128)(2,1)S(1)}, bf16[288,1024]{1,0:T(8,128)(2,1)S(1)}, u32[]{:S(2)}, u32[]{:S(2)}) collective-permute-start(bf16[288,1024]{1,0:T(8,128)(2,1)S(1)} %constant_dynamic-slice_fusion.4), channel_id=1, source_target_pairs={{0,2},{1,3},{2,0},{3,1},{4,6},{5,7},{6,4},{7,5},{8,10},{9,11},{10,... | collective-permute-start | bytes 1769480 | tf_op jit(solution)/shard_map/ppermute | solution.py:92
  329.5 23.5 %collective-permute-start.20 = (bf16[144,1024]{1,0:T(8,128)(2,1)S(1)}, bf16[144,1024]{1,0:T(8,128)(2,1)S(1)}, u32[]{:S(2)}, u32[]{:S(2)}) collective-permute-start(bf16[144,1024]{1,0:T(8,128)(2,1)S(1)} %constant_dynamic-slice_fusion.1), channel_id=1, source_target_pairs={{0,1},{1,0},{2,3},{3,2},{4,5},{5,4},{6,7},{7,6},{8,9},{9,8},{10,11... | collective-permute-start | bytes 884744 | tf_op jit(solution)/shard_map/ppermute | solution.py:92
  331.1 21.0 %collective-permute-start.23 = (bf16[288,1024]{1,0:T(8,128)(2,1)S(1)}, bf16[288,1024]{1,0:T(8,128)(2,1)S(1)}, u32[]{:S(2)}, u32[]{:S(2)}) collective-permute-start(bf16[288,1024]{1,0:T(8,128)(2,1)S(1)} %constant_dynamic-slice_fusion), channel_id=1, source_target_pairs={{0,1},{1,0},{2,3},{3,2},{4,5},{5,4},{6,7},{7,6},{8,9},{9,8},{10,11... | collective-permute-start | bytes 1769480 | tf_op jit(solution)/shard_map/ppermute | solution.py:92
  333.0 27.3 %collective-permute-start.16 = (bf16[144,1024]{1,0:T(8,128)(2,1)S(1)}, bf16[144,1024]{1,0:T(8,128)(2,1)S(1)}, u32[]{:S(2)}, u32[]{:S(2)}) collective-permute-start(bf16[144,1024]{1,0:T(8,128)(2,1)S(1)} %constant_dynamic-slice_fusion.5), channel_id=1, source_target_pairs={{0,2},{1,3},{2,0},{3,1},{4,6},{5,7},{6,4},{7,5},{8,10},{9,11},{10,... | collective-permute-start | bytes 884744 | tf_op jit(solution)/shard_map/ppermute | solution.py:92
  361.8 18.0 %collective-permute-start.25 = (bf16[144,1024]{1,0:T(8,128)(2,1)S(1)}, bf16[144,1024]{1,0:T(8,128)(2,1)S(1)}, u32[]{:S(2)}, u32[]{:S(2)}) collective-permute-start(bf16[144,1024]{1,0:T(8,128)(2,1)S(1)} %get-tuple-element.76), channel_id=1, source_target_pairs={{0,2},{1,3},{2,0},{3,1},{4,6},{5,7},{6,4},{7,5},{8,10},{9,11},{10,... | collective-permute-start | bytes 884744 | tf_op jit(solution)/shard_map/ppermute | solution.py:92
  369.3 31.7 %collective-permute-start.30 = (bf16[288,1024]{1,0:T(8,128)(2,1)S(1)}, bf16[288,1024]{1,0:T(8,128)(2,1)S(1)}, u32[]{:S(2)}, u32[]{:S(2)}) collective-permute-start(bf16[288,1024]{1,0:T(8,128)(2,1)S(1)} %pad_maximum_fusion.14), channel_id=1, source_target_pairs={{0,2},{1,3},{2,0},{3,1},{4,6},{5,7},{6,4},{7,5},{8,10},{9,11},{10,... | collective-permute-start | bytes 1769480 | tf_op jit(solution)/shard_map/ppermute | solution.py:92
  371.9 28.2 %collective-permute-start.22 = (bf16[288,1024]{1,0:T(8,128)(2,1)S(1)}, bf16[288,1024]{1,0:T(8,128)(2,1)S(1)}, u32[]{:S(2)}, u32[]{:S(2)}) collective-permute-start(bf16[288,1024]{1,0:T(8,128)(2,1)S(1)} %pad_maximum_fusion.12), channel_id=1, source_target_pairs={{0,2},{1,3},{2,0},{3,1},{4,6},{5,7},{6,4},{7,5},{8,10},{9,11},{10,... | collective-permute-start | bytes 1769480 | tf_op jit(solution)/shard_map/ppermute | solution.py:92
  378.2 22.3 %collective-permute-start.18 = (bf16[288,1024]{1,0:T(8,128)(2,1)S(1)}, bf16[288,1024]{1,0:T(8,128)(2,1)S(1)}, u32[]{:S(2)}, u32[]{:S(2)}) collective-permute-start(bf16[288,1024]{1,0:T(8,128)(2,1)S(1)} %pad_maximum_fusion.11), channel_id=1, source_target_pairs={{0,1},{1,0},{2,3},{3,2},{4,5},{5,4},{6,7},{7,6},{8,9},{9,8},{10,11... | collective-permute-start | bytes 1769480 | tf_op jit(solution)/shard_map/ppermute | solution.py:92
  379.9 21.5 %collective-permute-start.26 = (bf16[288,1024]{1,0:T(8,128)(2,1)S(1)}, bf16[288,1024]{1,0:T(8,128)(2,1)S(1)}, u32[]{:S(2)}, u32[]{:S(2)}) collective-permute-start(bf16[288,1024]{1,0:T(8,128)(2,1)S(1)} %pad_maximum_fusion.13), channel_id=1, source_target_pairs={{0,1},{1,0},{2,3},{3,2},{4,5},{5,4},{6,7},{7,6},{8,9},{9,8},{10,11... | collective-permute-start | bytes 1769480 | tf_op jit(solution)/shard_map/ppermute | solution.py:92
  (20 other events, 175.7 us)
Sparse Core Ops, SparseCore 0:
  9.0 40.9 all-gather.4
  51.6 29.6 all-gather.6
  82.9 183.6 all-gather.8
  268.1 46.5 all-gather.10
